TPU v7x, 256 devices: a whole 4x4x8 slice. The times are simulated.
256 devices in a mesh: rows: 64 (over z, y_hi, x), cols: 4 (over y_lo, core).
Axes of the slice: x: 4, y: 4 (y_hi: 2, y_lo: 2; y = y_hi * 2 + y_lo), z: 8, core: 2. Of those that a mesh axis runs over, the one named last changes fastest.
Arguments:
- images: bfloat16 [2, 96, 256, 512], P(None, None, 'rows', 'cols'), may hold values from -6 to 6
- conv_weight: bfloat16 [128, 864], replicated, may hold values from -0.048112522 to 0.048112522
- conv_bias: float32 [128], replicated, may hold values from -0.15 to 0.15
- proj_weight: bfloat16 [256, 128], replicated, may hold values from -0.125 to 0.125
- proj_bias: float32 [256], replicated, may hold values from -1.2 to 1.2
Outputs:
- level_zero: bfloat16 [32768, 32768], P('rows', 'cols')
- level_one: bfloat16 [32768, 8192], P('rows', 'cols')
- level_two: bfloat16 [32768, 2048], P('rows', 'cols')
- level_three: bfloat16 [32768, 512], P('rows', 'cols')
All inputs are finite; a program needn't handle non-finite values.
Results may differ from a plain program's by a relative error of at most 0.0039.
Values may be sent and summed in bfloat16 or wider, within the bound.
No kernel may reach another device: no remote copies, remote signals or barrier semaphores. Data moves between devices by JAX's collectives and lax.ppermute only.
A program may use at most 128 MiB of HBM per device.

v0:
```python
import jax
import jax.numpy as jnp
from jax import lax
from jax.sharding import PartitionSpec as P


def shifted(value, axis, steps):
    count = lax.axis_size(axis)
    first, last = (max(0, -steps), min(count, count - steps))
    return lax.ppermute(value, axis, [(source, source + steps) for source in range(first, last)])


def tap_columns(extended, out_rows, out_cols):
    slices = []
    for row_off in range(3):
        for col_off in range(3):
            slices.append(
                extended[
                    ...,
                    row_off : row_off + 2 * out_rows - 1 : 2,
                    col_off : col_off + 2 * out_cols - 1 : 2,
                ]
            )
    stacked = jnp.stack(slices, axis=-4)
    lead = stacked.shape[:-4]
    return stacked.reshape(lead + (9 * extended.shape[-3], out_rows * out_cols))


def hidden_of(extended, conv_weight, conv_bias, out_rows, out_cols):
    tap_stack = tap_columns(extended, out_rows, out_cols)
    pre = jnp.einsum("ok,...kp->...op", conv_weight, tap_stack, preferred_element_type=jnp.float32)
    return jnp.maximum(pre + conv_bias[:, None], 0.0).astype(jnp.bfloat16)


def project(hidden, proj_weight, proj_bias):
    feats = jnp.einsum("oc,...cp->...op", proj_weight, hidden, preferred_element_type=jnp.float32)
    return (feats + proj_bias[:, None]).astype(jnp.bfloat16)


def pool_level(volume, rows_h, cols_w):
    pixels = volume.shape[0]
    grouped = volume.astype(jnp.float32).reshape(pixels, rows_h // 2, 2, cols_w // 2, 2)
    pooled = jnp.sum(grouped, axis=(2, 4)) * 0.25
    return pooled.astype(jnp.bfloat16).reshape(pixels, -1)


def per_device(images, conv_weight, conv_bias, proj_weight, proj_bias):
    in_rows = images.shape[2]
    in_cols = images.shape[3]
    out_rows = in_rows // 2
    out_cols = in_cols // 2
    n_rows = lax.axis_size("rows")
    left_rim = shifted(images[:, :, :, in_cols - 1 :], "cols", 1)
    widened = jnp.concatenate([left_rim, images], axis=3)
    top_rim = shifted(widened[:, :, in_rows - 1 :, :], "rows", 1)
    extended = jnp.concatenate([top_rim, widened], axis=2)
    second_hidden = hidden_of(extended[1], conv_weight, conv_bias, out_rows, out_cols)
    own_feats = project(
        hidden_of(extended[0], conv_weight, conv_bias, out_rows, out_cols), proj_weight, proj_bias
    )
    own_tile = own_feats.reshape(own_feats.shape[0], out_rows, out_cols)
    frame_one = lax.all_gather(own_tile, "cols", axis=2, tiled=True).reshape(own_feats.shape[0], -1)
    score_scale = proj_weight.shape[0] ** (-0.5)
    frame_two = project(second_hidden, proj_weight, proj_bias)
    column_block = lax.all_gather(frame_two, "rows", axis=1, tiled=True)
    scores = lax.dot_general(
        frame_one, column_block, (((0,), (0,)), ((), ())), preferred_element_type=jnp.float32
    )
    level_zero = (scores * score_scale).astype(jnp.bfloat16)
    block_rows = out_rows * n_rows
    level_one = pool_level(level_zero, block_rows, out_cols)
    level_two = pool_level(level_one, block_rows // 2, out_cols // 2)
    level_three = pool_level(level_two, block_rows // 4, out_cols // 4)
    return (level_zero, level_one, level_two, level_three)


def solution(mesh):
    in_specs = (P(None, None, "rows", "cols"), P(), P(), P(), P())
    out_specs = (P("rows", "cols"), P("rows", "cols"), P("rows", "cols"), P("rows", "cols"))
    return jax.shard_map(
        per_device, mesh=mesh, in_specs=in_specs, out_specs=out_specs, check_vma=False
    )
```

profile of v0, /device:TPU:96, one launch (start us, length us, event | category | flops | bytes accessed | tf_op | source)
XLA Modules:
  0.0 235.5 jit_solution(6567841761008458286)
XLA Ops:
  7.2 0.0 copy-start
  7.2 0.0 copy-start.2
  7.2 0.0 copy-start.1
  7.2 0.0 copy-start.3
  7.2 0.0 all-gather.2.cloned.1.call-start
  7.3 1.2 copy.13
  8.5 1.7 collective-permute-start
  10.2 0.8 collective-permute-done
  11.0 3.4 %collective-permute-start.1 = (bf16[2,96,1,129]{1,3,2,0:T(8,128)(2,1)S(1)}, bf16[2,96,1,129]{1,3,2,0:T(8,128)(2,1)S(1)}, u32[]{:S(2)}, u32[]{:S(2)}) collective-permute-start(bf16[2,96,1,129]{1,3,2,0:T(8,128)(2,1)S(1)} %pad_maximum_fusion), channel_id=1, source_target_pairs={{0,4},{4,8},{8,12},{12,16},{16,20},{20,24},{24,28},{28,32},{32,36}... | collective-permute-start | bytes 148616 | tf_op jit(solution)/shard_map/ppermute | solution.py:10
  14.5 7.3 %collective-permute-done.1 = bf16[2,96,1,129]{1,3,2,0:T(8,128)(2,1)S(1)} collective-permute-done((bf16[2,96,1,129]{1,3,2,0:T(8,128)(2,1)S(1)}, bf16[2,96,1,129]{1,3,2,0:T(8,128)(2,1)S(1)}, u32[]{:S(2)}, u32[]{:S(2)}) %collective-permute-start.1) | collective-permute-done | bytes 49568 | tf_op jit(solution)/shard_map/ppermute | solution.py:10
  21.8 0.1 maximum_maximum_fusion
  21.9 0.2 slice.87
  22.2 0.1 slice.86
  22.3 0.1 slice.85
  22.5 0.1 slice.84
  22.6 0.1 slice.83
  22.7 0.1 slice.82
  22.8 0.1 slice.81
  23.0 0.1 slice.80
  23.1 0.1 slice.79
  23.3 1.2 copy.16
  24.5 0.2 reshape.60
  24.8 0.0 copy-done
  24.8 0.0 copy-done.2
  24.8 0.0 copy-done.1
  24.8 0.0 copy-done.3
  24.8 1.0 fusion.2
  25.8 0.0 all-gather.2.cloned.1.call-update
  25.9 0.2 slice.77
  26.1 0.1 slice.76
  26.3 0.1 slice.75
  26.4 0.1 slice.74
  26.5 0.1 slice.73
  26.7 0.1 slice.72
  26.8 0.1 slice.71
  26.9 0.1 slice.70
  27.0 0.1 slice.69
  27.3 1.2 copy.15
  28.4 0.2 reshape.57
  28.7 0.4 fusion
  29.1 8.4 %all_gather.6 = bf16[256,2,256]{0,2,1:T(8,128)(2,1)S(1)} all-gather(bf16[256,2,64]{0,2,1:T(8,128)(2,1)S(1)} %bitcast.67), channel_id=1, replica_groups=mesh['rows'=64,'cols'=4] {'cols'}, dimensions={2}, use_global_device_ids=true | all-gather | bytes 327680 | tf_op jit(solution)/shard_map/all_gather | solution.py:62
  37.5 117.0 %all-gather.2.cloned.1.call-done = bf16[256,8192]{0,1:T(8,128)(2,1)} async-done(((bf16[256,128]{0,1:T(8,128)(2,1)}), bf16[256,8192]{0,1:T(8,128)(2,1)}) %all-gather.2.cloned.1.call-update) | async-done | bytes 4194320 | tf_op jit(solution)/shard_map/all_gather | solution.py:65
  154.5 8.0 %multiply_convert_fusion = bf16[512,8192]{1,0:T(8,128)(2,1)} fusion(bf16[256,512]{0,1:T(8,128)(2,1)S(1)} %bitcast.66, bf16[256,8192]{0,1:T(8,128)(2,1)} %all-gather.2.cloned.1.call-done), kind=kOutput, calls=%fused_computation | convolution fusion | flops 2155872256 | bytes 12845056 | tf_op jit(solution)/shard_map/dot_general | solution.py:66
  162.4 12.4 %copy.17 = f32[512,8192]{0,1:T(8,128)} copy(bf16[512,8192]{1,0:T(8,128)(2,1)} %multiply_convert_fusion) | data formatting | bytes 25165824 | tf_op jit(solution)/shard_map/reshape | solution.py:42
  174.9 20.0 %reshape.64 = f32[512,64,2,32,2]{0,4,3,2,1:T(2,128)} reshape(f32[512,8192]{0,1:T(8,128)} %copy.17) | data formatting | bytes 33554432 | tf_op jit(solution)/shard_map/reshape | solution.py:42
  194.9 15.7 %reduce_sum.27 = f32[512,64,32]{0,2,1:T(8,128)} reduce(f32[512,64,2,32,2]{0,4,3,2,1:T(2,128)} %reshape.64, f32[]{:T(128)} %constant.3.clone.1), dimensions={2,4}, to_apply=%region_0.0 | reduce | flops 3145728 | bytes 20971524 | tf_op jit(solution)/shard_map/reduce_sum | solution.py:43
  210.6 2.8 %multiply_convert_fusion.1 = bf16[512,64,32]{0,2,1:T(8,128)(2,1)S(1)} fusion(f32[512,64,32]{0,2,1:T(8,128)} %reduce_sum.27), kind=kLoop, calls=%fused_computation.1 | loop fusion | flops 2097152 | bytes 6291456 | tf_op jit(solution)/shard_map/convert_element_type | solution.py:44
  213.4 4.0 %reshape.65 = f32[512,32,2,16,2]{0,4,3,2,1:T(2,128)} reshape(bf16[512,64,32]{0,2,1:T(8,128)(2,1)S(1)} %multiply_convert_fusion.1) | data formatting | bytes 6291456 | tf_op jit(solution)/shard_map/convert_element_type | solution.py:42
  217.4 2.4 %copy.18 = bf16[512,2048]{1,0:T(8,128)(2,1)} copy(bf16[512,2048]{0,1:T(8,128)(2,1)S(1)} %bitcast.64) | data formatting | bytes 4194304
  219.8 5.5 %reduce_sum.28 = f32[512,32,16]{0,2,1:T(8,128)S(1)} reduce(f32[512,32,2,16,2]{0,4,3,2,1:T(2,128)} %reshape.65, f32[]{:T(128)} %constant.3.clone.1), dimensions={2,4}, to_apply=%region_1.0 | reduce | flops 786432 | bytes 5242884 | tf_op jit(solution)/shard_map/reduce_sum | solution.py:43
  225.3 0.1 multiply_convert_fusion.2
  225.4 0.7 reshape.66
  226.1 1.0 copy.19
  227.1 0.8 reduce_sum.29
  227.9 0.8 copy.20
  (22 shorter events, 0.3 us)
Async XLA Ops:
  7.2 17.6 %copy-start = (bf16[128,864]{0,1:T(8,128)(2,1)S(1)}, bf16[128,864]{0,1:T(8,128)(2,1)}, u32[]{:S(2)}) copy-start(bf16[128,864]{0,1:T(8,128)(2,1)} %param.6) | copy-start | bytes 663556
  7.2 17.6 %copy-start.2 = (f32[256]{0:T(256)S(1)}, f32[256]{0:T(256)}, u32[]{:S(2)}) copy-start(f32[256]{0:T(256)} %param.9) | copy-start | bytes 3076
  7.2 17.6 %copy-start.1 = (bf16[256,128]{1,0:T(8,128)(2,1)S(1)}, bf16[256,128]{1,0:T(8,128)(2,1)}, u32[]{:S(2)}) copy-start(bf16[256,128]{1,0:T(8,128)(2,1)} %param.8) | copy-start | bytes 196612
  7.2 17.6 %copy-start.3 = (f32[128]{0:T(128)S(1)}, f32[128]{0:T(128)}, u32[]{:S(2)}) copy-start(f32[128]{0:T(128)} %param.7) | copy-start | bytes 1540
  7.2 147.3 %all-gather.2.cloned.1.call-start = ((), (), s32[]{:S(2)}) async-start(), calls=%async_computation | async-start | bytes 4259840 | tf_op jit(solution)/shard_map/all_gather | solution.py:65
  8.5 2.6 %collective-permute-start = (bf16[2,96,4,1]{1,3,2,0:T(2,128)(2,1)S(1)}, bf16[2,96,4,1]{1,3,2,0:T(2,128)(2,1)S(1)}, u32[]{:S(2)}, u32[]{:S(2)}) collective-permute-start(bf16[2,96,4,1]{1,3,2,0:T(2,128)(2,1)S(1)} %slice.88), channel_id=1, source_target_pairs={{0,1},{1,2},{2,3},{4,5},{5,6},{6,7},{8,9},{9,10},{10,11},{12,13},{... | collective-permute-start | bytes 4616 | tf_op jit(solution)/shard_map/ppermute | solution.py:10
  11.0 10.7 %collective-permute-start.1 = (bf16[2,96,1,129]{1,3,2,0:T(8,128)(2,1)S(1)}, bf16[2,96,1,129]{1,3,2,0:T(8,128)(2,1)S(1)}, u32[]{:S(2)}, u32[]{:S(2)}) collective-permute-start(bf16[2,96,1,129]{1,3,2,0:T(8,128)(2,1)S(1)} %pad_maximum_fusion), channel_id=1, source_target_pairs={{0,4},{4,8},{8,12},{12,16},{16,20},{20,24},{24,28},{28,32},{32,36}... | collective-permute-start | bytes 148616 | tf_op jit(solution)/shard_map/ppermute | solution.py:10
Sparse Core Ops, SparseCore 0:
  26.0 128.4 all-gather.1
where the time goes:
time: 238 us; the launch traced here: 235 us
  waiting for transfers between devices  125 us (53%)
  local copies, waits for them, and re-layouts  47.9 us (20%)
  other arithmetic  25 us (11%)
  between operations  14.5 us (6%)
  matrix products  9.4 us (4%)
  blocking collectives  8.39 us (4%)
  starting transfers between devices  5.18 us (2%)
    all_gather x1, waiting for transfers between devices, per_device(): column_block = lax.all_gather(frame_two, 'rows', axis=1, tiled=True)  117 us
    reshape x2, local copies, waits for them, and re-layouts, pool_level(): volume.astype(jnp.float32).reshape(pixels, rows_h // 2, 2, cols_w // 2, 2)  32.5 us
    reduce_sum x3, other arithmetic, pool_level(): pooled = jnp.sum(grouped, axis=(2, 4)) * 0.25  21.9 us
    all_gather x1, blocking collectives, per_device(): lax.all_gather(own_tile, 'cols', axis=2, tiled=True)  8.39 us
    ppermute x2, waiting for transfers between devices, shifted(): lax.ppermute(value, axis, [(source, source + steps) for source in range(f...  8.11 us
    dot_general x1, matrix products, per_device(): lax.dot_general(frame_one, column_block, (((0,), (0,)), ((), ())), prefer...  7.97 us
    unnamed x28, local copies, waits for them, and re-layouts  5.5 us
    ppermute x2, starting transfers between devices, shifted(): lax.ppermute(value, axis, [(source, source + steps) for source in range(f...  5.14 us
  transfers between devices with their start and end apart: 3, of which 3 were waited for; matrix products, arithmetic and copies ran while one was open for 1% of the time, Pallas kernels for 0%

commit v1 on v0

v1 whole, which is shorter than its diff:
```python
import jax
import jax.numpy as jnp
from jax import lax
from jax.experimental import pallas as pl
from jax.experimental.pallas import tpu as pltpu
from jax.sharding import PartitionSpec as P

PLANE = 8


def shifted(value, axis, steps):
    count = lax.axis_size(axis)
    first, last = (max(0, -steps), min(count, count - steps))
    return lax.ppermute(value, axis, [(source, source + steps) for source in range(first, last)])


def tap_columns(extended, out_rows, out_cols):
    slices = []
    for row_off in range(3):
        for col_off in range(3):
            slices.append(
                extended[
                    ...,
                    row_off : row_off + 2 * out_rows - 1 : 2,
                    col_off : col_off + 2 * out_cols - 1 : 2,
                ]
            )
    stacked = jnp.stack(slices, axis=-4)
    lead = stacked.shape[:-4]
    return stacked.reshape(lead + (9 * extended.shape[-3], out_rows * out_cols))


def hidden_of(extended, conv_weight, conv_bias, out_rows, out_cols):
    tap_stack = tap_columns(extended, out_rows, out_cols)
    pre = jnp.einsum("ok,...kp->...op", conv_weight, tap_stack, preferred_element_type=jnp.float32)
    return jnp.maximum(pre + conv_bias[:, None], 0.0).astype(jnp.bfloat16)


def feats_one_kernel(hid_ref, weight_ref, bias_ref, out_ref):
    for k in range(4):
        feats = lax.dot_general(
            hid_ref[k], weight_ref[...], (((0,), (1,)), ((), ())), preferred_element_type=jnp.float32
        )
        feats = (feats + bias_ref[...]).astype(jnp.bfloat16) * jnp.bfloat16(0.0625)
        for i in range(2):
            out_ref[i * 256 + k * 64 : i * 256 + (k + 1) * 64, :] = feats[i * 64 : (i + 1) * 64, :]


def feats_one(hidden, proj_weight, proj_bias):
    return pl.pallas_call(
        feats_one_kernel,
        out_shape=jax.ShapeDtypeStruct((512, 256), jnp.bfloat16),
        name="feats_one",
    )(hidden, proj_weight, proj_bias[None, :])


def plane_kernel(place_ref, first_ref, u_ref, v_ref, weight_ref, bias_ref, pool1_ref, pool2_ref, pool3_ref, *rest):
    zero_ref, one_ref, small_ref, one_scr = rest[-4:]
    step = pl.program_id(0)
    hid = jnp.where(step == 0, u_ref[...], v_ref[...])
    hid = jnp.concatenate([hid[j] for j in range(4)], axis=1)
    feats = jnp.dot(weight_ref[...], hid, preferred_element_type=jnp.float32)
    feats = (feats + bias_ref[...]).astype(jnp.bfloat16)
    zero = jnp.dot(first_ref[...], feats, preferred_element_type=jnp.float32).astype(jnp.bfloat16)
    zero_ref[...] = zero
    one = jnp.dot(zero, pool1_ref[...], preferred_element_type=jnp.float32).astype(jnp.bfloat16)
    one_ref[...] = one
    one_scr[step] = one

    @pl.when(step == 1)
    def _():
        whole = jnp.concatenate([one_scr[0], one_scr[1]], axis=1)
        two = jnp.dot(whole, pool2_ref[...], preferred_element_type=jnp.float32).astype(jnp.bfloat16)
        three = jnp.dot(two, pool3_ref[...], preferred_element_type=jnp.float32).astype(jnp.bfloat16)
        small_ref[0] = jnp.concatenate([two, three], axis=1)


def plane_call(place, first, u, u_block, v, v_block, consts, outs):
    full = lambda *shape: pl.BlockSpec(shape, lambda s, place: (0,) * len(shape))
    in_specs = [
        full(512, 256),
        pl.BlockSpec((4, 128, 128), lambda s, place: (u_block, 0, 0)),
        pl.BlockSpec((4, 128, 128), lambda s, place: (v_block, 0, 0)),
        full(256, 128),
        full(256, 1),
        full(512, 128),
        full(256, 64),
        full(64, 64),
    ]
    args = [place, first, u, v, *consts]
    aliases = {}
    if outs is not None:
        in_specs += [pl.BlockSpec(memory_space=pl.ANY)] * 3
        aliases = {len(args) + n: n for n in range(3)}
        args += list(outs)
    return pl.pallas_call(
        plane_kernel,
        grid_spec=pltpu.PrefetchScalarGridSpec(
            num_scalar_prefetch=1,
            grid=(2,),
            in_specs=in_specs,
            out_specs=[
                pl.BlockSpec((512, 512), lambda s, place: (0, 2 * place[0] + s)),
                pl.BlockSpec((512, 128), lambda s, place: (0, 2 * place[0] + s)),
                pl.BlockSpec((1, 512, 128), lambda s, place: (place[0], 0, 0)),
            ],
            scratch_shapes=[pltpu.VMEM((2, 512, 128), jnp.bfloat16)],
        ),
        out_shape=[
            jax.ShapeDtypeStruct((512, 8192), jnp.bfloat16),
            jax.ShapeDtypeStruct((512, 2048), jnp.bfloat16),
            jax.ShapeDtypeStruct((8, 512, 128), jnp.bfloat16),
        ],
        input_output_aliases=aliases,
        cost_estimate=pl.CostEstimate(flops=1_400_000_000, bytes_accessed=4_000_000, transcendentals=0),
        name="plane",
    )(*args)


def last_kernel(small_ref, two_ref, three_ref):
    for z in range(8):
        two_ref[:, z * 64 : (z + 1) * 64] = small_ref[z, :, 0:64]
        three_ref[:, z * 16 : (z + 1) * 16] = small_ref[z, :, 64:80]


def pool_matrix(rows, cols, pad):
    pixel = lax.broadcasted_iota(jnp.int32, (rows * cols, pad), 0)
    cell = lax.broadcasted_iota(jnp.int32, (rows * cols, pad), 1)
    own = (pixel // cols // 2) * (cols // 2) + (pixel % cols) // 2
    return jnp.where(own == cell, 0.25, 0.0).astype(jnp.bfloat16)


def per_device(images, conv_weight, conv_bias, proj_weight, proj_bias):
    in_rows = images.shape[2]
    in_cols = images.shape[3]
    out_rows = in_rows // 2
    out_cols = in_cols // 2
    n_rows = lax.axis_size("rows")
    left_rim = shifted(images[:, :, :, in_cols - 1 :], "cols", 1)
    widened = jnp.concatenate([left_rim, images], axis=3)
    top_rim = shifted(widened[:, :, in_rows - 1 :, :], "rows", 1)
    extended = jnp.concatenate([top_rim, widened], axis=2)
    hidden = hidden_of(extended, conv_weight, conv_bias, out_rows, out_cols)

    plane_groups = [[z * PLANE + n for n in range(PLANE)] for z in range(n_rows // PLANE)]
    mine = lax.all_to_all(
        jnp.broadcast_to(hidden[1][None], (PLANE,) + hidden[1].shape),
        "rows", 0, 0, axis_index_groups=plane_groups,
    )
    band = lax.all_to_all(jnp.broadcast_to(hidden[0][None], (4,) + hidden[0].shape), "cols", 0, 0)

    up = [(r, (r + PLANE) % n_rows) for r in range(n_rows)]
    down = [(r, (r - PLANE) % n_rows) for r in range(n_rows)]
    z = lax.axis_index("rows") // PLANE
    planes = n_rows // PLANE
    place = lambda off: jnp.reshape((z + off) % planes, (1,)).astype(jnp.int32)

    first = feats_one(band, proj_weight, proj_bias)
    consts = (
        proj_weight,
        proj_bias[:, None],
        pool_matrix(8, 64, 128),
        pool_matrix(8, 32, 64),
        pool_matrix(4, 16, 64),
    )
    below, above = mine, mine
    outs = plane_call(place(0), first, mine, 0, mine, 1, consts, None)
    for off in range(1, planes // 2):
        below = lax.ppermute(below, "rows", up)
        above = lax.ppermute(above, "rows", down)
        outs = plane_call(place(-off), first, below, 0, below, 1, consts, outs)
        outs = plane_call(place(off), first, above, 0, above, 1, consts, outs)
    below = lax.ppermute(below[:4], "rows", up)
    above = lax.ppermute(above[4:], "rows", down)
    outs = plane_call(place(planes // 2), first, below, 0, above, 0, consts, outs)
    level_two, level_three = pl.pallas_call(
        last_kernel,
        out_shape=[
            jax.ShapeDtypeStruct((512, 512), jnp.bfloat16),
            jax.ShapeDtypeStruct((512, 128), jnp.bfloat16),
        ],
        name="small_levels",
    )(outs[2])
    return (outs[0], outs[1], level_two, level_three)


def solution(mesh):
    in_specs = (P(None, None, "rows", "cols"), P(), P(), P(), P())
    out_specs = (P("rows", "cols"), P("rows", "cols"), P("rows", "cols"), P("rows", "cols"))
    return jax.shard_map(
        per_device, mesh=mesh, in_specs=in_specs, out_specs=out_specs, check_vma=False
    )
```

time: 238 us -> 96.9 us (0.41)
  the two profiles are of different devices: /device:TPU:96 before, /device:TPU:8 now
where the time goes in v1:
time: 96.9 us; the launch traced here: 96.2 us
  Pallas kernels  37.7 us (39%)
  starting transfers between devices  33.3 us (34%)
  waiting for transfers between devices  10.8 us (11%)
  local copies, waits for them, and re-layouts  8.45 us (9%)
  other arithmetic  3.83 us (4%)
  between operations  1.04 us (1%)
  matrix products  1.01 us (1%)
    pallas_call x8, Pallas kernels, plane_call(): pl.pallas_call(plane_kernel, grid_spec=pltpu.PrefetchScalarGridSpec(num_s...  33 us
    ppermute x3, starting transfers between devices, per_device(): above = lax.ppermute(above, 'rows', down)  10.4 us
    all_to_all x1, starting transfers between devices, per_device(): lax.all_to_all(jnp.broadcast_to(hidden[1][None], (PLANE,) + hidden[1].sha...  8.05 us
    all_to_all x1, waiting for transfers between devices, per_device(): lax.all_to_all(jnp.broadcast_to(hidden[1][None], (PLANE,) + hidden[1].sha...  7.38 us
    ppermute x2, starting transfers between devices, shifted(): lax.ppermute(value, axis, [(source, source + steps) for source in range(f...  5.32 us
    ppermute x2, waiting for transfers between devices, shifted(): lax.ppermute(value, axis, [(source, source + steps) for source in range(f...  3.44 us
    all_to_all x1, starting transfers between devices, per_device(): lax.all_to_all(jnp.broadcast_to(hidden[0][None], (4,) + hidden[0].shape),...  3.31 us
    ppermute x1, starting transfers between devices, per_device(): above = lax.ppermute(above[4:], 'rows', down)  3.28 us
  transfers between devices with their start and end apart: 12, of which 3 were waited for; matrix products, arithmetic and copies ran while one was open for 4% of the time, Pallas kernels for 32%

profile of v1, /device:TPU:8, one launch (start us, length us, event | category | flops | bytes accessed | tf_op | source)
XLA Modules:
  0.0 96.2 jit_solution(12462418510288392759)
XLA Ops:
  0.6 0.0 copy-start
  0.6 0.0 copy-start.11
  0.7 1.2 %copy.44 = bf16[2,96,4,128]{1,0,3,2:T(2,128)(2,1)S(1)} copy(bf16[2,96,4,128]{3,2,1,0:T(4,128)(2,1)} %param.5) | data formatting | bytes 393216 | tf_op args[0]
  1.9 1.9 %collective-permute-start = (bf16[2,96,4,1]{1,0,3,2:T(2,128)(2,1)S(1)}, bf16[2,96,4,1]{1,0,3,2:T(2,128)(2,1)S(1)}, u32[]{:S(2)}, u32[]{:S(2)}) collective-permute-start(bf16[2,96,4,1]{1,0,3,2:T(2,128)(2,1)S(1)} %slice.60), channel_id=1, source_target_pairs={{0,1},{1,2},{2,3},{4,5},{5,6},{6,7},{8,9},{9,10},{10,11},{12,13},{... | collective-permute-start | bytes 4616 | tf_op jit(solution)/shard_map/ppermute | solution.py:14
  3.9 0.9 select_convert_fusion.1.pool2_ref
  4.9 2.0 %collective-permute-done = bf16[2,96,4,1]{1,0,3,2:T(2,128)(2,1)S(1)} collective-permute-done((bf16[2,96,4,1]{1,0,3,2:T(2,128)(2,1)S(1)}, bf16[2,96,4,1]{1,0,3,2:T(2,128)(2,1)S(1)}, u32[]{:S(2)}, u32[]{:S(2)}) %collective-permute-start) | collective-permute-done | bytes 1568 | tf_op jit(solution)/shard_map/ppermute | solution.py:14
  6.8 0.1 fusion.30
  6.9 3.4 %collective-permute-start.1 = (bf16[2,96,1,129]{1,0,3,2:T(2,128)(2,1)S(1)}, bf16[2,96,1,129]{1,0,3,2:T(2,128)(2,1)S(1)}, u32[]{:S(2)}, u32[]{:S(2)}) collective-permute-start(bf16[2,96,1,129]{1,0,3,2:T(2,128)(2,1)S(1)} %fusion.30), channel_id=1, source_target_pairs={{0,4},{4,8},{8,12},{12,16},{16,20},{20,24},{24,28},{28,32},{32,36}... | collective-permute-start | bytes 148616 | tf_op jit(solution)/shard_map/ppermute | solution.py:14
  10.3 0.4 pad_maximum_fusion
  10.7 1.5 %collective-permute-done.1 = bf16[2,96,1,129]{1,0,3,2:T(2,128)(2,1)S(1)} collective-permute-done((bf16[2,96,1,129]{1,0,3,2:T(2,128)(2,1)S(1)}, bf16[2,96,1,129]{1,0,3,2:T(2,128)(2,1)S(1)}, u32[]{:S(2)}, u32[]{:S(2)}) %collective-permute-start.1) | collective-permute-done | bytes 49568 | tf_op jit(solution)/shard_map/ppermute | solution.py:14
  12.2 0.4 maximum_maximum_fusion
  12.6 0.1 bitcast_dynamic-update-slice_fusion.7
  12.7 0.1 bitcast_dynamic-update-slice_fusion.6
  12.7 0.1 bitcast_dynamic-update-slice_fusion.5
  12.8 0.1 bitcast_dynamic-update-slice_fusion.4
  12.9 0.1 bitcast_dynamic-update-slice_fusion.3
  12.9 0.1 bitcast_dynamic-update-slice_fusion.2
  13.0 0.1 bitcast_dynamic-update-slice_fusion.1
  13.0 0.1 bitcast_dynamic-update-slice_fusion
  13.1 2.4 %copy.50 = bf16[2,9,96,2,64]{4,3,2,1,0:T(2,128)(2,1)S(1)} copy(bf16[2,9,96,2,64]{2,0,4,3,1:T(2,128)(2,1)S(1)} %bitcast_dynamic-update-slice_fusion) | data formatting | bytes 884736 | tf_op jit(solution)/shard_map/stack | solution.py:28
  15.5 0.4 reshape.37
  15.9 1.0 %fusion.2 = bf16[2,128,128]{1,2,0:T(8,128)(2,1)S(1)} fusion(bf16[2,864,128]{2,1,0:T(8,128)(2,1)S(1)} %reshape.37, bf16[128,864]{0,1:T(8,128)(2,1)S(1)} %copy-done, f32[128]{0:T(128)} %param.7), kind=kOutput, calls=%fused_computation.3 | convolution fusion | flops 56721408 | bytes 729600 | tf_op jit(solution)/shard_map/ok,...kp->...op/dot_general | solution.py:35
  17.0 0.1 copy.52
  17.1 0.7 broadcast_in_dim.48
  17.8 8.1 %all-to-all-start.1 = ((bf16[8,128,128]{2,1,0:T(8,128)(2,1)}), bf16[8,128,128]{2,1,0:T(8,128)(2,1)S(1)}, u32[]{:S(2)}, u32[]{:S(2)}) async-start(bf16[8,128,128]{2,1,0:T(8,128)(2,1)} %broadcast_in_dim.48), calls=%async_computation.1 | async-start | bytes 524288 | tf_op jit(solution)/shard_map/all_to_all | solution.py:146
  25.9 1.3 %select_convert_fusion.pool1_ref = bf16[512,128]{1,0:T(8,128)(2,1)} fusion(s32[512]{0:T(512)S(1)} %get-tuple-element.59, s32[512]{0:T(512)S(1)} %get-tuple-element.60, s32[512]{0:T(512)S(1)} %get-tuple-element.58, s32[512]{0:T(512)S(1)} %get-tuple-element.61, pred[512]{0:T(512)(128)(4,1)S(1)} %get-tuple-element.63, pred[512]{0:T(512)(128)(4,1)S(1)} %get-tuple-element.62), kind=kLoop, calls=%fused_computation.40 | loop fusion | flops 2424832 | bytes 140288 | tf_op jit(solution)/shard_map/convert_element_type | solution.py:130
  27.2 0.1 copy.51
  27.3 7.4 %all-to-all-done.1.u_ref.v_ref = bf16[8,128,128]{2,1,0:T(8,128)(2,1)S(1)} async-done(((bf16[8,128,128]{2,1,0:T(8,128)(2,1)}), bf16[8,128,128]{2,1,0:T(8,128)(2,1)S(1)}, u32[]{:S(2)}, u32[]{:S(2)}) %all-to-all-start.1) | async-done | bytes 262176 | tf_op jit(solution)/shard_map/all_to_all | solution.py:146
  34.7 0.7 broadcast_in_dim.45
  35.4 3.3 %all-to-all-start = ((bf16[4,128,128]{2,1,0:T(8,128)(2,1)}), bf16[4,128,128]{2,1,0:T(8,128)(2,1)S(1)}, u32[]{:S(2)}, u32[]{:S(2)}) async-start(bf16[4,128,128]{2,1,0:T(8,128)(2,1)} %broadcast_in_dim.45), calls=%async_computation | async-start | bytes 262144 | tf_op jit(solution)/shard_map/all_to_all | solution.py:150
  38.7 2.7 %collective-permute-start.2 = (bf16[8,128,128]{2,1,0:T(8,128)(2,1)S(1)}, bf16[8,128,128]{2,1,0:T(8,128)(2,1)S(1)}, u32[]{:S(2)}, u32[]{:S(2)}) collective-permute-start(bf16[8,128,128]{2,1,0:T(8,128)(2,1)S(1)} %all-to-all-done.1.u_ref.v_ref), channel_id=1, source_target_pairs={{0,32},{4,36},{8,40},{12,44},{16,48},{20,52},{24,56},{28,60},{32,6... | collective-permute-start | bytes 786440 | tf_op jit(solution)/shard_map/ppermute | solution.py:169
  41.4 4.0 %collective-permute-start.6 = (bf16[8,128,128]{2,1,0:T(8,128)(2,1)S(1)}, bf16[8,128,128]{2,1,0:T(8,128)(2,1)S(1)}, u32[]{:S(2)}, u32[]{:S(2)}) collective-permute-start(bf16[8,128,128]{2,1,0:T(8,128)(2,1)S(1)} %all-to-all-done.1.u_ref.v_ref), channel_id=1, source_target_pairs={{0,224},{4,228},{8,232},{12,236},{16,240},{20,244},{24,248},{28,25... | collective-permute-start | bytes 786440 | tf_op jit(solution)/shard_map/ppermute | solution.py:170
  45.4 0.7 select_convert_fusion.2.pool3_ref
  46.1 0.8 copy.60.bias_ref
  46.9 0.0 all-to-all-done.hid_ref
  46.9 0.7 copy-done.7
  47.6 1.9 %feats_one.1.first_ref = bf16[512,256]{1,0:T(8,128)(2,1)} custom-call(bf16[4,128,128]{2,1,0:T(8,128)(2,1)} %copy-done.7, bf16[256,128]{1,0:T(8,128)(2,1)} %weight_ref.17, f32[1,256]{1,0:T(1,128)} %bitcast.38), custom_call_target="tpu_custom_call" | custom-call | tf_op jit(solution)/shard_map/feats_one/pallas_call | solution.py:50
  49.5 4.1 %plane.8 = (bf16[512,8192]{1,0:T(8,128)(2,1)}, bf16[512,2048]{1,0:T(8,128)(2,1)}, bf16[8,512,128]{2,1,0:T(8,128)(2,1)}) custom-call(s32[1]{0:T(128)} %bitcast.22.place_ref, bf16[512,256]{1,0:T(8,128)(2,1)} %feats_one.1.first_ref, bf16[8,128,128]{2,1,0:T(8,128)(2,1)} %copy-done.8, bf16[8,128,128]{2,1,0:T(8,128)(2,1)} %copy-done.8, ...), custom_call_target="tpu_custom_call" | custom-call | flops 1400000000 | bytes 4000000 | tf_op jit(solution)/shard_map/plane/pallas_call | solution.py:96
  53.6 0.0 collective-permute-done.2.u_ref.v_ref
  53.7 0.0 copy-start.4
  53.7 0.1 collective-permute-start.3
  53.8 0.0 collective-permute-done.6.u_ref.v_ref
  53.8 3.2 %collective-permute-start.7 = (bf16[8,128,128]{2,1,0:T(8,128)(2,1)S(1)}, bf16[8,128,128]{2,1,0:T(8,128)(2,1)S(1)}, u32[]{:S(2)}, u32[]{:S(2)}) collective-permute-start(bf16[8,128,128]{2,1,0:T(8,128)(2,1)S(1)} %collective-permute-done.6.u_ref.v_ref), channel_id=1, source_target_pairs={{0,224},{4,228},{8,232},{12,236},{16,240},{20,244},{24,248},{28,25... | collective-permute-start | bytes 786440 | tf_op jit(solution)/shard_map/ppermute | solution.py:170
  57.0 4.1 %plane.9 = (bf16[512,8192]{1,0:T(8,128)(2,1)}, bf16[512,2048]{1,0:T(8,128)(2,1)}, bf16[8,512,128]{2,1,0:T(8,128)(2,1)}) custom-call(s32[1]{0:T(128)} %bitcast.21.place_ref, bf16[512,256]{1,0:T(8,128)(2,1)} %feats_one.1.first_ref, bf16[8,128,128]{2,1,0:T(8,128)(2,1)} %copy-done.4, ...), custom_call_target="tpu_custom_call", output_to_operand_aliasing={{0}: (9, {}), {1}: (10, {}), {2}: (11, {})} | custom-call | flops 1400000000 | bytes 4000000 | tf_op jit(solution)/shard_map/plane/pallas_call | solution.py:96
  61.1 4.1 %plane.10 = (bf16[512,8192]{1,0:T(8,128)(2,1)}, bf16[512,2048]{1,0:T(8,128)(2,1)}, bf16[8,512,128]{2,1,0:T(8,128)(2,1)}) custom-call(s32[1]{0:T(128)} %bitcast.20.place_ref, bf16[512,256]{1,0:T(8,128)(2,1)} %feats_one.1.first_ref, bf16[8,128,128]{2,1,0:T(8,128)(2,1)} %copy-done.3, ...), custom_call_target="tpu_custom_call", output_to_operand_aliasing={{0}: (9, {}), {1}: (10, {}), {2}: (11, {})} | custom-call | flops 1400000000 | bytes 4000000 | tf_op jit(solution)/shard_map/plane/pallas_call | solution.py:96
  65.3 0.0 collective-permute-done.3.u_ref.v_ref
  65.3 0.1 collective-permute-start.4
  65.4 0.0 collective-permute-done.7.u_ref.v_ref
  65.4 3.2 %collective-permute-start.8 = (bf16[8,128,128]{2,1,0:T(8,128)(2,1)S(1)}, bf16[8,128,128]{2,1,0:T(8,128)(2,1)S(1)}, u32[]{:S(2)}, u32[]{:S(2)}) collective-permute-start(bf16[8,128,128]{2,1,0:T(8,128)(2,1)S(1)} %collective-permute-done.7.u_ref.v_ref), channel_id=1, source_target_pairs={{0,224},{4,228},{8,232},{12,236},{16,240},{20,244},{24,248},{28,25... | collective-permute-start | bytes 786440 | tf_op jit(solution)/shard_map/ppermute | solution.py:170
  68.6 4.1 %plane.11 = (bf16[512,8192]{1,0:T(8,128)(2,1)}, bf16[512,2048]{1,0:T(8,128)(2,1)}, bf16[8,512,128]{2,1,0:T(8,128)(2,1)}) custom-call(s32[1]{0:T(128)} %bitcast.19.place_ref, bf16[512,256]{1,0:T(8,128)(2,1)} %feats_one.1.first_ref, bf16[8,128,128]{2,1,0:T(8,128)(2,1)} %copy-done.6, ...), custom_call_target="tpu_custom_call", output_to_operand_aliasing={{0}: (9, {}), {1}: (10, {}), {2}: (11, {})} | custom-call | flops 1400000000 | bytes 4000000 | tf_op jit(solution)/shard_map/plane/pallas_call | solution.py:96
  72.8 4.2 %plane.12 = (bf16[512,8192]{1,0:T(8,128)(2,1)}, bf16[512,2048]{1,0:T(8,128)(2,1)}, bf16[8,512,128]{2,1,0:T(8,128)(2,1)}) custom-call(s32[1]{0:T(128)} %bitcast.18.place_ref, bf16[512,256]{1,0:T(8,128)(2,1)} %feats_one.1.first_ref, bf16[8,128,128]{2,1,0:T(8,128)(2,1)} %copy-done.5, ...), custom_call_target="tpu_custom_call", output_to_operand_aliasing={{0}: (9, {}), {1}: (10, {}), {2}: (11, {})} | custom-call | flops 1400000000 | bytes 4000000 | tf_op jit(solution)/shard_map/plane/pallas_call | solution.py:96
  76.9 0.0 collective-permute-done.4.u_ref.v_ref
  77.0 0.1 collective-permute-start.5
  77.0 0.0 collective-permute-done.8.u_ref.v_ref
  77.1 3.3 %collective-permute-start.9 = (bf16[4,128,128]{2,1,0:T(8,128)(2,1)S(1)}, bf16[4,128,128]{2,1,0:T(8,128)(2,1)S(1)}, u32[]{:S(2)}, u32[]{:S(2)}) collective-permute-start(bf16[4,128,128]{2,1,0:T(8,128)(2,1)S(1)} %slice.66), channel_id=1, source_target_pairs={{0,224},{4,228},{8,232},{12,236},{16,240},{20,244},{24,248},{28,25... | collective-permute-start | bytes 393224 | tf_op jit(solution)/shard_map/ppermute | solution.py:174
  80.4 4.1 %plane.13 = (bf16[512,8192]{1,0:T(8,128)(2,1)}, bf16[512,2048]{1,0:T(8,128)(2,1)}, bf16[8,512,128]{2,1,0:T(8,128)(2,1)}) custom-call(s32[1]{0:T(128)} %bitcast.17.place_ref, bf16[512,256]{1,0:T(8,128)(2,1)} %feats_one.1.first_ref, bf16[8,128,128]{2,1,0:T(8,128)(2,1)} %copy-done.2, ...), custom_call_target="tpu_custom_call", output_to_operand_aliasing={{0}: (9, {}), {1}: (10, {}), {2}: (11, {})} | custom-call | flops 1400000000 | bytes 4000000 | tf_op jit(solution)/shard_map/plane/pallas_call | solution.py:96
  84.5 4.1 %plane.14 = (bf16[512,8192]{1,0:T(8,128)(2,1)}, bf16[512,2048]{1,0:T(8,128)(2,1)}, bf16[8,512,128]{2,1,0:T(8,128)(2,1)}) custom-call(s32[1]{0:T(128)} %bitcast.16.place_ref, bf16[512,256]{1,0:T(8,128)(2,1)} %feats_one.1.first_ref, bf16[8,128,128]{2,1,0:T(8,128)(2,1)} %copy-done.1, ...), custom_call_target="tpu_custom_call", output_to_operand_aliasing={{0}: (9, {}), {1}: (10, {}), {2}: (11, {})} | custom-call | flops 1400000000 | bytes 4000000 | tf_op jit(solution)/shard_map/plane/pallas_call | solution.py:96
  88.7 0.0 collective-permute-done.5.u_ref
  88.7 0.0 copy-start.9
  88.7 0.0 collective-permute-done.9.v_ref
  88.7 0.6 copy-done.9
  89.3 0.0 copy-done.10
  89.4 4.1 %plane.15 = (bf16[512,8192]{1,0:T(8,128)(2,1)}, bf16[512,2048]{1,0:T(8,128)(2,1)}, bf16[8,512,128]{2,1,0:T(8,128)(2,1)}) custom-call(s32[1]{0:T(128)} %bitcast.place_ref, bf16[512,256]{1,0:T(8,128)(2,1)} %feats_one.1.first_ref, bf16[4,128,128]{2,1,0:T(8,128)(2,1)} %copy-done.9, ...), custom_call_target="tpu_custom_call", output_to_operand_aliasing={{0}: (9, {}), {1}: (10, {}), {2}: (11, {})} | custom-call | flops 1400000000 | bytes 4000000 | tf_op jit(solution)/shard_map/plane/pallas_call | solution.py:96
  93.4 2.8 %small_levels.1 = (bf16[512,512]{1,0:T(8,128)(2,1)}, bf16[512,128]{1,0:T(8,128)(2,1)}) custom-call(bf16[8,512,128]{2,1,0:T(8,128)(2,1)} %get-tuple-element.53.small_ref), custom_call_target="tpu_custom_call" | custom-call | tf_op jit(solution)/shard_map/small_levels/pallas_call | solution.py:176
  (31 shorter events, 0.2 us)
Async XLA Ops:
  0.6 15.3 %copy-start = (bf16[128,864]{0,1:T(8,128)(2,1)S(1)}, bf16[128,864]{0,1:T(8,128)(2,1)}, u32[]{:S(2)}) copy-start(bf16[128,864]{0,1:T(8,128)(2,1)} %param.6) | copy-start | bytes 663556
  0.6 45.5 %copy-start.11 = (f32[256]{0:T(256)S(1)}, f32[256]{0:T(256)}, u32[]{:S(2)}) copy-start(f32[256]{0:T(256)} %param.9) | copy-start | bytes 3076
  1.9 4.9 %collective-permute-start = (bf16[2,96,4,1]{1,0,3,2:T(2,128)(2,1)S(1)}, bf16[2,96,4,1]{1,0,3,2:T(2,128)(2,1)S(1)}, u32[]{:S(2)}, u32[]{:S(2)}) collective-permute-start(bf16[2,96,4,1]{1,0,3,2:T(2,128)(2,1)S(1)} %slice.60), channel_id=1, source_target_pairs={{0,1},{1,2},{2,3},{4,5},{5,6},{6,7},{8,9},{9,10},{10,11},{12,13},{... | collective-permute-start | bytes 4616 | tf_op jit(solution)/shard_map/ppermute | solution.py:14
  6.9 5.3 %collective-permute-start.1 = (bf16[2,96,1,129]{1,0,3,2:T(2,128)(2,1)S(1)}, bf16[2,96,1,129]{1,0,3,2:T(2,128)(2,1)S(1)}, u32[]{:S(2)}, u32[]{:S(2)}) collective-permute-start(bf16[2,96,1,129]{1,0,3,2:T(2,128)(2,1)S(1)} %fusion.30), channel_id=1, source_target_pairs={{0,4},{4,8},{8,12},{12,16},{16,20},{20,24},{24,28},{28,32},{32,36}... | collective-permute-start | bytes 148616 | tf_op jit(solution)/shard_map/ppermute | solution.py:14
  17.8 16.8 %all-to-all-start.1 = ((bf16[8,128,128]{2,1,0:T(8,128)(2,1)}), bf16[8,128,128]{2,1,0:T(8,128)(2,1)S(1)}, u32[]{:S(2)}, u32[]{:S(2)}) async-start(bf16[8,128,128]{2,1,0:T(8,128)(2,1)} %broadcast_in_dim.48), calls=%async_computation.1 | async-start | bytes 524288 | tf_op jit(solution)/shard_map/all_to_all | solution.py:146
  34.7 14.8 %copy-start.8 = (bf16[8,128,128]{2,1,0:T(8,128)(2,1)}, bf16[8,128,128]{2,1,0:T(8,128)(2,1)S(1)}, u32[]{:S(2)}) copy-start(bf16[8,128,128]{2,1,0:T(8,128)(2,1)S(1)} %all-to-all-done.1.u_ref.v_ref) | copy-start | bytes 786436
  35.4 11.6 %all-to-all-start = ((bf16[4,128,128]{2,1,0:T(8,128)(2,1)}), bf16[4,128,128]{2,1,0:T(8,128)(2,1)S(1)}, u32[]{:S(2)}, u32[]{:S(2)}) async-start(bf16[4,128,128]{2,1,0:T(8,128)(2,1)} %broadcast_in_dim.45), calls=%async_computation | async-start | bytes 262144 | tf_op jit(solution)/shard_map/all_to_all | solution.py:150
  38.7 14.9 %collective-permute-start.2 = (bf16[8,128,128]{2,1,0:T(8,128)(2,1)S(1)}, bf16[8,128,128]{2,1,0:T(8,128)(2,1)S(1)}, u32[]{:S(2)}, u32[]{:S(2)}) collective-permute-start(bf16[8,128,128]{2,1,0:T(8,128)(2,1)S(1)} %all-to-all-done.1.u_ref.v_ref), channel_id=1, source_target_pairs={{0,32},{4,36},{8,40},{12,44},{16,48},{20,52},{24,56},{28,60},{32,6... | collective-permute-start | bytes 786440 | tf_op jit(solution)/shard_map/ppermute | solution.py:169
  41.4 12.4 %collective-permute-start.6 = (bf16[8,128,128]{2,1,0:T(8,128)(2,1)S(1)}, bf16[8,128,128]{2,1,0:T(8,128)(2,1)S(1)}, u32[]{:S(2)}, u32[]{:S(2)}) collective-permute-start(bf16[8,128,128]{2,1,0:T(8,128)(2,1)S(1)} %all-to-all-done.1.u_ref.v_ref), channel_id=1, source_target_pairs={{0,224},{4,228},{8,232},{12,236},{16,240},{20,244},{24,248},{28,25... | collective-permute-start | bytes 786440 | tf_op jit(solution)/shard_map/ppermute | solution.py:170
  46.9 0.7 copy-start.7
  53.7 3.3 %copy-start.4 = (bf16[8,128,128]{2,1,0:T(8,128)(2,1)}, bf16[8,128,128]{2,1,0:T(8,128)(2,1)S(1)}, u32[]{:S(2)}) copy-start(bf16[8,128,128]{2,1,0:T(8,128)(2,1)S(1)} %collective-permute-done.2.u_ref.v_ref) | copy-start | bytes 786436
  53.7 11.6 %collective-permute-start.3 = (bf16[8,128,128]{2,1,0:T(8,128)(2,1)S(1)}, bf16[8,128,128]{2,1,0:T(8,128)(2,1)S(1)}, u32[]{:S(2)}, u32[]{:S(2)}) collective-permute-start(bf16[8,128,128]{2,1,0:T(8,128)(2,1)S(1)} %collective-permute-done.2.u_ref.v_ref), channel_id=1, source_target_pairs={{0,32},{4,36},{8,40},{12,44},{16,48},{20,52},{24,56},{28,60},{32,6... | collective-permute-start | bytes 786440 | tf_op jit(solution)/shard_map/ppermute | solution.py:169
  53.8 7.4 %copy-start.3 = (bf16[8,128,128]{2,1,0:T(8,128)(2,1)}, bf16[8,128,128]{2,1,0:T(8,128)(2,1)S(1)}, u32[]{:S(2)}) copy-start(bf16[8,128,128]{2,1,0:T(8,128)(2,1)S(1)} %collective-permute-done.6.u_ref.v_ref) | copy-start | bytes 786436
  53.8 11.6 %collective-permute-start.7 = (bf16[8,128,128]{2,1,0:T(8,128)(2,1)S(1)}, bf16[8,128,128]{2,1,0:T(8,128)(2,1)S(1)}, u32[]{:S(2)}, u32[]{:S(2)}) collective-permute-start(bf16[8,128,128]{2,1,0:T(8,128)(2,1)S(1)} %collective-permute-done.6.u_ref.v_ref), channel_id=1, source_target_pairs={{0,224},{4,228},{8,232},{12,236},{16,240},{20,244},{24,248},{28,25... | collective-permute-start | bytes 786440 | tf_op jit(solution)/shard_map/ppermute | solution.py:170
  65.3 3.3 %copy-start.6 = (bf16[8,128,128]{2,1,0:T(8,128)(2,1)}, bf16[8,128,128]{2,1,0:T(8,128)(2,1)S(1)}, u32[]{:S(2)}) copy-start(bf16[8,128,128]{2,1,0:T(8,128)(2,1)S(1)} %collective-permute-done.3.u_ref.v_ref) | copy-start | bytes 786436
  65.3 11.6 %collective-permute-start.4 = (bf16[8,128,128]{2,1,0:T(8,128)(2,1)S(1)}, bf16[8,128,128]{2,1,0:T(8,128)(2,1)S(1)}, u32[]{:S(2)}, u32[]{:S(2)}) collective-permute-start(bf16[8,128,128]{2,1,0:T(8,128)(2,1)S(1)} %collective-permute-done.3.u_ref.v_ref), channel_id=1, source_target_pairs={{0,32},{4,36},{8,40},{12,44},{16,48},{20,52},{24,56},{28,60},{32,6... | collective-permute-start | bytes 786440 | tf_op jit(solution)/shard_map/ppermute | solution.py:169
  65.4 7.4 %copy-start.5 = (bf16[8,128,128]{2,1,0:T(8,128)(2,1)}, bf16[8,128,128]{2,1,0:T(8,128)(2,1)S(1)}, u32[]{:S(2)}) copy-start(bf16[8,128,128]{2,1,0:T(8,128)(2,1)S(1)} %collective-permute-done.7.u_ref.v_ref) | copy-start | bytes 786436
  65.4 11.6 %collective-permute-start.8 = (bf16[8,128,128]{2,1,0:T(8,128)(2,1)S(1)}, bf16[8,128,128]{2,1,0:T(8,128)(2,1)S(1)}, u32[]{:S(2)}, u32[]{:S(2)}) collective-permute-start(bf16[8,128,128]{2,1,0:T(8,128)(2,1)S(1)} %collective-permute-done.7.u_ref.v_ref), channel_id=1, source_target_pairs={{0,224},{4,228},{8,232},{12,236},{16,240},{20,244},{24,248},{28,25... | collective-permute-start | bytes 786440 | tf_op jit(solution)/shard_map/ppermute | solution.py:170
  76.9 3.4 %copy-start.2 = (bf16[8,128,128]{2,1,0:T(8,128)(2,1)}, bf16[8,128,128]{2,1,0:T(8,128)(2,1)S(1)}, u32[]{:S(2)}) copy-start(bf16[8,128,128]{2,1,0:T(8,128)(2,1)S(1)} %collective-permute-done.4.u_ref.v_ref) | copy-start | bytes 786436
  77.0 11.7 %collective-permute-start.5 = (bf16[4,128,128]{2,1,0:T(8,128)(2,1)S(1)}, bf16[4,128,128]{2,1,0:T(8,128)(2,1)S(1)}, u32[]{:S(2)}, u32[]{:S(2)}) collective-permute-start(bf16[4,128,128]{2,1,0:T(8,128)(2,1)S(1)} %slice.65), channel_id=1, source_target_pairs={{0,32},{4,36},{8,40},{12,44},{16,48},{20,52},{24,56},{28,60},{32,6... | collective-permute-start | bytes 393224 | tf_op jit(solution)/shard_map/ppermute | solution.py:173
  77.1 7.5 %copy-start.1 = (bf16[8,128,128]{2,1,0:T(8,128)(2,1)}, bf16[8,128,128]{2,1,0:T(8,128)(2,1)S(1)}, u32[]{:S(2)}) copy-start(bf16[8,128,128]{2,1,0:T(8,128)(2,1)S(1)} %collective-permute-done.8.u_ref.v_ref) | copy-start | bytes 786436
  77.1 11.6 %collective-permute-start.9 = (bf16[4,128,128]{2,1,0:T(8,128)(2,1)S(1)}, bf16[4,128,128]{2,1,0:T(8,128)(2,1)S(1)}, u32[]{:S(2)}, u32[]{:S(2)}) collective-permute-start(bf16[4,128,128]{2,1,0:T(8,128)(2,1)S(1)} %slice.66), channel_id=1, source_target_pairs={{0,224},{4,228},{8,232},{12,236},{16,240},{20,244},{24,248},{28,25... | collective-permute-start | bytes 393224 | tf_op jit(solution)/shard_map/ppermute | solution.py:174
  88.7 0.7 copy-start.9
  88.7 0.7 copy-start.10

commit v2 on v0

v2 whole, which is shorter than its diff:
```python
import functools

import jax
import jax.numpy as jnp
from jax import lax
from jax.experimental import pallas as pl
from jax.experimental.pallas import tpu as pltpu
from jax.sharding import PartitionSpec as P

Z, YH, X = 8, 2, 4
PLANE = YH * X
ROWS, COLS = Z * PLANE, 4
BF, F32 = jnp.bfloat16, jnp.float32


def dot(a, b):
    return jnp.dot(a, b, preferred_element_type=F32)


def iotas(*shape):
    return lax.broadcasted_iota(jnp.int32, shape, 0), lax.broadcasted_iota(jnp.int32, shape, 1)


def one_hot(mask, value=1.0):
    return jnp.where(mask, value, 0.0).astype(BF)


def split_kernel(tile_ref, main_ref, top_ref, left_ref, corner_ref):
    row, col = iotas(384, 384)
    tap = (row >= 96).astype(jnp.int32) + (row >= 192).astype(jnp.int32) + (row >= 288).astype(jnp.int32)
    order = one_hot(col == (row - 96 * tap) * 4 + tap)
    main = dot(order, jnp.concatenate([tile_ref[0], tile_ref[1]], axis=1)).astype(BF)
    row, col = iotas(256, 128)
    rim = one_hot(((row == 127) & (col == 0)) | ((row == 255) & (col == 64)))
    left = dot(main, rim).astype(BF)
    main_ref[...] = main
    top_ref[...] = main[288:384]
    left_ref[...] = left
    corner_ref[...] = left[288:384]


def split_tile(images):
    return pl.pallas_call(
        split_kernel,
        out_shape=[
            jax.ShapeDtypeStruct((384, 256), BF),
            jax.ShapeDtypeStruct((96, 256), BF),
            jax.ShapeDtypeStruct((384, 128), BF),
            jax.ShapeDtypeStruct((96, 128), BF),
        ],
        name="split_tile",
    )(images.reshape(2, 384, 128))


def hidden_kernel(main_ref, top_ref, left_ref, corner_ref, weight_ref, bias_ref, one_ref, two_ref):
    rows = jnp.concatenate([top_ref[...], main_ref[...]], axis=0)
    row, col = iotas(256, 384)
    source = 2 * (col & 63) - 1 + (col >> 7) + jnp.where((col & 64) != 0, 128, 0)
    valid = ((col & 63) != 0) | (col >= 128)
    taps = dot(rows, one_hot((row == source) & valid))
    rim = jnp.concatenate([corner_ref[...], left_ref[...]], axis=0).astype(F32)
    first = (taps[:, :128] + rim).astype(BF)
    parts = [first, taps[:, 128:256].astype(BF), taps[:, 256:384].astype(BF)]
    stacked = jnp.concatenate(
        [
            jnp.concatenate(
                [parts[b][(2 * i + a) * 96 : (2 * i + a + 1) * 96] for a in range(3) for b in range(3)], axis=0
            )
            for i in range(2)
        ],
        axis=1,
    )
    pre = dot(weight_ref[...], stacked)
    bias = jnp.transpose(jnp.broadcast_to(bias_ref[...], (128, 128)))
    hidden = [jnp.maximum(pre[:, i * 128 : (i + 1) * 128] + bias, 0.0) for i in range(2)]
    lane = lax.broadcasted_iota(jnp.int32, (128, 128), 1)
    one_ref[...] = jnp.where(lane < 64, hidden[0], pltpu.roll(hidden[1], 64, 1)).astype(BF)
    two_ref[...] = jnp.where(lane < 64, pltpu.roll(hidden[0], 64, 1), hidden[1]).astype(BF)


def hidden_of(main, top, left, corner, conv_weight, conv_bias):
    return pl.pallas_call(
        hidden_kernel,
        out_shape=[jax.ShapeDtypeStruct((128, 128), BF)] * 2,
        name="hidden",
    )(main, top, left, corner, conv_weight, conv_bias[None, :])


def feats_one_kernel(meta_ref, *refs):
    hid_refs, (weight_ref, bias_ref, out_ref) = refs[:4], refs[4:]
    for m in range(4):
        k = meta_ref[9] ^ m
        feats = lax.dot_general(
            hid_refs[m][...], weight_ref[...], (((0,), (1,)), ((), ())), preferred_element_type=F32
        )
        feats = (feats + bias_ref[...]).astype(BF) * jnp.bfloat16(0.0625)
        for i in range(2):
            out_ref[pl.ds(pl.multiple_of(i * 256 + k * 64, 64), 64), :] = feats[i * 64 : (i + 1) * 64, :]


def feats_one(meta, hidden, proj_weight, proj_bias):
    vmem, smem = pl.BlockSpec(memory_space=pltpu.VMEM), pl.BlockSpec(memory_space=pltpu.SMEM)
    return pl.pallas_call(
        feats_one_kernel,
        in_specs=[smem] + [vmem] * 6,
        out_shape=jax.ShapeDtypeStruct((512, 256), BF),
        name="feats_one",
    )(meta, *hidden, proj_weight, proj_bias[None, :])


def planes_kernel(offsets, halves, n_alias, meta_ref, first_ref, weight_ref, bias_ref, *refs):
    hid_refs, rest = refs[: len(offsets) * halves], refs[len(offsets) * halves + n_alias :]
    zero_out, one_out, small_out, zero_buf, one_buf, small_buf, hid_buf, sems = rest
    row, col = iotas(512, 128)
    pool1 = one_hot(col == (row >> 7) * 32 + ((row & 63) >> 1), 0.25)
    row, col = iotas(256, 64)
    pool2 = one_hot(col == (row >> 6) * 16 + ((row & 31) >> 1), 0.25)
    row, col = iotas(64, 64)
    pool3 = one_hot(col == (row >> 5) * 8 + ((row & 15) >> 1), 0.25)
    bias = jnp.concatenate(
        [jnp.transpose(jnp.broadcast_to(bias_ref[n : n + 1, :], (128, 128))) for n in range(2)], axis=0
    )
    bias = jnp.concatenate([bias] * 4, axis=1)
    copies = []

    def send(source, target):
        copies.append(pltpu.make_async_copy(source, target, sems.at[len(copies)]))
        copies[-1].start()

    for n, offset in enumerate(offsets):
        place = (meta_ref[0] + (offset + Z)) & (Z - 1)
        if halves == 2:
            hid_buf[0:4] = hid_refs[0][...]
            hid_buf[4:8] = hid_refs[1][...]
            hid_ref = hid_buf
        else:
            hid_ref = hid_refs[n]
        ones = []
        for half in range(2):
            hid = jnp.concatenate([hid_ref[meta_ref[1 + 4 * half + j]] for j in range(4)], axis=1)
            feats = (dot(weight_ref[...], hid) + bias).astype(BF)
            zero = dot(first_ref[...], feats).astype(BF)
            slot = 2 * n + half
            zero_buf[slot] = zero
            send(zero_buf.at[slot], zero_out.at[:, pl.ds(pl.multiple_of(place * 1024 + half * 512, 512), 512)])
            ones.append(dot(zero, pool1).astype(BF))
        one = jnp.concatenate(ones, axis=1)
        one_buf[n] = one
        send(one_buf.at[n], one_out.at[:, pl.ds(pl.multiple_of(place * 256, 256), 256)])
        two = dot(one, pool2).astype(BF)
        three = dot(two, pool3).astype(BF)
        small_buf[n] = jnp.concatenate([two, three], axis=1)
        send(small_buf.at[n], small_out.at[place])
    for copy in copies:
        copy.wait()


def planes_call(offsets, hidden, meta, first, proj_weight, proj_bias, outs):
    halves = len(hidden) // len(offsets)
    count = len(offsets)
    args = [meta, first, proj_weight, proj_bias.reshape(2, 128), *hidden]
    vmem, smem = pl.BlockSpec(memory_space=pltpu.VMEM), pl.BlockSpec(memory_space=pltpu.SMEM)
    anywhere = pl.BlockSpec(memory_space=pl.ANY)
    in_specs = [smem] + [vmem] * (len(args) - 1)
    aliases = {}
    if outs is not None:
        aliases = {len(args) + n: n for n in range(3)}
        args += list(outs)
        in_specs += [anywhere] * 3
    return pl.pallas_call(
        functools.partial(planes_kernel, offsets, halves, len(aliases)),
        in_specs=in_specs,
        out_specs=[anywhere] * 3,
        out_shape=[
            jax.ShapeDtypeStruct((512, 8192), BF),
            jax.ShapeDtypeStruct((512, 2048), BF),
            jax.ShapeDtypeStruct((8, 512, 128), BF),
        ],
        scratch_shapes=[
            pltpu.VMEM((2 * count, 512, 512), BF),
            pltpu.VMEM((count, 512, 256), BF),
            pltpu.VMEM((count, 512, 128), BF),
            pltpu.VMEM((8, 128, 128), BF),
            pltpu.SemaphoreType.DMA((4 * count,)),
        ],
        input_output_aliases=aliases,
        compiler_params=pltpu.CompilerParams(vmem_limit_bytes=24 << 20),
        cost_estimate=pl.CostEstimate(
            flops=1_400_000_000 * count, bytes_accessed=1_500_000 * count, transcendentals=0
        ),
        name="planes",
    )(*args)


def last_kernel(small_ref, two_ref, three_ref):
    for z in range(Z):
        two_ref[:, z * 64 : (z + 1) * 64] = small_ref[z, :, 0:64]
        three_ref[:, z * 16 : (z + 1) * 16] = small_ref[z, :, 64:80]


def per_device(images, conv_weight, conv_bias, proj_weight, proj_bias):
    right = [(c, c + 1) for c in range(COLS - 1)]
    down = [(r, r + 1) for r in range(ROWS - 1)]
    diagonal = [(r * COLS + c, (r + 1) * COLS + c + 1) for r in range(ROWS - 1) for c in range(COLS - 1)]
    main, top, left, corner = split_tile(images)
    top = lax.ppermute(top, "rows", down)
    left = lax.ppermute(left, "cols", right)
    corner = lax.ppermute(corner, ("rows", "cols"), diagonal)
    hidden_one, hidden_two = hidden_of(main, top, left, corner, conv_weight, conv_bias)

    r, c = lax.axis_index("rows"), lax.axis_index("cols")
    z, yh, x = r // PLANE, (r // X) % YH, r % X
    order = [((j % X - x) % X) * 2 + (yh ^ (j // X)) for j in range(PLANE)]
    meta = jnp.stack([z, *order, c] + [jnp.int32(0)] * 6).astype(jnp.int32)

    def along(axis, steps):
        size, stride = {"z": (Z, PLANE), "yh": (YH, X), "x": (X, 1)}[axis]
        target = lambda r: r + ((r // stride + steps) % size - (r // stride) % size) * stride
        return [(r, target(r)) for r in range(ROWS)]

    other = lax.ppermute(hidden_two, "rows", along("yh", 1))
    pair = jnp.stack([hidden_two, other])
    ones = [hidden_one]
    ones += [lax.ppermute(hidden_one, "cols", [(k, k ^ m) for k in range(COLS)]) for m in range(1, 4)]
    mine = jnp.concatenate([pair] + [lax.ppermute(pair, "rows", along("x", -s)) for s in range(1, X)])
    first = feats_one(meta, ones, proj_weight, proj_bias)

    call = functools.partial(planes_call, meta=meta, first=first, proj_weight=proj_weight, proj_bias=proj_bias)
    below, above = mine, mine
    outs = call((0,), [mine], outs=None)
    for step in range(1, Z // 2):
        below = lax.ppermute(below, "rows", along("z", 1))
        above = lax.ppermute(above, "rows", along("z", -1))
        outs = call((-step, step), [below, above], outs=outs)
    below = lax.ppermute(below[:4], "rows", along("z", 1))
    above = lax.ppermute(above[4:], "rows", along("z", -1))
    outs = call((Z // 2,), [below, above], outs=outs)
    level_two, level_three = pl.pallas_call(
        last_kernel,
        out_shape=[jax.ShapeDtypeStruct((512, 512), BF), jax.ShapeDtypeStruct((512, 128), BF)],
        name="small_levels",
    )(outs[2])
    return (outs[0], outs[1], level_two, level_three)


def solution(mesh):
    in_specs = (P(None, None, "rows", "cols"), P(), P(), P(), P())
    out_specs = (P("rows", "cols"), P("rows", "cols"), P("rows", "cols"), P("rows", "cols"))
    return jax.shard_map(
        per_device, mesh=mesh, in_specs=in_specs, out_specs=out_specs, check_vma=False
    )
```

time: 238 us -> 86.2 us (0.36)
  waiting for transfers between devices: 125 us -> 16.1 us
  local copies, waits for them, and re-layouts: 47.9 us -> 8.52 us
  starting transfers between devices: 5.18 us -> 32.9 us
  Pallas kernels: 0 us -> 26.5 us
  other arithmetic: 25 us -> 0.76 us
  between operations: 14.5 us -> 0.77 us
  matrix products: 9.4 us -> 0 us
  blocking collectives: 8.39 us -> 0 us
    all_gather x1 -> x0, waiting for transfers between devices: 117 us -> none  [per_device(): column_block = lax.all_gather(frame_two, 'rows', axis=1, tiled=True)]
    reshape x4 -> x0, local copies, waits for them, and re-layouts: 33 us -> none  [the longest x2 32.5 us: pool_level(): volume.astype(jnp.float32).reshape(pixels, rows_h // 2, 2, cols_w // 2, 2)]
    ppermute x2 -> x18, starting transfers between devices: 5.14 us -> 32.9 us  [the longest x3 10.6 us: per_device(): below = lax.ppermute(below, 'rows', along('z', 1))]
    pallas_call x0 -> x9, Pallas kernels: none -> 26.5 us  [the longest x5 17.4 us: planes_call(): pl.pallas_call(functools.partial(planes_kernel, offsets, halves, len(alia...]
    reduce_sum x3 -> x0, other arithmetic: 21.9 us -> none  [pool_level(): pooled = jnp.sum(grouped, axis=(2, 4)) * 0.25]
    dot_general x3 -> x0, matrix products: 9.4 us -> none  [the longest x1 7.97 us: per_device(): lax.dot_general(frame_one, column_block, (((0,), (0,)), ((), ())), prefer...]
    all_gather x1 -> x0, blocking collectives: 8.39 us -> none  [per_device(): lax.all_gather(own_tile, 'cols', axis=2, tiled=True)]
    ppermute x2 -> x18, waiting for transfers between devices: 8.11 us -> 16.1 us  [the longest x3 5.46 us: per_device(): lax.ppermute(pair, 'rows', along('x', -s))]
  transfers between devices with their start and end apart: 3 -> 18, of which waited for: 3 -> 9; matrix products, arithmetic and copies ran while one was open for 1% -> 4% of each run, Pallas kernels for 0% -> 20%
where the time goes in v2:
time: 86.2 us; the launch traced here: 85.6 us
  starting transfers between devices  32.9 us (38%)
  Pallas kernels  26.5 us (31%)
  waiting for transfers between devices  16.1 us (19%)
  local copies, waits for them, and re-layouts  8.52 us (10%)
    pallas_call x5, Pallas kernels, planes_call(): pl.pallas_call(functools.partial(planes_kernel, offsets, halves, len(alia...  17.4 us
    ppermute x3, starting transfers between devices, per_device(): below = lax.ppermute(below, 'rows', along('z', 1))  10.6 us
    unnamed x27, local copies, waits for them, and re-layouts  7.89 us
    ppermute x3, waiting for transfers between devices, per_device(): lax.ppermute(pair, 'rows', along('x', -s))  5.46 us
    ppermute x3, starting transfers between devices, per_device(): lax.ppermute(pair, 'rows', along('x', -s))  4.6 us
    ppermute x1, starting transfers between devices, per_device(): corner = lax.ppermute(corner, ('rows', 'cols'), diagonal)  4.58 us
    ppermute x1, starting transfers between devices, per_device(): below = lax.ppermute(below[:4], 'rows', along('z', 1))  3.77 us
    ppermute x1, starting transfers between devices, per_device(): top = lax.ppermute(top, 'rows', down)  3.4 us
  transfers between devices with their start and end apart: 18, of which 9 were waited for; matrix products, arithmetic and copies ran while one was open for 4% of the time, Pallas kernels for 20%

profile of v2, /device:TPU:96, one launch (start us, length us, event | category | flops | bytes accessed | tf_op | source)
XLA Modules:
  0.0 85.6 jit_solution(269016650237822991)
XLA Ops:
  0.6 2.1 %split_tile.1 = (bf16[384,256]{1,0:T(8,128)(2,1)}, bf16[96,256]{1,0:T(8,128)(2,1)}, bf16[384,128]{1,0:T(8,128)(2,1)}, bf16[96,128]{1,0:T(8,128)(2,1)}) custom-call(bf16[2,384,128]{2,1,0:T(8,128)(2,1)} %bitcast.24), custom_call_target="tpu_custom_call" | custom-call | tf_op jit(solution)/shard_map/split_tile/pallas_call | solution.py:43
  2.7 1.7 %collective-permute-start.1 = (bf16[384,128]{1,0:T(8,128)(2,1)}, bf16[384,128]{1,0:T(8,128)(2,1)S(1)}, u32[]{:S(2)}, u32[]{:S(2)}) collective-permute-start(bf16[384,128]{1,0:T(8,128)(2,1)} %get-tuple-element.29), channel_id=1, source_target_pairs={{0,1},{1,2},{2,3},{4,5},{5,6},{6,7},{8,9},{9,10},{10,11},{12,13},{... | collective-permute-start | bytes 294920 | tf_op jit(solution)/shard_map/ppermute | solution.py:207
  4.4 3.4 %collective-permute-start = (bf16[96,256]{1,0:T(8,128)(2,1)}, bf16[96,256]{1,0:T(8,128)(2,1)S(1)}, u32[]{:S(2)}, u32[]{:S(2)}) collective-permute-start(bf16[96,256]{1,0:T(8,128)(2,1)} %get-tuple-element.28), channel_id=1, source_target_pairs={{0,4},{4,8},{8,12},{12,16},{16,20},{20,24},{24,28},{28,32},{32,36}... | collective-permute-start | bytes 147464 | tf_op jit(solution)/shard_map/ppermute | solution.py:206
  7.8 4.6 %collective-permute-start.2 = (bf16[96,128]{1,0:T(8,128)(2,1)}, bf16[96,128]{1,0:T(8,128)(2,1)S(1)}, u32[]{:S(2)}, u32[]{:S(2)}) collective-permute-start(bf16[96,128]{1,0:T(8,128)(2,1)} %get-tuple-element.30), channel_id=1, source_target_pairs={{0,5},{1,6},{2,7},{4,9},{5,10},{6,11},{8,13},{9,14},{10,15},{12,17... | collective-permute-start | bytes 73736 | tf_op jit(solution)/shard_map/ppermute | solution.py:208
  12.4 1.8 %copy.21.weight_ref = bf16[128,864]{1,0:T(8,128)(2,1)} copy(bf16[128,864]{0,1:T(8,128)(2,1)} %param.6) | data formatting | bytes 442368 | tf_op args[1]
  14.2 0.0 collective-permute-done.2.corner_ref
  14.2 0.0 copy-start.10
  14.2 0.9 %collective-permute-done.top_ref = bf16[96,256]{1,0:T(8,128)(2,1)S(1)} collective-permute-done((bf16[96,256]{1,0:T(8,128)(2,1)}, bf16[96,256]{1,0:T(8,128)(2,1)S(1)}, u32[]{:S(2)}, u32[]{:S(2)}) %collective-permute-start) | collective-permute-done | bytes 49184 | tf_op jit(solution)/shard_map/ppermute | solution.py:206
  15.1 0.0 copy-start.6
  15.1 0.0 collective-permute-done.1.left_ref
  15.1 0.0 copy-start.5
  15.2 0.0 copy-done.10
  15.2 0.6 copy-done.6
  15.8 0.0 copy-done.5
  15.8 2.4 %hidden.1 = (bf16[128,128]{1,0:T(8,128)(2,1)}, bf16[128,128]{1,0:T(8,128)(2,1)}) custom-call(bf16[384,256]{1,0:T(8,128)(2,1)} %get-tuple-element.27.main_ref, bf16[96,256]{1,0:T(8,128)(2,1)} %copy-done.6, bf16[384,128]{1,0:T(8,128)(2,1)} %copy-done.5, bf16[96,128]{1,0:T(8,128)(2,1)} %copy-done.10, bf16[128,864]{1,0:T(8,128)(2,1)} %copy.21.weight_ref, ...), custom_call_target="tpu_custom_call" | custom-call | tf_op jit(solution)/shard_map/hidden/pallas_call | solution.py:82
  18.2 2.3 %collective-permute-start.6 = (bf16[128,128]{1,0:T(8,128)(2,1)}, bf16[128,128]{1,0:T(8,128)(2,1)S(1)}, u32[]{:S(2)}, u32[]{:S(2)}) collective-permute-start(bf16[128,128]{1,0:T(8,128)(2,1)} %get-tuple-element.32), channel_id=1, source_target_pairs={{0,16},{4,20},{8,24},{12,28},{16,0},{20,4},{24,8},{28,12},{32,48},... | collective-permute-start | bytes 98312 | tf_op jit(solution)/shard_map/ppermute | solution.py:221
  20.5 0.8 constant_dynamic-update-slice_fusion.4
  21.3 2.5 %collective-permute-done.6 = bf16[128,128]{1,0:T(8,128)(2,1)S(1)} collective-permute-done((bf16[128,128]{1,0:T(8,128)(2,1)}, bf16[128,128]{1,0:T(8,128)(2,1)S(1)}, u32[]{:S(2)}, u32[]{:S(2)}) %collective-permute-start.6) | collective-permute-done | bytes 32800 | tf_op jit(solution)/shard_map/ppermute | solution.py:221
  23.8 0.8 pad_maximum_fusion
  24.6 3.3 %collective-permute-start.7 = (bf16[2,128,128]{2,1,0:T(8,128)(2,1)S(1)}, bf16[2,128,128]{2,1,0:T(8,128)(2,1)S(1)}, u32[]{:S(2)}, u32[]{:S(2)}) collective-permute-start(bf16[2,128,128]{2,1,0:T(8,128)(2,1)S(1)} %pad_maximum_fusion), channel_id=1, source_target_pairs={{0,12},{4,0},{8,4},{12,8},{16,28},{20,16},{24,20},{28,24},{32,44},... | collective-permute-start | bytes 196616 | tf_op jit(solution)/shard_map/ppermute | solution.py:225
  27.9 0.0 collective-permute-start.8
  27.9 1.3 %collective-permute-start.9 = (bf16[2,128,128]{2,1,0:T(8,128)(2,1)S(1)}, bf16[2,128,128]{2,1,0:T(8,128)(2,1)S(1)}, u32[]{:S(2)}, u32[]{:S(2)}) collective-permute-start(bf16[2,128,128]{2,1,0:T(8,128)(2,1)S(1)} %pad_maximum_fusion), channel_id=1, source_target_pairs={{0,4},{4,8},{8,12},{12,0},{16,20},{20,24},{24,28},{28,16},{32,36},... | collective-permute-start | bytes 196616 | tf_op jit(solution)/shard_map/ppermute | solution.py:225
  29.2 0.6 collective-permute-done.7
  29.8 4.0 %collective-permute-done.8 = bf16[2,128,128]{2,1,0:T(8,128)(2,1)S(1)} collective-permute-done((bf16[2,128,128]{2,1,0:T(8,128)(2,1)S(1)}, bf16[2,128,128]{2,1,0:T(8,128)(2,1)S(1)}, u32[]{:S(2)}, u32[]{:S(2)}) %collective-permute-start.8) | collective-permute-done | bytes 65568 | tf_op jit(solution)/shard_map/ppermute | solution.py:225
  33.8 0.9 %collective-permute-done.9 = bf16[2,128,128]{2,1,0:T(8,128)(2,1)S(1)} collective-permute-done((bf16[2,128,128]{2,1,0:T(8,128)(2,1)S(1)}, bf16[2,128,128]{2,1,0:T(8,128)(2,1)S(1)}, u32[]{:S(2)}, u32[]{:S(2)}) %collective-permute-start.9) | collective-permute-done | bytes 65568 | tf_op jit(solution)/shard_map/ppermute | solution.py:225
  34.7 3.6 %collective-permute-start.10 = (bf16[8,128,128]{2,1,0:T(8,128)(2,1)S(1)}, bf16[8,128,128]{2,1,0:T(8,128)(2,1)S(1)}, u32[]{:S(2)}, u32[]{:S(2)}) collective-permute-start(bf16[8,128,128]{2,1,0:T(8,128)(2,1)S(1)} %constant_dynamic-update-slice_fusion.refs_0_), channel_id=1, source_target_pairs={{0,32},{4,36},{8,40},{12,44},{16,48},{20,52},{24,56},{28,60},{32,6... | collective-permute-start | bytes 786440 | tf_op jit(solution)/shard_map/ppermute | solution.py:232
  38.3 0.0 collective-permute-start.14
  38.3 0.0 collective-permute-start.3
  38.3 0.6 collective-permute-start.4
  38.9 1.3 %collective-permute-start.5 = (bf16[128,128]{1,0:T(8,128)(2,1)}, bf16[128,128]{1,0:T(8,128)(2,1)S(1)}, u32[]{:S(2)}, u32[]{:S(2)}) collective-permute-start(bf16[128,128]{1,0:T(8,128)(2,1)} %get-tuple-element.31.refs_0_), channel_id=1, source_target_pairs={{0,3},{1,2},{2,1},{3,0},{4,7},{5,6},{6,5},{7,4},{8,11},{9,10},{10,... | collective-permute-start | bytes 98312 | tf_op jit(solution)/shard_map/ppermute | solution.py:224
  40.2 0.6 stack.52.meta_ref
  40.8 0.0 collective-permute-done.3.refs_1_
  40.8 2.0 %collective-permute-done.4.refs_2_ = bf16[128,128]{1,0:T(8,128)(2,1)S(1)} collective-permute-done((bf16[128,128]{1,0:T(8,128)(2,1)}, bf16[128,128]{1,0:T(8,128)(2,1)S(1)}, u32[]{:S(2)}, u32[]{:S(2)}) %collective-permute-start.4) | collective-permute-done | bytes 32800 | tf_op jit(solution)/shard_map/ppermute | solution.py:224
  42.8 0.0 collective-permute-done.5.refs_3_
  42.8 0.0 copy-done.7
  42.8 0.6 copy-done.8
  43.4 0.0 copy-done.9
  43.4 1.9 %feats_one.1.first_ref = bf16[512,256]{1,0:T(8,128)(2,1)} custom-call(s32[16]{0:T(128)} %stack.52.meta_ref, bf16[128,128]{1,0:T(8,128)(2,1)} %get-tuple-element.31.refs_0_, bf16[128,128]{1,0:T(8,128)(2,1)} %copy-done.7, bf16[128,128]{1,0:T(8,128)(2,1)} %copy-done.8, bf16[128,128]{1,0:T(8,128)(2,1)} %copy-done.9, bf16[256,128]{1,0:T(8,128)(2,1)} %weight_ref.10, ...), custom_call_target="tpu_custom_call" | custom-call | tf_op jit(solution)/shard_map/feats_one/pallas_call | solution.py:103
  45.3 0.9 %copy-done.1 = bf16[512,256]{1,0:T(8,128)(2,1)S(1)} copy-done((bf16[512,256]{1,0:T(8,128)(2,1)S(1)}, bf16[512,256]{1,0:T(8,128)(2,1)}, u32[]{:S(2)}) %copy-start.1) | copy-done | bytes 262168
  46.2 0.8 copy-done.2
  47.1 0.7 copy-done.3
  47.8 0.6 copy-done.4
  48.4 2.4 %planes.5 = (bf16[512,8192]{1,0:T(8,128)(2,1)}, bf16[512,2048]{1,0:T(8,128)(2,1)}, bf16[8,512,128]{2,1,0:T(8,128)(2,1)S(1)}) custom-call(s32[16]{0:T(128)S(1)} %copy-done.4, bf16[512,256]{1,0:T(8,128)(2,1)S(1)} %copy-done.1, bf16[256,128]{1,0:T(8,128)(2,1)S(1)} %copy-done.2, f32[2,128]{1,0:T(2,128)S(1)} %bitcast.19, ...), custom_call_target="tpu_custom_call" | custom-call | flops 1400000000 | bytes 1500000 | tf_op jit(solution)/shard_map/planes/pallas_call | solution.py:170
  50.8 0.0 collective-permute-done.10.refs_0_
  50.8 3.3 %collective-permute-start.11 = (bf16[8,128,128]{2,1,0:T(8,128)(2,1)S(1)}, bf16[8,128,128]{2,1,0:T(8,128)(2,1)S(1)}, u32[]{:S(2)}, u32[]{:S(2)}) collective-permute-start(bf16[8,128,128]{2,1,0:T(8,128)(2,1)S(1)} %collective-permute-done.10.refs_0_), channel_id=1, source_target_pairs={{0,32},{4,36},{8,40},{12,44},{16,48},{20,52},{24,56},{28,60},{32,6... | collective-permute-start | bytes 786440 | tf_op jit(solution)/shard_map/ppermute | solution.py:232
  54.1 0.0 collective-permute-done.14.refs_1_
  54.1 0.0 collective-permute-start.15
  54.1 4.2 %planes.6 = (bf16[512,8192]{1,0:T(8,128)(2,1)}, bf16[512,2048]{1,0:T(8,128)(2,1)}, bf16[8,512,128]{2,1,0:T(8,128)(2,1)S(1)}) custom-call(s32[16]{0:T(128)S(1)} %copy-done.4, bf16[512,256]{1,0:T(8,128)(2,1)S(1)} %copy-done.1, bf16[256,128]{1,0:T(8,128)(2,1)S(1)} %copy-done.2, ...), custom_call_target="tpu_custom_call", output_to_operand_aliasing={{0}: (6, {}), {1}: (7, {}), {2}: (8, {})} | custom-call | flops 2800000000 | bytes 3000000 | tf_op jit(solution)/shard_map/planes/pallas_call | solution.py:170
  58.3 2.0 %collective-permute-done.11.refs_0_ = bf16[8,128,128]{2,1,0:T(8,128)(2,1)S(1)} collective-permute-done((bf16[8,128,128]{2,1,0:T(8,128)(2,1)S(1)}, bf16[8,128,128]{2,1,0:T(8,128)(2,1)S(1)}, u32[]{:S(2)}, u32[]{:S(2)}) %collective-permute-start.11) | collective-permute-done | bytes 262176 | tf_op jit(solution)/shard_map/ppermute | solution.py:232
  60.3 3.7 %collective-permute-start.12 = (bf16[8,128,128]{2,1,0:T(8,128)(2,1)S(1)}, bf16[8,128,128]{2,1,0:T(8,128)(2,1)S(1)}, u32[]{:S(2)}, u32[]{:S(2)}) collective-permute-start(bf16[8,128,128]{2,1,0:T(8,128)(2,1)S(1)} %collective-permute-done.11.refs_0_), channel_id=1, source_target_pairs={{0,32},{4,36},{8,40},{12,44},{16,48},{20,52},{24,56},{28,60},{32,6... | collective-permute-start | bytes 786440 | tf_op jit(solution)/shard_map/ppermute | solution.py:232
  64.0 0.0 collective-permute-done.15.refs_1_
  64.0 0.0 collective-permute-start.16
  64.0 4.2 %planes.7 = (bf16[512,8192]{1,0:T(8,128)(2,1)}, bf16[512,2048]{1,0:T(8,128)(2,1)}, bf16[8,512,128]{2,1,0:T(8,128)(2,1)S(1)}) custom-call(s32[16]{0:T(128)S(1)} %copy-done.4, bf16[512,256]{1,0:T(8,128)(2,1)S(1)} %copy-done.1, bf16[256,128]{1,0:T(8,128)(2,1)S(1)} %copy-done.2, ...), custom_call_target="tpu_custom_call", output_to_operand_aliasing={{0}: (6, {}), {1}: (7, {}), {2}: (8, {})} | custom-call | flops 2800000000 | bytes 3000000 | tf_op jit(solution)/shard_map/planes/pallas_call | solution.py:170
  68.2 1.2 %collective-permute-done.12.refs_0_ = bf16[8,128,128]{2,1,0:T(8,128)(2,1)S(1)} collective-permute-done((bf16[8,128,128]{2,1,0:T(8,128)(2,1)S(1)}, bf16[8,128,128]{2,1,0:T(8,128)(2,1)S(1)}, u32[]{:S(2)}, u32[]{:S(2)}) %collective-permute-start.12) | collective-permute-done | bytes 262176 | tf_op jit(solution)/shard_map/ppermute | solution.py:232
  69.4 3.8 %collective-permute-start.13 = (bf16[4,128,128]{2,1,0:T(8,128)(2,1)S(1)}, bf16[4,128,128]{2,1,0:T(8,128)(2,1)S(1)}, u32[]{:S(2)}, u32[]{:S(2)}) collective-permute-start(bf16[4,128,128]{2,1,0:T(8,128)(2,1)S(1)} %slice.8), channel_id=1, source_target_pairs={{0,32},{4,36},{8,40},{12,44},{16,48},{20,52},{24,56},{28,60},{32,6... | collective-permute-start | bytes 393224 | tf_op jit(solution)/shard_map/ppermute | solution.py:235
  73.1 0.0 collective-permute-done.16.refs_1_
  73.2 0.1 collective-permute-start.17
  73.3 4.2 %planes.8 = (bf16[512,8192]{1,0:T(8,128)(2,1)}, bf16[512,2048]{1,0:T(8,128)(2,1)}, bf16[8,512,128]{2,1,0:T(8,128)(2,1)S(1)}) custom-call(s32[16]{0:T(128)S(1)} %copy-done.4, bf16[512,256]{1,0:T(8,128)(2,1)S(1)} %copy-done.1, bf16[256,128]{1,0:T(8,128)(2,1)S(1)} %copy-done.2, ...), custom_call_target="tpu_custom_call", output_to_operand_aliasing={{0}: (6, {}), {1}: (7, {}), {2}: (8, {})} | custom-call | flops 2800000000 | bytes 3000000 | tf_op jit(solution)/shard_map/planes/pallas_call | solution.py:170
  77.5 0.0 collective-permute-done.13.refs_0_
  77.5 1.9 %collective-permute-done.17.refs_1_ = bf16[4,128,128]{2,1,0:T(8,128)(2,1)S(1)} collective-permute-done((bf16[4,128,128]{2,1,0:T(8,128)(2,1)S(1)}, bf16[4,128,128]{2,1,0:T(8,128)(2,1)S(1)}, u32[]{:S(2)}, u32[]{:S(2)}) %collective-permute-start.17) | collective-permute-done | bytes 131104 | tf_op jit(solution)/shard_map/ppermute | solution.py:236
  79.4 2.4 %planes.9 = (bf16[512,8192]{1,0:T(8,128)(2,1)}, bf16[512,2048]{1,0:T(8,128)(2,1)}, bf16[8,512,128]{2,1,0:T(8,128)(2,1)S(1)}) custom-call(s32[16]{0:T(128)S(1)} %copy-done.4, bf16[512,256]{1,0:T(8,128)(2,1)S(1)} %copy-done.1, bf16[256,128]{1,0:T(8,128)(2,1)S(1)} %copy-done.2, ...), custom_call_target="tpu_custom_call", output_to_operand_aliasing={{0}: (6, {}), {1}: (7, {}), {2}: (8, {})} | custom-call | flops 1400000000 | bytes 1500000 | tf_op jit(solution)/shard_map/planes/pallas_call | solution.py:170
  81.8 0.0 copy-start
  81.8 1.0 %copy-done = bf16[8,512,128]{2,1,0:T(8,128)(2,1)} copy-done((bf16[8,512,128]{2,1,0:T(8,128)(2,1)}, bf16[8,512,128]{2,1,0:T(8,128)(2,1)S(1)}, u32[]{:S(2)}) %copy-start) | copy-done | bytes 1048600
  82.8 2.8 %small_levels.1 = (bf16[512,512]{1,0:T(8,128)(2,1)}, bf16[512,128]{1,0:T(8,128)(2,1)}) custom-call(bf16[8,512,128]{2,1,0:T(8,128)(2,1)} %copy-done), custom_call_target="tpu_custom_call" | custom-call | tf_op jit(solution)/shard_map/small_levels/pallas_call | solution.py:238
  (15 shorter events, 0.1 us)
Async XLA Ops:
  2.7 12.5 %collective-permute-start.1 = (bf16[384,128]{1,0:T(8,128)(2,1)}, bf16[384,128]{1,0:T(8,128)(2,1)S(1)}, u32[]{:S(2)}, u32[]{:S(2)}) collective-permute-start(bf16[384,128]{1,0:T(8,128)(2,1)} %get-tuple-element.29), channel_id=1, source_target_pairs={{0,1},{1,2},{2,3},{4,5},{5,6},{6,7},{8,9},{9,10},{10,11},{12,13},{... | collective-permute-start | bytes 294920 | tf_op jit(solution)/shard_map/ppermute | solution.py:207
  4.4 10.7 %collective-permute-start = (bf16[96,256]{1,0:T(8,128)(2,1)}, bf16[96,256]{1,0:T(8,128)(2,1)S(1)}, u32[]{:S(2)}, u32[]{:S(2)}) collective-permute-start(bf16[96,256]{1,0:T(8,128)(2,1)} %get-tuple-element.28), channel_id=1, source_target_pairs={{0,4},{4,8},{8,12},{12,16},{16,20},{20,24},{24,28},{28,32},{32,36}... | collective-permute-start | bytes 147464 | tf_op jit(solution)/shard_map/ppermute | solution.py:206
  7.8 6.4 %collective-permute-start.2 = (bf16[96,128]{1,0:T(8,128)(2,1)}, bf16[96,128]{1,0:T(8,128)(2,1)S(1)}, u32[]{:S(2)}, u32[]{:S(2)}) collective-permute-start(bf16[96,128]{1,0:T(8,128)(2,1)} %get-tuple-element.30), channel_id=1, source_target_pairs={{0,5},{1,6},{2,7},{4,9},{5,10},{6,11},{8,13},{9,14},{10,15},{12,17... | collective-permute-start | bytes 73736 | tf_op jit(solution)/shard_map/ppermute | solution.py:208
  14.2 1.0 %copy-start.10 = (bf16[96,128]{1,0:T(8,128)(2,1)}, bf16[96,128]{1,0:T(8,128)(2,1)S(1)}, u32[]{:S(2)}) copy-start(bf16[96,128]{1,0:T(8,128)(2,1)S(1)} %collective-permute-done.2.corner_ref) | copy-start | bytes 73732
  15.1 0.6 copy-start.6
  15.1 0.7 copy-start.5
  18.2 5.6 %collective-permute-start.6 = (bf16[128,128]{1,0:T(8,128)(2,1)}, bf16[128,128]{1,0:T(8,128)(2,1)S(1)}, u32[]{:S(2)}, u32[]{:S(2)}) collective-permute-start(bf16[128,128]{1,0:T(8,128)(2,1)} %get-tuple-element.32), channel_id=1, source_target_pairs={{0,16},{4,20},{8,24},{12,28},{16,0},{20,4},{24,8},{28,12},{32,48},... | collective-permute-start | bytes 98312 | tf_op jit(solution)/shard_map/ppermute | solution.py:221
  24.6 5.2 %collective-permute-start.7 = (bf16[2,128,128]{2,1,0:T(8,128)(2,1)S(1)}, bf16[2,128,128]{2,1,0:T(8,128)(2,1)S(1)}, u32[]{:S(2)}, u32[]{:S(2)}) collective-permute-start(bf16[2,128,128]{2,1,0:T(8,128)(2,1)S(1)} %pad_maximum_fusion), channel_id=1, source_target_pairs={{0,12},{4,0},{8,4},{12,8},{16,28},{20,16},{24,20},{28,24},{32,44},... | collective-permute-start | bytes 196616 | tf_op jit(solution)/shard_map/ppermute | solution.py:225
  27.9 5.9 %collective-permute-start.8 = (bf16[2,128,128]{2,1,0:T(8,128)(2,1)S(1)}, bf16[2,128,128]{2,1,0:T(8,128)(2,1)S(1)}, u32[]{:S(2)}, u32[]{:S(2)}) collective-permute-start(bf16[2,128,128]{2,1,0:T(8,128)(2,1)S(1)} %pad_maximum_fusion), channel_id=1, source_target_pairs={{0,8},{4,12},{8,0},{12,4},{16,24},{20,28},{24,16},{28,20},{32,40},... | collective-permute-start | bytes 196616 | tf_op jit(solution)/shard_map/ppermute | solution.py:225
  27.9 6.8 %collective-permute-start.9 = (bf16[2,128,128]{2,1,0:T(8,128)(2,1)S(1)}, bf16[2,128,128]{2,1,0:T(8,128)(2,1)S(1)}, u32[]{:S(2)}, u32[]{:S(2)}) collective-permute-start(bf16[2,128,128]{2,1,0:T(8,128)(2,1)S(1)} %pad_maximum_fusion), channel_id=1, source_target_pairs={{0,4},{4,8},{8,12},{12,0},{16,20},{20,24},{24,28},{28,16},{32,36},... | collective-permute-start | bytes 196616 | tf_op jit(solution)/shard_map/ppermute | solution.py:225
  34.7 16.0 %collective-permute-start.10 = (bf16[8,128,128]{2,1,0:T(8,128)(2,1)S(1)}, bf16[8,128,128]{2,1,0:T(8,128)(2,1)S(1)}, u32[]{:S(2)}, u32[]{:S(2)}) collective-permute-start(bf16[8,128,128]{2,1,0:T(8,128)(2,1)S(1)} %constant_dynamic-update-slice_fusion.refs_0_), channel_id=1, source_target_pairs={{0,32},{4,36},{8,40},{12,44},{16,48},{20,52},{24,56},{28,60},{32,6... | collective-permute-start | bytes 786440 | tf_op jit(solution)/shard_map/ppermute | solution.py:232
  38.3 15.8 %collective-permute-start.14 = (bf16[8,128,128]{2,1,0:T(8,128)(2,1)S(1)}, bf16[8,128,128]{2,1,0:T(8,128)(2,1)S(1)}, u32[]{:S(2)}, u32[]{:S(2)}) collective-permute-start(bf16[8,128,128]{2,1,0:T(8,128)(2,1)S(1)} %constant_dynamic-update-slice_fusion.refs_0_), channel_id=1, source_target_pairs={{0,224},{4,228},{8,232},{12,236},{16,240},{20,244},{24,248},{28,25... | collective-permute-start | bytes 786440 | tf_op jit(solution)/shard_map/ppermute | solution.py:233
  38.3 2.5 %collective-permute-start.3 = (bf16[128,128]{1,0:T(8,128)(2,1)}, bf16[128,128]{1,0:T(8,128)(2,1)S(1)}, u32[]{:S(2)}, u32[]{:S(2)}) collective-permute-start(bf16[128,128]{1,0:T(8,128)(2,1)} %get-tuple-element.31.refs_0_), channel_id=1, source_target_pairs={{0,1},{1,0},{2,3},{3,2},{4,5},{5,4},{6,7},{7,6},{8,9},{9,8},{10,11... | collective-permute-start | bytes 98312 | tf_op jit(solution)/shard_map/ppermute | solution.py:224
  38.3 4.5 %collective-permute-start.4 = (bf16[128,128]{1,0:T(8,128)(2,1)}, bf16[128,128]{1,0:T(8,128)(2,1)S(1)}, u32[]{:S(2)}, u32[]{:S(2)}) collective-permute-start(bf16[128,128]{1,0:T(8,128)(2,1)} %get-tuple-element.31.refs_0_), channel_id=1, source_target_pairs={{0,2},{1,3},{2,0},{3,1},{4,6},{5,7},{6,4},{7,5},{8,10},{9,11},{10,... | collective-permute-start | bytes 98312 | tf_op jit(solution)/shard_map/ppermute | solution.py:224
  38.9 3.9 %collective-permute-start.5 = (bf16[128,128]{1,0:T(8,128)(2,1)}, bf16[128,128]{1,0:T(8,128)(2,1)S(1)}, u32[]{:S(2)}, u32[]{:S(2)}) collective-permute-start(bf16[128,128]{1,0:T(8,128)(2,1)} %get-tuple-element.31.refs_0_), channel_id=1, source_target_pairs={{0,3},{1,2},{2,1},{3,0},{4,7},{5,6},{6,5},{7,4},{8,11},{9,10},{10,... | collective-permute-start | bytes 98312 | tf_op jit(solution)/shard_map/ppermute | solution.py:224
  40.8 2.0 %copy-start.7 = (bf16[128,128]{1,0:T(8,128)(2,1)}, bf16[128,128]{1,0:T(8,128)(2,1)S(1)}, u32[]{:S(2)}) copy-start(bf16[128,128]{1,0:T(8,128)(2,1)S(1)} %collective-permute-done.3.refs_1_) | copy-start | bytes 98308
  42.8 0.6 copy-start.8
  42.8 0.6 copy-start.9
  45.3 0.9 %copy-start.1 = (bf16[512,256]{1,0:T(8,128)(2,1)S(1)}, bf16[512,256]{1,0:T(8,128)(2,1)}, u32[]{:S(2)}) copy-start(bf16[512,256]{1,0:T(8,128)(2,1)} %feats_one.1.first_ref) | copy-start | bytes 786436
  46.2 0.8 copy-start.2
  47.1 0.7 copy-start.3
  47.8 0.6 copy-start.4
  50.8 9.5 %collective-permute-start.11 = (bf16[8,128,128]{2,1,0:T(8,128)(2,1)S(1)}, bf16[8,128,128]{2,1,0:T(8,128)(2,1)S(1)}, u32[]{:S(2)}, u32[]{:S(2)}) collective-permute-start(bf16[8,128,128]{2,1,0:T(8,128)(2,1)S(1)} %collective-permute-done.10.refs_0_), channel_id=1, source_target_pairs={{0,32},{4,36},{8,40},{12,44},{16,48},{20,52},{24,56},{28,60},{32,6... | collective-permute-start | bytes 786440 | tf_op jit(solution)/shard_map/ppermute | solution.py:232
  54.1 9.9 %collective-permute-start.15 = (bf16[8,128,128]{2,1,0:T(8,128)(2,1)S(1)}, bf16[8,128,128]{2,1,0:T(8,128)(2,1)S(1)}, u32[]{:S(2)}, u32[]{:S(2)}) collective-permute-start(bf16[8,128,128]{2,1,0:T(8,128)(2,1)S(1)} %collective-permute-done.14.refs_1_), channel_id=1, source_target_pairs={{0,224},{4,228},{8,232},{12,236},{16,240},{20,244},{24,248},{28,25... | collective-permute-start | bytes 786440 | tf_op jit(solution)/shard_map/ppermute | solution.py:233
  60.3 9.1 %collective-permute-start.12 = (bf16[8,128,128]{2,1,0:T(8,128)(2,1)S(1)}, bf16[8,128,128]{2,1,0:T(8,128)(2,1)S(1)}, u32[]{:S(2)}, u32[]{:S(2)}) collective-permute-start(bf16[8,128,128]{2,1,0:T(8,128)(2,1)S(1)} %collective-permute-done.11.refs_0_), channel_id=1, source_target_pairs={{0,32},{4,36},{8,40},{12,44},{16,48},{20,52},{24,56},{28,60},{32,6... | collective-permute-start | bytes 786440 | tf_op jit(solution)/shard_map/ppermute | solution.py:232
  64.0 9.2 %collective-permute-start.16 = (bf16[8,128,128]{2,1,0:T(8,128)(2,1)S(1)}, bf16[8,128,128]{2,1,0:T(8,128)(2,1)S(1)}, u32[]{:S(2)}, u32[]{:S(2)}) collective-permute-start(bf16[8,128,128]{2,1,0:T(8,128)(2,1)S(1)} %collective-permute-done.15.refs_1_), channel_id=1, source_target_pairs={{0,224},{4,228},{8,232},{12,236},{16,240},{20,244},{24,248},{28,25... | collective-permute-start | bytes 786440 | tf_op jit(solution)/shard_map/ppermute | solution.py:233
  69.4 8.1 %collective-permute-start.13 = (bf16[4,128,128]{2,1,0:T(8,128)(2,1)S(1)}, bf16[4,128,128]{2,1,0:T(8,128)(2,1)S(1)}, u32[]{:S(2)}, u32[]{:S(2)}) collective-permute-start(bf16[4,128,128]{2,1,0:T(8,128)(2,1)S(1)} %slice.8), channel_id=1, source_target_pairs={{0,32},{4,36},{8,40},{12,44},{16,48},{20,52},{24,56},{28,60},{32,6... | collective-permute-start | bytes 393224 | tf_op jit(solution)/shard_map/ppermute | solution.py:235
  73.2 6.3 %collective-permute-start.17 = (bf16[4,128,128]{2,1,0:T(8,128)(2,1)S(1)}, bf16[4,128,128]{2,1,0:T(8,128)(2,1)S(1)}, u32[]{:S(2)}, u32[]{:S(2)}) collective-permute-start(bf16[4,128,128]{2,1,0:T(8,128)(2,1)S(1)} %slice.9), channel_id=1, source_target_pairs={{0,224},{4,228},{8,232},{12,236},{16,240},{20,244},{24,248},{28,25... | collective-permute-start | bytes 393224 | tf_op jit(solution)/shard_map/ppermute | solution.py:236
  81.8 1.0 %copy-start = (bf16[8,512,128]{2,1,0:T(8,128)(2,1)}, bf16[8,512,128]{2,1,0:T(8,128)(2,1)S(1)}, u32[]{:S(2)}) copy-start(bf16[8,512,128]{2,1,0:T(8,128)(2,1)S(1)} %get-tuple-element.47.small_ref) | copy-start | bytes 3145732

commit v3 on v2

v3 whole, which is shorter than its diff:
```python
import functools

import jax
import jax.numpy as jnp
from jax import lax
from jax.experimental import pallas as pl
from jax.experimental.pallas import tpu as pltpu
from jax.sharding import PartitionSpec as P

Z, YH, X = 8, 2, 4
PLANE = YH * X
ROWS, COLS = Z * PLANE, 4
BF, F32 = jnp.bfloat16, jnp.float32


def dot(a, b):
    return jnp.dot(a, b, preferred_element_type=F32)


def iotas(*shape):
    return lax.broadcasted_iota(jnp.int32, shape, 0), lax.broadcasted_iota(jnp.int32, shape, 1)


def position():
    r = lax.axis_index("rows")
    return r // PLANE, r // X % YH, r % X


VMEM, SMEM = pl.BlockSpec(memory_space=pltpu.VMEM), pl.BlockSpec(memory_space=pltpu.SMEM)
ANYWHERE = pl.BlockSpec(memory_space=pl.ANY)
SMALL = pltpu.CompilerParams(vmem_limit_bytes=12 << 20)


def one_hot(mask, value=1.0):
    return jnp.where(mask, value, 0.0).astype(BF)


def split_kernel(tile_ref, main_ref, left_ref):
    row, col = iotas(384, 384)
    tap = (row >= 96).astype(jnp.int32) + (row >= 192).astype(jnp.int32) + (row >= 288).astype(jnp.int32)
    order = one_hot(col == (row - 96 * tap) * 4 + tap)
    main = dot(order, jnp.concatenate([tile_ref[0], tile_ref[1]], axis=1)).astype(BF)
    row, col = iotas(256, 128)
    rim = one_hot(((row == 127) & (col == 0)) | ((row == 255) & (col == 64)))
    main_ref[...] = main
    left_ref[...] = dot(main, rim).astype(BF)


def split_tile(images):
    return pl.pallas_call(
        split_kernel,
        out_shape=[jax.ShapeDtypeStruct((384, 256), BF), jax.ShapeDtypeStruct((384, 128), BF)],
        compiler_params=SMALL,
        name="split_tile",
    )(images.reshape(2, 384, 128))


def hidden_kernel(main_ref, top_ref, left_ref, weight_ref, bias_ref, one_ref, two_ref):
    rows = jnp.concatenate([top_ref[:, :256], main_ref[...]], axis=0)
    row, col = iotas(256, 384)
    source = 2 * (col & 63) - 1 + (col >> 7) + jnp.where((col & 64) != 0, 128, 0)
    valid = ((col & 63) != 0) | (col >= 128)
    taps = dot(rows, one_hot((row == source) & valid))
    rim = jnp.concatenate([top_ref[:, 256:], left_ref[...]], axis=0).astype(F32)
    first = (taps[:, :128] + rim).astype(BF)
    parts = [first, taps[:, 128:256].astype(BF), taps[:, 256:384].astype(BF)]
    stacked = jnp.concatenate(
        [
            jnp.concatenate(
                [parts[b][(2 * i + a) * 96 : (2 * i + a + 1) * 96] for a in range(3) for b in range(3)], axis=0
            )
            for i in range(2)
        ],
        axis=1,
    )
    pre = lax.dot_general(weight_ref[...], stacked, (((0,), (0,)), ((), ())), preferred_element_type=F32)
    bias = jnp.transpose(jnp.broadcast_to(bias_ref[...], (128, 128)))
    hidden = [jnp.maximum(pre[:, i * 128 : (i + 1) * 128] + bias, 0.0) for i in range(2)]
    lane = lax.broadcasted_iota(jnp.int32, (128, 128), 1)
    one_ref[...] = jnp.where(lane < 64, hidden[0], pltpu.roll(hidden[1], 64, 1)).astype(BF)
    two_ref[...] = jnp.where(lane < 64, pltpu.roll(hidden[0], 64, 1), hidden[1]).astype(BF)


def hidden_of(main, top, left, conv_weight, conv_bias):
    return pl.pallas_call(
        hidden_kernel,
        out_shape=[jax.ShapeDtypeStruct((128, 128), BF)] * 2,
        compiler_params=SMALL,
        name="hidden",
    )(main, top, left, conv_weight.T, conv_bias[None, :])


def feats_one_kernel(*refs):
    hid_refs, (weight_ref, bias_ref, out_ref) = refs[:4], refs[4:]
    for m in range(4):
        k = lax.axis_index("cols") ^ m
        feats = lax.dot_general(
            hid_refs[m][...], weight_ref[...], (((0,), (1,)), ((), ())), preferred_element_type=F32
        )
        feats = (feats + bias_ref[...]).astype(BF) * jnp.bfloat16(0.0625)
        for i in range(2):
            out_ref[pl.ds(pl.multiple_of(i * 256 + k * 64, 64), 64), :] = feats[i * 64 : (i + 1) * 64, :]


def feats_one(hidden, proj_weight, proj_bias):
    return pl.pallas_call(
        feats_one_kernel,
        out_shape=jax.ShapeDtypeStruct((512, 256), BF),
        compiler_params=SMALL,
        name="feats_one",
    )(*hidden, proj_weight, proj_bias[None, :])


def planes_kernel(offsets, last, n_alias, first_ref, weight_ref, bias_ref, *refs):
    n_hid = 2 if last else len(offsets)
    hid_refs, rest = refs[:n_hid], refs[n_hid + n_alias :]
    if last:
        small_ref, zero_out, one_out, two_out, three_out, zero_buf, one_buf, two_buf, three_buf, hid_buf, sems = rest
    else:
        zero_out, one_out, small_out, zero_buf, one_buf, small_buf, sems = rest
    z, yh, x = position()
    order = [((j % X - x) & (X - 1)) * 2 + (yh ^ (j // X)) for j in range(PLANE)]
    row, col = iotas(512, 128)
    pool1 = one_hot(col == (row >> 7) * 32 + ((row & 63) >> 1), 0.25)
    row, col = iotas(256, 64)
    pool2 = one_hot(col == (row >> 6) * 16 + ((row & 31) >> 1), 0.25)
    row, col = iotas(64, 64)
    pool3 = one_hot(col == (row >> 5) * 8 + ((row & 15) >> 1), 0.25)
    bias = jnp.concatenate(
        [jnp.transpose(jnp.broadcast_to(bias_ref[n : n + 1, :], (128, 128))) for n in range(2)], axis=0
    )
    bias = jnp.concatenate([bias] * 4, axis=1)
    copies = []

    def send(source, target):
        copies.append(pltpu.make_async_copy(source, target, sems.at[len(copies)]))
        copies[-1].start()

    for n, offset in enumerate(offsets):
        place = (z + (offset + Z)) & (Z - 1)
        if last:
            hid_buf[0:4] = hid_refs[0][...]
            hid_buf[4:8] = hid_refs[1][...]
            hid_ref = hid_buf
        else:
            hid_ref = hid_refs[n]
        ones = []
        for half in range(2):
            hid = jnp.concatenate([hid_ref[order[4 * half + j]] for j in range(4)], axis=1)
            feats = (dot(weight_ref[...], hid) + bias).astype(BF)
            zero = dot(first_ref[...], feats).astype(BF)
            slot = 2 * n + half
            zero_buf[slot] = zero
            send(zero_buf.at[slot], zero_out.at[:, pl.ds(pl.multiple_of(place * 1024 + half * 512, 512), 512)])
            ones.append(dot(zero, pool1).astype(BF))
        one = jnp.concatenate(ones, axis=1)
        one_buf[n] = one
        send(one_buf.at[n], one_out.at[:, pl.ds(pl.multiple_of(place * 256, 256), 256)])
        two = dot(one, pool2).astype(BF)
        three = dot(two, pool3).astype(BF)
        small = jnp.concatenate([two, three], axis=1)
        if not last:
            small_buf[n] = small
            send(small_buf.at[n], small_out.at[place])
    if last:
        for m in range(Z):
            piece = jnp.where(place == m, small, small_ref[m])
            two_buf[:, m * 64 : (m + 1) * 64] = piece[:, 0:64]
            three_buf[:, m * 16 : (m + 1) * 16] = piece[:, 64:80]
        send(two_buf, two_out)
        send(three_buf, three_out)
    for copy in copies:
        copy.wait()


def planes_call(offsets, hidden, first, proj_weight, proj_bias, outs, last=False):
    count = len(offsets)
    args = [first, proj_weight, proj_bias.reshape(2, 128), *hidden]
    in_specs = [VMEM] * len(args)
    aliases = {}
    if outs is not None:
        shared = 2 if last else 3
        aliases = {len(args) + n: n for n in range(shared)}
        args += list(outs)
        in_specs += [ANYWHERE] * shared + [VMEM] * (3 - shared)
    shapes = [(512, 8192), (512, 2048)] + ([(512, 512), (512, 128)] if last else [(8, 512, 128)])
    scratch = [(2 * count, 512, 512), (count, 512, 256)]
    scratch += [(512, 512), (512, 128), (8, 128, 128)] if last else [(count, 512, 128)]
    return pl.pallas_call(
        functools.partial(planes_kernel, offsets, last, len(aliases)),
        in_specs=in_specs,
        out_specs=[ANYWHERE] * len(shapes),
        out_shape=[jax.ShapeDtypeStruct(shape, BF) for shape in shapes],
        scratch_shapes=[pltpu.VMEM(shape, BF) for shape in scratch] + [pltpu.SemaphoreType.DMA((5 * count,))],
        input_output_aliases=aliases,
        compiler_params=pltpu.CompilerParams(vmem_limit_bytes=24 << 20),
        cost_estimate=pl.CostEstimate(
            flops=1_400_000_000 * count, bytes_accessed=1_500_000 * count, transcendentals=0
        ),
        name="planes",
    )(*args)


def per_device(images, conv_weight, conv_bias, proj_weight, proj_bias):
    right = [(c, c + 1) for c in range(COLS - 1)]
    down = [(r, r + 1) for r in range(ROWS - 1)]
    main, left = split_tile(images)
    left = lax.ppermute(left, "cols", right)
    top = lax.ppermute(jnp.concatenate([main[288:], left[288:]], axis=1), "rows", down)
    hidden_one, hidden_two = hidden_of(main, top, left, conv_weight, conv_bias)

    def along(axis, steps):
        size, stride = {"z": (Z, PLANE), "yh": (YH, X), "x": (X, 1)}[axis]
        target = lambda r: r + ((r // stride + steps) % size - (r // stride) % size) * stride
        return [(r, target(r)) for r in range(ROWS)]

    other = lax.ppermute(hidden_two, "rows", along("yh", 1))
    pair = jnp.stack([hidden_two, other])
    ones = [hidden_one]
    ones += [lax.ppermute(hidden_one, "cols", [(k, k ^ m) for k in range(COLS)]) for m in range(1, 4)]
    mine = jnp.concatenate([pair] + [lax.ppermute(pair, "rows", along("x", -s)) for s in range(1, X)])
    mine, ones = lax.optimization_barrier((mine, ones))
    first = feats_one(ones, proj_weight, proj_bias)

    call = functools.partial(planes_call, first=first, proj_weight=proj_weight, proj_bias=proj_bias)
    below, above = mine, mine
    outs = call((0,), [mine], outs=None)
    for step in range(1, Z // 2):
        below = lax.ppermute(below, "rows", along("z", 1))
        above = lax.ppermute(above, "rows", along("z", -1))
        outs = call((-step, step), [below, above], outs=outs)
    below = lax.ppermute(below[:4], "rows", along("z", 1))
    above = lax.ppermute(above[4:], "rows", along("z", -1))
    return tuple(call((Z // 2,), [below, above], outs=outs, last=True))


def solution(mesh):
    in_specs = (P(None, None, "rows", "cols"), P(), P(), P(), P())
    out_specs = (P("rows", "cols"), P("rows", "cols"), P("rows", "cols"), P("rows", "cols"))
    return jax.shard_map(
        per_device, mesh=mesh, in_specs=in_specs, out_specs=out_specs, check_vma=False
    )
```

time: 86.2 us -> 78.4 us (0.910)
  the two profiles are of different devices: /device:TPU:96 before, /device:TPU:104 now
where the time goes in v3:
time: 78.4 us; the launch traced here: 78 us
  waiting for transfers between devices  30.2 us (39%)
  starting transfers between devices  24.4 us (31%)
  Pallas kernels  16.9 us (22%)
  local copies, waits for them, and re-layouts  5.62 us (7%)
  between operations  0.99 us (1%)
    pallas_call x5, Pallas kernels, planes_call(): pl.pallas_call(functools.partial(planes_kernel, offsets, last, len(aliase...  15.5 us
    ppermute x3, starting transfers between devices, per_device(): below = lax.ppermute(below, 'rows', along('z', 1))  11.6 us
    ppermute x3, waiting for transfers between devices, per_device(): lax.ppermute(pair, 'rows', along('x', -s))  9.58 us
    ppermute x1, waiting for transfers between devices, per_device(): lax.ppermute(jnp.concatenate([main[288:], left[288:]], axis=1), 'rows', d...  7.35 us
    unnamed x18, local copies, waits for them, and re-layouts  5.58 us
    ppermute x1, waiting for transfers between devices, per_device(): left = lax.ppermute(left, 'cols', right)  3.99 us
    ppermute x1, starting transfers between devices, per_device(): below = lax.ppermute(below[:4], 'rows', along('z', 1))  3.77 us
    ppermute x1, starting transfers between devices, per_device(): lax.ppermute(jnp.concatenate([main[288:], left[288:]], axis=1), 'rows', d...  3.4 us
  transfers between devices with their start and end apart: 17, of which 12 were waited for; matrix products, arithmetic and copies ran while one was open for 0% of the time, Pallas kernels for 16%

profile of v3, /device:TPU:104, one launch (start us, length us, event | category | flops | bytes accessed | tf_op | source)
XLA Modules:
  0.0 78.0 jit_solution(1975440089845118874)
XLA Ops:
  0.6 0.0 copy-start.3
  0.6 0.9 %copy-done.3 = bf16[2,96,4,128]{3,2,1,0:T(4,128)(2,1)S(1)} copy-done((bf16[2,96,4,128]{3,2,1,0:T(4,128)(2,1)S(1)}, bf16[2,96,4,128]{3,2,1,0:T(4,128)(2,1)}, u32[]{:S(2)}) %copy-start.3) | copy-done | bytes 196632
  1.6 0.5 split_tile.1
  2.0 1.9 %collective-permute-start = (bf16[384,128]{1,0:T(8,128)(2,1)S(1)}, bf16[384,128]{1,0:T(8,128)(2,1)S(1)}, u32[]{:S(2)}, u32[]{:S(2)}) collective-permute-start(bf16[384,128]{1,0:T(8,128)(2,1)S(1)} %get-tuple-element.26), channel_id=1, source_target_pairs={{0,1},{1,2},{2,3},{4,5},{5,6},{6,7},{8,9},{9,10},{10,11},{12,13},{... | collective-permute-start | bytes 294920 | tf_op jit(solution)/shard_map/ppermute | solution.py:208
  4.0 4.0 %collective-permute-done.left_ref = bf16[384,128]{1,0:T(8,128)(2,1)S(1)} collective-permute-done((bf16[384,128]{1,0:T(8,128)(2,1)S(1)}, bf16[384,128]{1,0:T(8,128)(2,1)S(1)}, u32[]{:S(2)}, u32[]{:S(2)}) %collective-permute-start) | collective-permute-done | bytes 98336 | tf_op jit(solution)/shard_map/ppermute | solution.py:208
  8.0 3.4 %collective-permute-start.1 = (bf16[96,384]{1,0:T(8,128)(2,1)S(1)}, bf16[96,384]{1,0:T(8,128)(2,1)S(1)}, u32[]{:S(2)}, u32[]{:S(2)}) collective-permute-start(bf16[96,384]{1,0:T(8,128)(2,1)S(1)} %pad_maximum_fusion), channel_id=1, source_target_pairs={{0,4},{4,8},{8,12},{12,16},{16,20},{20,24},{24,28},{28,32},{32,36}... | collective-permute-start | bytes 221192 | tf_op jit(solution)/shard_map/ppermute | solution.py:209
  11.4 7.4 %collective-permute-done.1.top_ref = bf16[96,384]{1,0:T(8,128)(2,1)S(1)} collective-permute-done((bf16[96,384]{1,0:T(8,128)(2,1)S(1)}, bf16[96,384]{1,0:T(8,128)(2,1)S(1)}, u32[]{:S(2)}, u32[]{:S(2)}) %collective-permute-start.1) | collective-permute-done | bytes 73760 | tf_op jit(solution)/shard_map/ppermute | solution.py:209
  18.8 0.0 copy-start.2
  18.8 0.9 %copy-done.2 = bf16[128,864]{0,1:T(8,128)(2,1)S(1)} copy-done((bf16[128,864]{0,1:T(8,128)(2,1)S(1)}, bf16[128,864]{0,1:T(8,128)(2,1)}, u32[]{:S(2)}) %copy-start.2) | copy-done | bytes 221208
  19.7 0.0 copy-start.6
  19.7 0.7 copy-done.6
  20.4 0.6 hidden.1
  21.0 1.5 %collective-permute-start.2 = (bf16[128,128]{1,0:T(8,128)(2,1)S(1)}, bf16[128,128]{1,0:T(8,128)(2,1)S(1)}, u32[]{:S(2)}, u32[]{:S(2)}) collective-permute-start(bf16[128,128]{1,0:T(8,128)(2,1)S(1)} %get-tuple-element.27), channel_id=1, source_target_pairs={{0,16},{4,20},{8,24},{12,28},{16,0},{20,4},{24,8},{28,12},{32,48},... | collective-permute-start | bytes 98312 | tf_op jit(solution)/shard_map/ppermute | solution.py:217
  22.5 0.0 collective-permute-start.6
  22.5 0.0 collective-permute-start.7
  22.5 1.9 %collective-permute-start.8 = (bf16[128,128]{1,0:T(8,128)(2,1)S(1)}, bf16[128,128]{1,0:T(8,128)(2,1)S(1)}, u32[]{:S(2)}, u32[]{:S(2)}) collective-permute-start(bf16[128,128]{1,0:T(8,128)(2,1)S(1)} %get-tuple-element.29.refs_0_), channel_id=1, source_target_pairs={{0,3},{1,2},{2,1},{3,0},{4,7},{5,6},{6,5},{7,4},{8,11},{9,10},{10,... | collective-permute-start | bytes 98312 | tf_op jit(solution)/shard_map/ppermute | solution.py:220
  24.4 2.3 %collective-permute-done.2 = bf16[128,128]{1,0:T(8,128)(2,1)S(1)} collective-permute-done((bf16[128,128]{1,0:T(8,128)(2,1)S(1)}, bf16[128,128]{1,0:T(8,128)(2,1)S(1)}, u32[]{:S(2)}, u32[]{:S(2)}) %collective-permute-start.2) | collective-permute-done | bytes 32800 | tf_op jit(solution)/shard_map/ppermute | solution.py:217
  26.7 0.1 collective-permute-start.3
  26.8 0.1 collective-permute-start.4
  26.9 4.1 %collective-permute-done.3 = bf16[2,128,128]{2,1,0:T(8,128)(2,1)S(1)} collective-permute-done((bf16[2,128,128]{2,1,0:T(8,128)(2,1)S(1)}, bf16[2,128,128]{2,1,0:T(8,128)(2,1)S(1)}, u32[]{:S(2)}, u32[]{:S(2)}) %collective-permute-start.3) | collective-permute-done | bytes 65568 | tf_op jit(solution)/shard_map/ppermute | solution.py:221
  31.0 0.0 collective-permute-start.5
  31.1 1.9 %collective-permute-done.4 = bf16[2,128,128]{2,1,0:T(8,128)(2,1)S(1)} collective-permute-done((bf16[2,128,128]{2,1,0:T(8,128)(2,1)S(1)}, bf16[2,128,128]{2,1,0:T(8,128)(2,1)S(1)}, u32[]{:S(2)}, u32[]{:S(2)}) %collective-permute-start.4) | collective-permute-done | bytes 65568 | tf_op jit(solution)/shard_map/ppermute | solution.py:221
  33.0 3.5 %collective-permute-done.5 = bf16[2,128,128]{2,1,0:T(8,128)(2,1)S(1)} collective-permute-done((bf16[2,128,128]{2,1,0:T(8,128)(2,1)S(1)}, bf16[2,128,128]{2,1,0:T(8,128)(2,1)S(1)}, u32[]{:S(2)}, u32[]{:S(2)}) %collective-permute-start.5) | collective-permute-done | bytes 65568 | tf_op jit(solution)/shard_map/ppermute | solution.py:221
  36.5 0.0 collective-permute-done.6.refs_1_
  36.5 0.0 collective-permute-done.7.refs_2_
  36.5 0.0 collective-permute-done.8.refs_3_
  36.6 4.4 %collective-permute-start.9 = (bf16[8,128,128]{2,1,0:T(8,128)(2,1)S(1)}, bf16[8,128,128]{2,1,0:T(8,128)(2,1)S(1)}, u32[]{:S(2)}, u32[]{:S(2)}) collective-permute-start(bf16[8,128,128]{2,1,0:T(8,128)(2,1)S(1)} %constant_dynamic-update-slice_fusion.refs_0_), channel_id=1, source_target_pairs={{0,32},{4,36},{8,40},{12,44},{16,48},{20,52},{24,56},{28,60},{32,6... | collective-permute-start | bytes 786440 | tf_op jit(solution)/shard_map/ppermute | solution.py:229
  41.0 0.0 collective-permute-start.13
  41.0 0.0 copy-start
  41.0 0.8 %copy-done = bf16[256,128]{1,0:T(8,128)(2,1)S(1)} copy-done((bf16[256,128]{1,0:T(8,128)(2,1)S(1)}, bf16[256,128]{1,0:T(8,128)(2,1)}, u32[]{:S(2)}) %copy-start) | copy-done | bytes 65560
  41.8 0.0 copy-start.4
  41.8 0.7 copy-done.4
  42.5 0.3 feats_one.1.first_ref
  42.8 0.0 copy-start.1
  42.8 0.8 %copy-done.1 = bf16[256,128]{1,0:T(8,128)(2,1)S(1)} copy-done((bf16[256,128]{1,0:T(8,128)(2,1)S(1)}, bf16[256,128]{1,0:T(8,128)(2,1)}, u32[]{:S(2)}) %copy-start.1) | copy-done | bytes 65560
  43.6 0.0 copy-start.5
  43.6 0.7 copy-done.5
  44.3 1.9 %planes.5 = (bf16[512,8192]{1,0:T(8,128)(2,1)}, bf16[512,2048]{1,0:T(8,128)(2,1)}, bf16[8,512,128]{2,1,0:T(8,128)(2,1)S(1)}) custom-call(bf16[512,256]{1,0:T(8,128)(2,1)S(1)} %feats_one.1.first_ref, bf16[256,128]{1,0:T(8,128)(2,1)S(1)} %copy-done.1, f32[2,128]{1,0:T(2,128)S(1)} %bitcast.13, bf16[8,128,128]{2,1,0:T(8,128)(2,1)S(1)} %constant_dynamic-update-slice_fusion.refs_0_), custom_call_target="tpu_custom_call" | custom-call | flops 1400000000 | bytes 1500000 | tf_op jit(solution)/shard_map/planes/pallas_call | solution.py:189
  46.2 0.0 collective-permute-done.9.refs_0_
  46.2 3.5 %collective-permute-start.10 = (bf16[8,128,128]{2,1,0:T(8,128)(2,1)S(1)}, bf16[8,128,128]{2,1,0:T(8,128)(2,1)S(1)}, u32[]{:S(2)}, u32[]{:S(2)}) collective-permute-start(bf16[8,128,128]{2,1,0:T(8,128)(2,1)S(1)} %collective-permute-done.9.refs_0_), channel_id=1, source_target_pairs={{0,32},{4,36},{8,40},{12,44},{16,48},{20,52},{24,56},{28,60},{32,6... | collective-permute-start | bytes 786440 | tf_op jit(solution)/shard_map/ppermute | solution.py:229
  49.7 0.3 collective-permute-done.13.refs_1_
  50.0 0.0 collective-permute-start.14
  50.0 3.5 %planes.6 = (bf16[512,8192]{1,0:T(8,128)(2,1)}, bf16[512,2048]{1,0:T(8,128)(2,1)}, bf16[8,512,128]{2,1,0:T(8,128)(2,1)S(1)}) custom-call(bf16[512,256]{1,0:T(8,128)(2,1)S(1)} %feats_one.1.first_ref, bf16[256,128]{1,0:T(8,128)(2,1)S(1)} %copy-done.1, f32[2,128]{1,0:T(2,128)S(1)} %bitcast.14, ...), custom_call_target="tpu_custom_call", output_to_operand_aliasing={{0}: (5, {}), {1}: (6, {}), {2}: (7, {})} | custom-call | flops 2800000000 | bytes 3000000 | tf_op jit(solution)/shard_map/planes/pallas_call | solution.py:189
  53.5 2.5 %collective-permute-done.10.refs_0_ = bf16[8,128,128]{2,1,0:T(8,128)(2,1)S(1)} collective-permute-done((bf16[8,128,128]{2,1,0:T(8,128)(2,1)S(1)}, bf16[8,128,128]{2,1,0:T(8,128)(2,1)S(1)}, u32[]{:S(2)}, u32[]{:S(2)}) %collective-permute-start.10) | collective-permute-done | bytes 262176 | tf_op jit(solution)/shard_map/ppermute | solution.py:229
  56.0 3.7 %collective-permute-start.11 = (bf16[8,128,128]{2,1,0:T(8,128)(2,1)S(1)}, bf16[8,128,128]{2,1,0:T(8,128)(2,1)S(1)}, u32[]{:S(2)}, u32[]{:S(2)}) collective-permute-start(bf16[8,128,128]{2,1,0:T(8,128)(2,1)S(1)} %collective-permute-done.10.refs_0_), channel_id=1, source_target_pairs={{0,32},{4,36},{8,40},{12,44},{16,48},{20,52},{24,56},{28,60},{32,6... | collective-permute-start | bytes 786440 | tf_op jit(solution)/shard_map/ppermute | solution.py:229
  59.7 0.5 collective-permute-done.14.refs_1_
  60.2 0.0 collective-permute-start.15
  60.2 3.5 %planes.7 = (bf16[512,8192]{1,0:T(8,128)(2,1)}, bf16[512,2048]{1,0:T(8,128)(2,1)}, bf16[8,512,128]{2,1,0:T(8,128)(2,1)S(1)}) custom-call(bf16[512,256]{1,0:T(8,128)(2,1)S(1)} %feats_one.1.first_ref, bf16[256,128]{1,0:T(8,128)(2,1)S(1)} %copy-done.1, f32[2,128]{1,0:T(2,128)S(1)} %bitcast.15, ...), custom_call_target="tpu_custom_call", output_to_operand_aliasing={{0}: (5, {}), {1}: (6, {}), {2}: (7, {})} | custom-call | flops 2800000000 | bytes 3000000 | tf_op jit(solution)/shard_map/planes/pallas_call | solution.py:189
  63.6 0.7 collective-permute-done.11.refs_0_
  64.3 3.8 %collective-permute-start.12 = (bf16[4,128,128]{2,1,0:T(8,128)(2,1)S(1)}, bf16[4,128,128]{2,1,0:T(8,128)(2,1)S(1)}, u32[]{:S(2)}, u32[]{:S(2)}) collective-permute-start(bf16[4,128,128]{2,1,0:T(8,128)(2,1)S(1)} %slice.17), channel_id=1, source_target_pairs={{0,32},{4,36},{8,40},{12,44},{16,48},{20,52},{24,56},{28,60},{32,6... | collective-permute-start | bytes 393224 | tf_op jit(solution)/shard_map/ppermute | solution.py:232
  68.1 0.3 collective-permute-done.15.refs_1_
  68.4 0.1 collective-permute-start.16
  68.5 3.5 %planes.8 = (bf16[512,8192]{1,0:T(8,128)(2,1)}, bf16[512,2048]{1,0:T(8,128)(2,1)}, bf16[8,512,128]{2,1,0:T(8,128)(2,1)S(1)}) custom-call(bf16[512,256]{1,0:T(8,128)(2,1)S(1)} %feats_one.1.first_ref, bf16[256,128]{1,0:T(8,128)(2,1)S(1)} %copy-done.1, f32[2,128]{1,0:T(2,128)S(1)} %bitcast.16, ...), custom_call_target="tpu_custom_call", output_to_operand_aliasing={{0}: (5, {}), {1}: (6, {}), {2}: (7, {})} | custom-call | flops 2800000000 | bytes 3000000 | tf_op jit(solution)/shard_map/planes/pallas_call | solution.py:189
  72.0 0.0 collective-permute-done.12.refs_0_
  72.0 2.7 %collective-permute-done.16.refs_1_ = bf16[4,128,128]{2,1,0:T(8,128)(2,1)S(1)} collective-permute-done((bf16[4,128,128]{2,1,0:T(8,128)(2,1)S(1)}, bf16[4,128,128]{2,1,0:T(8,128)(2,1)S(1)}, u32[]{:S(2)}, u32[]{:S(2)}) %collective-permute-start.16) | collective-permute-done | bytes 131104 | tf_op jit(solution)/shard_map/ppermute | solution.py:233
  74.7 3.2 %planes.9 = (bf16[512,8192]{1,0:T(8,128)(2,1)}, bf16[512,2048]{1,0:T(8,128)(2,1)}, bf16[512,512]{1,0:T(8,128)(2,1)}, bf16[512,128]{1,0:T(8,128)(2,1)}) custom-call(bf16[512,256]{1,0:T(8,128)(2,1)S(1)} %feats_one.1.first_ref, bf16[256,128]{1,0:T(8,128)(2,1)S(1)} %copy-done.1, f32[2,128]{1,0:T(2,128)S(1)} %bitcast.17, ...), custom_call_target="tpu_custom_call", output_to_operand_aliasing={{0}: (5, {}), {1}: (6, {})} | custom-call | flops 1400000000 | bytes 1500000 | tf_op jit(solution)/shard_map/planes/pallas_call | solution.py:189
  (11 shorter events, 0.1 us)
Async XLA Ops:
  0.6 0.9 %copy-start.3 = (bf16[2,96,4,128]{3,2,1,0:T(4,128)(2,1)S(1)}, bf16[2,96,4,128]{3,2,1,0:T(4,128)(2,1)}, u32[]{:S(2)}) copy-start(bf16[2,96,4,128]{3,2,1,0:T(4,128)(2,1)} %param.5) | copy-start | bytes 589828
  2.0 5.9 %collective-permute-start = (bf16[384,128]{1,0:T(8,128)(2,1)S(1)}, bf16[384,128]{1,0:T(8,128)(2,1)S(1)}, u32[]{:S(2)}, u32[]{:S(2)}) collective-permute-start(bf16[384,128]{1,0:T(8,128)(2,1)S(1)} %get-tuple-element.26), channel_id=1, source_target_pairs={{0,1},{1,2},{2,3},{4,5},{5,6},{6,7},{8,9},{9,10},{10,11},{12,13},{... | collective-permute-start | bytes 294920 | tf_op jit(solution)/shard_map/ppermute | solution.py:208
  8.0 10.8 %collective-permute-start.1 = (bf16[96,384]{1,0:T(8,128)(2,1)S(1)}, bf16[96,384]{1,0:T(8,128)(2,1)S(1)}, u32[]{:S(2)}, u32[]{:S(2)}) collective-permute-start(bf16[96,384]{1,0:T(8,128)(2,1)S(1)} %pad_maximum_fusion), channel_id=1, source_target_pairs={{0,4},{4,8},{8,12},{12,16},{16,20},{20,24},{24,28},{28,32},{32,36}... | collective-permute-start | bytes 221192 | tf_op jit(solution)/shard_map/ppermute | solution.py:209
  18.8 0.9 %copy-start.2 = (bf16[128,864]{0,1:T(8,128)(2,1)S(1)}, bf16[128,864]{0,1:T(8,128)(2,1)}, u32[]{:S(2)}) copy-start(bf16[128,864]{0,1:T(8,128)(2,1)} %param.6) | copy-start | bytes 663556
  19.7 0.7 copy-start.6
  21.0 5.7 %collective-permute-start.2 = (bf16[128,128]{1,0:T(8,128)(2,1)S(1)}, bf16[128,128]{1,0:T(8,128)(2,1)S(1)}, u32[]{:S(2)}, u32[]{:S(2)}) collective-permute-start(bf16[128,128]{1,0:T(8,128)(2,1)S(1)} %get-tuple-element.27), channel_id=1, source_target_pairs={{0,16},{4,20},{8,24},{12,28},{16,0},{20,4},{24,8},{28,12},{32,48},... | collective-permute-start | bytes 98312 | tf_op jit(solution)/shard_map/ppermute | solution.py:217
  22.5 14.0 %collective-permute-start.6 = (bf16[128,128]{1,0:T(8,128)(2,1)S(1)}, bf16[128,128]{1,0:T(8,128)(2,1)S(1)}, u32[]{:S(2)}, u32[]{:S(2)}) collective-permute-start(bf16[128,128]{1,0:T(8,128)(2,1)S(1)} %get-tuple-element.29.refs_0_), channel_id=1, source_target_pairs={{0,1},{1,0},{2,3},{3,2},{4,5},{5,4},{6,7},{7,6},{8,9},{9,8},{10,11... | collective-permute-start | bytes 98312 | tf_op jit(solution)/shard_map/ppermute | solution.py:220
  22.5 14.0 %collective-permute-start.7 = (bf16[128,128]{1,0:T(8,128)(2,1)S(1)}, bf16[128,128]{1,0:T(8,128)(2,1)S(1)}, u32[]{:S(2)}, u32[]{:S(2)}) collective-permute-start(bf16[128,128]{1,0:T(8,128)(2,1)S(1)} %get-tuple-element.29.refs_0_), channel_id=1, source_target_pairs={{0,2},{1,3},{2,0},{3,1},{4,6},{5,7},{6,4},{7,5},{8,10},{9,11},{10,... | collective-permute-start | bytes 98312 | tf_op jit(solution)/shard_map/ppermute | solution.py:220
  22.5 14.1 %collective-permute-start.8 = (bf16[128,128]{1,0:T(8,128)(2,1)S(1)}, bf16[128,128]{1,0:T(8,128)(2,1)S(1)}, u32[]{:S(2)}, u32[]{:S(2)}) collective-permute-start(bf16[128,128]{1,0:T(8,128)(2,1)S(1)} %get-tuple-element.29.refs_0_), channel_id=1, source_target_pairs={{0,3},{1,2},{2,1},{3,0},{4,7},{5,6},{6,5},{7,4},{8,11},{9,10},{10,... | collective-permute-start | bytes 98312 | tf_op jit(solution)/shard_map/ppermute | solution.py:220
  26.7 4.3 %collective-permute-start.3 = (bf16[2,128,128]{2,1,0:T(8,128)(2,1)S(1)}, bf16[2,128,128]{2,1,0:T(8,128)(2,1)S(1)}, u32[]{:S(2)}, u32[]{:S(2)}) collective-permute-start(bf16[2,128,128]{2,1,0:T(8,128)(2,1)S(1)} %pad_maximum_fusion.1), channel_id=1, source_target_pairs={{0,12},{4,0},{8,4},{12,8},{16,28},{20,16},{24,20},{28,24},{32,44},... | collective-permute-start | bytes 196616 | tf_op jit(solution)/shard_map/ppermute | solution.py:221
  26.8 6.2 %collective-permute-start.4 = (bf16[2,128,128]{2,1,0:T(8,128)(2,1)S(1)}, bf16[2,128,128]{2,1,0:T(8,128)(2,1)S(1)}, u32[]{:S(2)}, u32[]{:S(2)}) collective-permute-start(bf16[2,128,128]{2,1,0:T(8,128)(2,1)S(1)} %pad_maximum_fusion.1), channel_id=1, source_target_pairs={{0,8},{4,12},{8,0},{12,4},{16,24},{20,28},{24,16},{28,20},{32,40},... | collective-permute-start | bytes 196616 | tf_op jit(solution)/shard_map/ppermute | solution.py:221
  31.0 5.5 %collective-permute-start.5 = (bf16[2,128,128]{2,1,0:T(8,128)(2,1)S(1)}, bf16[2,128,128]{2,1,0:T(8,128)(2,1)S(1)}, u32[]{:S(2)}, u32[]{:S(2)}) collective-permute-start(bf16[2,128,128]{2,1,0:T(8,128)(2,1)S(1)} %pad_maximum_fusion.1), channel_id=1, source_target_pairs={{0,4},{4,8},{8,12},{12,0},{16,20},{20,24},{24,28},{28,16},{32,36},... | collective-permute-start | bytes 196616 | tf_op jit(solution)/shard_map/ppermute | solution.py:221
  36.6 9.6 %collective-permute-start.9 = (bf16[8,128,128]{2,1,0:T(8,128)(2,1)S(1)}, bf16[8,128,128]{2,1,0:T(8,128)(2,1)S(1)}, u32[]{:S(2)}, u32[]{:S(2)}) collective-permute-start(bf16[8,128,128]{2,1,0:T(8,128)(2,1)S(1)} %constant_dynamic-update-slice_fusion.refs_0_), channel_id=1, source_target_pairs={{0,32},{4,36},{8,40},{12,44},{16,48},{20,52},{24,56},{28,60},{32,6... | collective-permute-start | bytes 786440 | tf_op jit(solution)/shard_map/ppermute | solution.py:229
  41.0 9.0 %collective-permute-start.13 = (bf16[8,128,128]{2,1,0:T(8,128)(2,1)S(1)}, bf16[8,128,128]{2,1,0:T(8,128)(2,1)S(1)}, u32[]{:S(2)}, u32[]{:S(2)}) collective-permute-start(bf16[8,128,128]{2,1,0:T(8,128)(2,1)S(1)} %constant_dynamic-update-slice_fusion.refs_0_), channel_id=1, source_target_pairs={{0,224},{4,228},{8,232},{12,236},{16,240},{20,244},{24,248},{28,25... | collective-permute-start | bytes 786440 | tf_op jit(solution)/shard_map/ppermute | solution.py:230
  41.0 0.8 %copy-start = (bf16[256,128]{1,0:T(8,128)(2,1)S(1)}, bf16[256,128]{1,0:T(8,128)(2,1)}, u32[]{:S(2)}) copy-start(bf16[256,128]{1,0:T(8,128)(2,1)} %weight_ref.9) | copy-start | bytes 196612
  41.8 0.7 copy-start.4
  42.8 0.8 %copy-start.1 = (bf16[256,128]{1,0:T(8,128)(2,1)S(1)}, bf16[256,128]{1,0:T(8,128)(2,1)}, u32[]{:S(2)}) copy-start(bf16[256,128]{1,0:T(8,128)(2,1)} %weight_ref.9) | copy-start | bytes 196612
  43.6 0.7 copy-start.5
  46.2 9.8 %collective-permute-start.10 = (bf16[8,128,128]{2,1,0:T(8,128)(2,1)S(1)}, bf16[8,128,128]{2,1,0:T(8,128)(2,1)S(1)}, u32[]{:S(2)}, u32[]{:S(2)}) collective-permute-start(bf16[8,128,128]{2,1,0:T(8,128)(2,1)S(1)} %collective-permute-done.9.refs_0_), channel_id=1, source_target_pairs={{0,32},{4,36},{8,40},{12,44},{16,48},{20,52},{24,56},{28,60},{32,6... | collective-permute-start | bytes 786440 | tf_op jit(solution)/shard_map/ppermute | solution.py:229
  50.0 10.2 %collective-permute-start.14 = (bf16[8,128,128]{2,1,0:T(8,128)(2,1)S(1)}, bf16[8,128,128]{2,1,0:T(8,128)(2,1)S(1)}, u32[]{:S(2)}, u32[]{:S(2)}) collective-permute-start(bf16[8,128,128]{2,1,0:T(8,128)(2,1)S(1)} %collective-permute-done.13.refs_1_), channel_id=1, source_target_pairs={{0,224},{4,228},{8,232},{12,236},{16,240},{20,244},{24,248},{28,25... | collective-permute-start | bytes 786440 | tf_op jit(solution)/shard_map/ppermute | solution.py:230
  56.0 8.4 %collective-permute-start.11 = (bf16[8,128,128]{2,1,0:T(8,128)(2,1)S(1)}, bf16[8,128,128]{2,1,0:T(8,128)(2,1)S(1)}, u32[]{:S(2)}, u32[]{:S(2)}) collective-permute-start(bf16[8,128,128]{2,1,0:T(8,128)(2,1)S(1)} %collective-permute-done.10.refs_0_), channel_id=1, source_target_pairs={{0,32},{4,36},{8,40},{12,44},{16,48},{20,52},{24,56},{28,60},{32,6... | collective-permute-start | bytes 786440 | tf_op jit(solution)/shard_map/ppermute | solution.py:229
  60.2 8.2 %collective-permute-start.15 = (bf16[8,128,128]{2,1,0:T(8,128)(2,1)S(1)}, bf16[8,128,128]{2,1,0:T(8,128)(2,1)S(1)}, u32[]{:S(2)}, u32[]{:S(2)}) collective-permute-start(bf16[8,128,128]{2,1,0:T(8,128)(2,1)S(1)} %collective-permute-done.14.refs_1_), channel_id=1, source_target_pairs={{0,224},{4,228},{8,232},{12,236},{16,240},{20,244},{24,248},{28,25... | collective-permute-start | bytes 786440 | tf_op jit(solution)/shard_map/ppermute | solution.py:230
  64.3 7.6 %collective-permute-start.12 = (bf16[4,128,128]{2,1,0:T(8,128)(2,1)S(1)}, bf16[4,128,128]{2,1,0:T(8,128)(2,1)S(1)}, u32[]{:S(2)}, u32[]{:S(2)}) collective-permute-start(bf16[4,128,128]{2,1,0:T(8,128)(2,1)S(1)} %slice.17), channel_id=1, source_target_pairs={{0,32},{4,36},{8,40},{12,44},{16,48},{20,52},{24,56},{28,60},{32,6... | collective-permute-start | bytes 393224 | tf_op jit(solution)/shard_map/ppermute | solution.py:232
  68.4 6.3 %collective-permute-start.16 = (bf16[4,128,128]{2,1,0:T(8,128)(2,1)S(1)}, bf16[4,128,128]{2,1,0:T(8,128)(2,1)S(1)}, u32[]{:S(2)}, u32[]{:S(2)}) collective-permute-start(bf16[4,128,128]{2,1,0:T(8,128)(2,1)S(1)} %slice.18), channel_id=1, source_target_pairs={{0,224},{4,228},{8,232},{12,236},{16,240},{20,244},{24,248},{28,25... | collective-permute-start | bytes 393224 | tf_op jit(solution)/shard_map/ppermute | solution.py:233

commit v4 on v3

--- a/solution.py
+++ b/solution.py
@@ -35,33 +35,57 @@
     return jnp.where(mask, value, 0.0).astype(BF)
 
 
-def split_kernel(tile_ref, main_ref, left_ref):
+def stage_kernel(*refs):
+    count = len(refs) // 2
+    copies = [pltpu.make_async_copy(refs[n], refs[count + n], refs[-1].at[n]) for n in range(count)]
+    for copy in copies:
+        copy.start()
+    for copy in copies:
+        copy.wait()
+
+
+def stage(*params):
+    return pl.pallas_call(
+        stage_kernel,
+        in_specs=[ANYWHERE] * len(params),
+        out_shape=[jax.ShapeDtypeStruct(param.shape, param.dtype) for param in params],
+        scratch_shapes=[pltpu.SemaphoreType.DMA((len(params),))],
+        compiler_params=SMALL,
+        cost_estimate=pl.CostEstimate(flops=1_000_000_000, bytes_accessed=600_000, transcendentals=0),
+        name="stage",
+    )(*params)
+
+
+def split_kernel(tile_ref, main_ref, top_ref, left_ref, corner_ref):
     row, col = iotas(384, 384)
     tap = (row >= 96).astype(jnp.int32) + (row >= 192).astype(jnp.int32) + (row >= 288).astype(jnp.int32)
     order = one_hot(col == (row - 96 * tap) * 4 + tap)
     main = dot(order, jnp.concatenate([tile_ref[0], tile_ref[1]], axis=1)).astype(BF)
     row, col = iotas(256, 128)
     rim = one_hot(((row == 127) & (col == 0)) | ((row == 255) & (col == 64)))
+    left = dot(main, rim).astype(BF)
     main_ref[...] = main
-    left_ref[...] = dot(main, rim).astype(BF)
+    top_ref[...] = main[288:384]
+    left_ref[...] = left
+    corner_ref[...] = left[288:384]
 
 
 def split_tile(images):
     return pl.pallas_call(
         split_kernel,
-        out_shape=[jax.ShapeDtypeStruct((384, 256), BF), jax.ShapeDtypeStruct((384, 128), BF)],
+        out_shape=[jax.ShapeDtypeStruct(shape, BF) for shape in ((384, 256), (96, 256), (384, 128), (96, 128))],
         compiler_params=SMALL,
         name="split_tile",
     )(images.reshape(2, 384, 128))
 
 
-def hidden_kernel(main_ref, top_ref, left_ref, weight_ref, bias_ref, one_ref, two_ref):
-    rows = jnp.concatenate([top_ref[:, :256], main_ref[...]], axis=0)
+def hidden_kernel(main_ref, top_ref, left_ref, corner_ref, weight_ref, bias_ref, one_ref, two_ref):
+    rows = jnp.concatenate([top_ref[...], main_ref[...]], axis=0)
     row, col = iotas(256, 384)
     source = 2 * (col & 63) - 1 + (col >> 7) + jnp.where((col & 64) != 0, 128, 0)
     valid = ((col & 63) != 0) | (col >= 128)
     taps = dot(rows, one_hot((row == source) & valid))
-    rim = jnp.concatenate([top_ref[:, 256:], left_ref[...]], axis=0).astype(F32)
+    rim = jnp.concatenate([corner_ref[...], left_ref[...]], axis=0).astype(F32)
     first = (taps[:, :128] + rim).astype(BF)
     parts = [first, taps[:, 128:256].astype(BF), taps[:, 256:384].astype(BF)]
     stacked = jnp.concatenate(
@@ -81,13 +105,13 @@
     two_ref[...] = jnp.where(lane < 64, pltpu.roll(hidden[0], 64, 1), hidden[1]).astype(BF)
 
 
-def hidden_of(main, top, left, conv_weight, conv_bias):
+def hidden_of(main, top, left, corner, conv_weight, conv_bias):
     return pl.pallas_call(
         hidden_kernel,
         out_shape=[jax.ShapeDtypeStruct((128, 128), BF)] * 2,
         compiler_params=SMALL,
         name="hidden",
-    )(main, top, left, conv_weight.T, conv_bias[None, :])
+    )(main, top, left, corner, conv_weight, conv_bias)
 
 
 def feats_one_kernel(*refs):
@@ -97,7 +121,8 @@
         feats = lax.dot_general(
             hid_refs[m][...], weight_ref[...], (((0,), (1,)), ((), ())), preferred_element_type=F32
         )
-        feats = (feats + bias_ref[...]).astype(BF) * jnp.bfloat16(0.0625)
+        bias = jnp.concatenate([bias_ref[0:1, :], bias_ref[1:2, :]], axis=1)
+        feats = (feats + bias).astype(BF) * jnp.bfloat16(0.0625)
         for i in range(2):
             out_ref[pl.ds(pl.multiple_of(i * 256 + k * 64, 64), 64), :] = feats[i * 64 : (i + 1) * 64, :]
 
@@ -108,14 +133,17 @@
         out_shape=jax.ShapeDtypeStruct((512, 256), BF),
         compiler_params=SMALL,
         name="feats_one",
-    )(*hidden, proj_weight, proj_bias[None, :])
-
-
-def planes_kernel(offsets, last, n_alias, first_ref, weight_ref, bias_ref, *refs):
+    )(*hidden, proj_weight, proj_bias)
+
+
+def planes_kernel(offsets, merge, last, n_alias, first_ref, weight_ref, bias_ref, *refs):
     n_hid = 2 if last else len(offsets)
     hid_refs, rest = refs[:n_hid], refs[n_hid + n_alias :]
-    if last:
-        small_ref, zero_out, one_out, two_out, three_out, zero_buf, one_buf, two_buf, three_buf, hid_buf, sems = rest
+    if merge:
+        small_ref, zero_out, one_out, two_buf, three_buf, zero_buf, one_buf, sems = rest
+    elif last:
+        two_ref, three_ref, zero_out, one_out, two_out, three_out = rest[:6]
+        zero_buf, one_buf, two_buf, three_buf, hid_buf, sems = rest[6:]
     else:
         zero_out, one_out, small_out, zero_buf, one_buf, small_buf, sems = rest
     z, yh, x = position()
@@ -130,7 +158,7 @@
         [jnp.transpose(jnp.broadcast_to(bias_ref[n : n + 1, :], (128, 128))) for n in range(2)], axis=0
     )
     bias = jnp.concatenate([bias] * 4, axis=1)
-    copies = []
+    copies, places, smalls = [], [], []
 
     def send(source, target):
         copies.append(pltpu.make_async_copy(source, target, sems.at[len(copies)]))
@@ -159,37 +187,53 @@
         two = dot(one, pool2).astype(BF)
         three = dot(two, pool3).astype(BF)
         small = jnp.concatenate([two, three], axis=1)
-        if not last:
+        places.append(place)
+        smalls.append(small)
+        if not merge and not last:
             small_buf[n] = small
             send(small_buf.at[n], small_out.at[place])
-    if last:
+    if merge:
         for m in range(Z):
-            piece = jnp.where(place == m, small, small_ref[m])
+            piece = small_ref[m]
+            for place, small in zip(places, smalls):
+                piece = jnp.where(place == m, small, piece)
             two_buf[:, m * 64 : (m + 1) * 64] = piece[:, 0:64]
             three_buf[:, m * 16 : (m + 1) * 16] = piece[:, 64:80]
+    if last:
+        two_buf[...] = two_ref[...]
+        three_buf[...] = three_ref[...]
+        for m in range(Z):
+
+            @pl.when(places[0] == m)
+            def _():
+                two_buf[:, m * 64 : (m + 1) * 64] = smalls[0][:, 0:64]
+                three_buf[:, m * 16 : (m + 1) * 16] = smalls[0][:, 64:80]
+
         send(two_buf, two_out)
         send(three_buf, three_out)
     for copy in copies:
         copy.wait()
 
 
-def planes_call(offsets, hidden, first, proj_weight, proj_bias, outs, last=False):
+def planes_call(offsets, hidden, first, proj_weight, proj_bias, outs, merge=False, last=False):
     count = len(offsets)
-    args = [first, proj_weight, proj_bias.reshape(2, 128), *hidden]
+    args = [first, proj_weight, proj_bias, *hidden]
     in_specs = [VMEM] * len(args)
     aliases = {}
     if outs is not None:
-        shared = 2 if last else 3
+        shared = 2 if merge or last else 3
         aliases = {len(args) + n: n for n in range(shared)}
         args += list(outs)
-        in_specs += [ANYWHERE] * shared + [VMEM] * (3 - shared)
-    shapes = [(512, 8192), (512, 2048)] + ([(512, 512), (512, 128)] if last else [(8, 512, 128)])
+        in_specs += [ANYWHERE] * shared + [VMEM] * (len(outs) - shared)
+    small = [(512, 512), (512, 128)] if merge or last else [(8, 512, 128)]
+    shapes = [(512, 8192), (512, 2048)] + small
+    out_specs = [ANYWHERE] * 2 + [VMEM if merge else ANYWHERE] * len(small)
     scratch = [(2 * count, 512, 512), (count, 512, 256)]
-    scratch += [(512, 512), (512, 128), (8, 128, 128)] if last else [(count, 512, 128)]
-    return pl.pallas_call(
-        functools.partial(planes_kernel, offsets, last, len(aliases)),
+    scratch += [] if merge else small + [(8, 128, 128)] if last else [(count, 512, 128)]
+    return pl.pallas_call(
+        functools.partial(planes_kernel, offsets, merge, last, len(aliases)),
         in_specs=in_specs,
-        out_specs=[ANYWHERE] * len(shapes),
+        out_specs=out_specs,
         out_shape=[jax.ShapeDtypeStruct(shape, BF) for shape in shapes],
         scratch_shapes=[pltpu.VMEM(shape, BF) for shape in scratch] + [pltpu.SemaphoreType.DMA((5 * count,))],
         input_output_aliases=aliases,
@@ -204,10 +248,15 @@
 def per_device(images, conv_weight, conv_bias, proj_weight, proj_bias):
     right = [(c, c + 1) for c in range(COLS - 1)]
     down = [(r, r + 1) for r in range(ROWS - 1)]
-    main, left = split_tile(images)
+    diagonal = [(r * COLS + c, (r + 1) * COLS + c + 1) for r in range(ROWS - 1) for c in range(COLS - 1)]
+    main, top, left, corner = split_tile(images)
+    params = (conv_weight.T, conv_bias[None, :], proj_weight, proj_bias.reshape(2, 128))
+    main, top, left, corner, params = lax.optimization_barrier((main, top, left, corner, params))
     left = lax.ppermute(left, "cols", right)
-    top = lax.ppermute(jnp.concatenate([main[288:], left[288:]], axis=1), "rows", down)
-    hidden_one, hidden_two = hidden_of(main, top, left, conv_weight, conv_bias)
+    top = lax.ppermute(top, "rows", down)
+    corner = lax.ppermute(corner, ("rows", "cols"), diagonal)
+    conv_weight, conv_bias, proj_weight, proj_bias = stage(*params)
+    hidden_one, hidden_two = hidden_of(main, top, left, corner, conv_weight, conv_bias)
 
     def along(axis, steps):
         size, stride = {"z": (Z, PLANE), "yh": (YH, X), "x": (X, 1)}[axis]
@@ -215,11 +264,11 @@
         return [(r, target(r)) for r in range(ROWS)]
 
     other = lax.ppermute(hidden_two, "rows", along("yh", 1))
-    pair = jnp.stack([hidden_two, other])
     ones = [hidden_one]
     ones += [lax.ppermute(hidden_one, "cols", [(k, k ^ m) for k in range(COLS)]) for m in range(1, 4)]
+    other, ones = lax.optimization_barrier((other, ones))
+    pair = jnp.stack([hidden_two, other])
     mine = jnp.concatenate([pair] + [lax.ppermute(pair, "rows", along("x", -s)) for s in range(1, X)])
-    mine, ones = lax.optimization_barrier((mine, ones))
     first = feats_one(ones, proj_weight, proj_bias)
 
     call = functools.partial(planes_call, first=first, proj_weight=proj_weight, proj_bias=proj_bias)
@@ -228,7 +277,7 @@
     for step in range(1, Z // 2):
         below = lax.ppermute(below, "rows", along("z", 1))
         above = lax.ppermute(above, "rows", along("z", -1))
-        outs = call((-step, step), [below, above], outs=outs)
+        outs = call((-step, step), [below, above], outs=outs, merge=step == Z // 2 - 1)
     below = lax.ppermute(below[:4], "rows", along("z", 1))
     above = lax.ppermute(above[4:], "rows", along("z", -1))
     return tuple(call((Z // 2,), [below, above], outs=outs, last=True))

time: 78.4 us -> 71.5 us (0.912)
  the two profiles are of different devices: /device:TPU:104 before, /device:TPU:96 now
where the time goes in v4:
time: 71.5 us; the launch traced here: 70.6 us
  starting transfers between devices  34.6 us (48%)
  Pallas kernels  17.4 us (24%)
  waiting for transfers between devices  13.5 us (19%)
  local copies, waits for them, and re-layouts  4.09 us (6%)
  between operations  0.97 us (1%)
    pallas_call x5, Pallas kernels, planes_call(): pl.pallas_call(functools.partial(planes_kernel, offsets, merge, last, len...  15.6 us
    ppermute x3, starting transfers between devices, per_device(): below = lax.ppermute(below, 'rows', along('z', 1))  10.6 us
    ppermute x3, starting transfers between devices, per_device(): lax.ppermute(hidden_one, 'cols', [(k, k ^ m) for k in range(COLS)])  4.66 us
    ppermute x1, starting transfers between devices, per_device(): corner = lax.ppermute(corner, ('rows', 'cols'), diagonal)  4.58 us
    ppermute x3, waiting for transfers between devices, per_device(): lax.ppermute(pair, 'rows', along('x', -s))  4.42 us
    unnamed x14, local copies, waits for them, and re-layouts  4.06 us
    ppermute x3, starting transfers between devices, per_device(): lax.ppermute(pair, 'rows', along('x', -s))  3.8 us
    ppermute x1, starting transfers between devices, per_device(): below = lax.ppermute(below[:4], 'rows', along('z', 1))  3.77 us
  transfers between devices with their start and end apart: 18, of which 9 were waited for; matrix products, arithmetic and copies ran while one was open for 0% of the time, Pallas kernels for 20%

profile of v4, /device:TPU:96, one launch (start us, length us, event | category | flops | bytes accessed | tf_op | source)
XLA Modules:
  0.0 70.6 jit_solution(3876761184885991717)
XLA Ops:
  0.6 0.0 copy-start
  0.6 0.9 %copy-done = bf16[2,96,4,128]{3,2,1,0:T(4,128)(2,1)S(1)} copy-done((bf16[2,96,4,128]{3,2,1,0:T(4,128)(2,1)S(1)}, bf16[2,96,4,128]{3,2,1,0:T(4,128)(2,1)}, u32[]{:S(2)}) %copy-start) | copy-done | bytes 196632
  1.6 0.5 split_tile.1
  2.0 1.7 %collective-permute-start.1 = (bf16[384,128]{1,0:T(8,128)(2,1)S(1)}, bf16[384,128]{1,0:T(8,128)(2,1)S(1)}, u32[]{:S(2)}, u32[]{:S(2)}) collective-permute-start(bf16[384,128]{1,0:T(8,128)(2,1)S(1)} %get-tuple-element.46), channel_id=1, source_target_pairs={{0,1},{1,2},{2,3},{4,5},{5,6},{6,7},{8,9},{9,10},{10,11},{12,13},{... | collective-permute-start | bytes 294920 | tf_op jit(solution)/shard_map/ppermute | solution.py:255
  3.8 3.4 %collective-permute-start = (bf16[96,256]{1,0:T(8,128)(2,1)S(1)}, bf16[96,256]{1,0:T(8,128)(2,1)S(1)}, u32[]{:S(2)}, u32[]{:S(2)}) collective-permute-start(bf16[96,256]{1,0:T(8,128)(2,1)S(1)} %get-tuple-element.45), channel_id=1, source_target_pairs={{0,4},{4,8},{8,12},{12,16},{16,20},{20,24},{24,28},{28,32},{32,36}... | collective-permute-start | bytes 147464 | tf_op jit(solution)/shard_map/ppermute | solution.py:256
  7.2 4.6 %collective-permute-start.2 = (bf16[96,128]{1,0:T(8,128)(2,1)S(1)}, bf16[96,128]{1,0:T(8,128)(2,1)S(1)}, u32[]{:S(2)}, u32[]{:S(2)}) collective-permute-start(bf16[96,128]{1,0:T(8,128)(2,1)S(1)} %get-tuple-element.47), channel_id=1, source_target_pairs={{0,5},{1,6},{2,7},{4,9},{5,10},{6,11},{8,13},{9,14},{10,15},{12,17... | collective-permute-start | bytes 73736 | tf_op jit(solution)/shard_map/ppermute | solution.py:257
  11.8 0.0 copy-start.1
  11.8 0.9 %copy-done.1 = bf16[128,864]{0,1:T(8,128)(2,1)S(1)} copy-done((bf16[128,864]{0,1:T(8,128)(2,1)S(1)}, bf16[128,864]{0,1:T(8,128)(2,1)}, u32[]{:S(2)}) %copy-start.1) | copy-done | bytes 221208
  12.7 0.0 copy-start.2
  12.7 0.8 %copy-done.2 = bf16[256,128]{1,0:T(8,128)(2,1)S(1)} copy-done((bf16[256,128]{1,0:T(8,128)(2,1)S(1)}, bf16[256,128]{1,0:T(8,128)(2,1)}, u32[]{:S(2)}) %copy-start.2) | copy-done | bytes 65560
  13.6 0.0 copy-start.3
  13.6 0.7 copy-done.3
  14.3 0.0 copy-start.4
  14.3 0.7 copy-done.4
  14.9 0.4 stage.1
  15.3 0.0 collective-permute-done.2.corner_ref
  15.3 0.0 collective-permute-done.top_ref
  15.3 0.0 collective-permute-done.1.left_ref
  15.3 0.6 hidden.1
  16.0 3.2 %collective-permute-start.4 = (bf16[128,128]{1,0:T(8,128)(2,1)S(1)}, bf16[128,128]{1,0:T(8,128)(2,1)S(1)}, u32[]{:S(2)}, u32[]{:S(2)}) collective-permute-start(bf16[128,128]{1,0:T(8,128)(2,1)S(1)} %get-tuple-element.56.refs_0_), channel_id=1, source_target_pairs={{0,1},{1,0},{2,3},{3,2},{4,5},{5,4},{6,7},{7,6},{8,9},{9,8},{10,11... | collective-permute-start | bytes 98312 | tf_op jit(solution)/shard_map/ppermute | solution.py:268
  19.2 0.0 collective-permute-start.5
  19.2 1.4 %collective-permute-start.6 = (bf16[128,128]{1,0:T(8,128)(2,1)S(1)}, bf16[128,128]{1,0:T(8,128)(2,1)S(1)}, u32[]{:S(2)}, u32[]{:S(2)}) collective-permute-start(bf16[128,128]{1,0:T(8,128)(2,1)S(1)} %get-tuple-element.56.refs_0_), channel_id=1, source_target_pairs={{0,3},{1,2},{2,1},{3,0},{4,7},{5,6},{6,5},{7,4},{8,11},{9,10},{10,... | collective-permute-start | bytes 98312 | tf_op jit(solution)/shard_map/ppermute | solution.py:268
  20.6 2.0 %collective-permute-start.3 = (bf16[128,128]{1,0:T(8,128)(2,1)S(1)}, bf16[128,128]{1,0:T(8,128)(2,1)S(1)}, u32[]{:S(2)}, u32[]{:S(2)}) collective-permute-start(bf16[128,128]{1,0:T(8,128)(2,1)S(1)} %get-tuple-element.54), channel_id=1, source_target_pairs={{0,16},{4,20},{8,24},{12,28},{16,0},{20,4},{24,8},{28,12},{32,48},... | collective-permute-start | bytes 98312 | tf_op jit(solution)/shard_map/ppermute | solution.py:266
  22.6 3.5 %collective-permute-done.3 = bf16[128,128]{1,0:T(8,128)(2,1)S(1)} collective-permute-done((bf16[128,128]{1,0:T(8,128)(2,1)S(1)}, bf16[128,128]{1,0:T(8,128)(2,1)S(1)}, u32[]{:S(2)}, u32[]{:S(2)}) %collective-permute-start.3) | collective-permute-done | bytes 32800 | tf_op jit(solution)/shard_map/ppermute | solution.py:266
  26.1 0.0 collective-permute-done.4.refs_1_
  26.1 0.0 collective-permute-done.5.refs_2_
  26.1 0.0 collective-permute-done.6.refs_3_
  26.2 1.8 %collective-permute-start.7 = (bf16[2,128,128]{2,1,0:T(8,128)(2,1)S(1)}, bf16[2,128,128]{2,1,0:T(8,128)(2,1)S(1)}, u32[]{:S(2)}, u32[]{:S(2)}) collective-permute-start(bf16[2,128,128]{2,1,0:T(8,128)(2,1)S(1)} %pad_maximum_fusion), channel_id=1, source_target_pairs={{0,12},{4,0},{8,4},{12,8},{16,28},{20,16},{24,20},{28,24},{32,44},... | collective-permute-start | bytes 196616 | tf_op jit(solution)/shard_map/ppermute | solution.py:271
  27.9 0.7 collective-permute-start.8
  28.6 1.3 %collective-permute-start.9 = (bf16[2,128,128]{2,1,0:T(8,128)(2,1)S(1)}, bf16[2,128,128]{2,1,0:T(8,128)(2,1)S(1)}, u32[]{:S(2)}, u32[]{:S(2)}) collective-permute-start(bf16[2,128,128]{2,1,0:T(8,128)(2,1)S(1)} %pad_maximum_fusion), channel_id=1, source_target_pairs={{0,4},{4,8},{8,12},{12,0},{16,20},{20,24},{24,28},{28,16},{32,36},... | collective-permute-start | bytes 196616 | tf_op jit(solution)/shard_map/ppermute | solution.py:271
  30.0 0.7 %collective-permute-done.7 = bf16[2,128,128]{2,1,0:T(8,128)(2,1)S(1)} collective-permute-done((bf16[2,128,128]{2,1,0:T(8,128)(2,1)S(1)}, bf16[2,128,128]{2,1,0:T(8,128)(2,1)S(1)}, u32[]{:S(2)}, u32[]{:S(2)}) %collective-permute-start.7) | collective-permute-done | bytes 65568 | tf_op jit(solution)/shard_map/ppermute | solution.py:271
  30.7 3.0 %collective-permute-done.8 = bf16[2,128,128]{2,1,0:T(8,128)(2,1)S(1)} collective-permute-done((bf16[2,128,128]{2,1,0:T(8,128)(2,1)S(1)}, bf16[2,128,128]{2,1,0:T(8,128)(2,1)S(1)}, u32[]{:S(2)}, u32[]{:S(2)}) %collective-permute-start.8) | collective-permute-done | bytes 65568 | tf_op jit(solution)/shard_map/ppermute | solution.py:271
  33.8 0.7 collective-permute-done.9
  34.4 3.2 %collective-permute-start.10 = (bf16[8,128,128]{2,1,0:T(8,128)(2,1)S(1)}, bf16[8,128,128]{2,1,0:T(8,128)(2,1)S(1)}, u32[]{:S(2)}, u32[]{:S(2)}) collective-permute-start(bf16[8,128,128]{2,1,0:T(8,128)(2,1)S(1)} %constant_dynamic-update-slice_fusion.refs_0_), channel_id=1, source_target_pairs={{0,32},{4,36},{8,40},{12,44},{16,48},{20,52},{24,56},{28,60},{32,6... | collective-permute-start | bytes 786440 | tf_op jit(solution)/shard_map/ppermute | solution.py:278
  37.6 0.0 collective-permute-start.14
  37.6 0.3 feats_one.1.first_ref
  37.9 1.9 %planes.5 = (bf16[512,8192]{1,0:T(8,128)(2,1)}, bf16[512,2048]{1,0:T(8,128)(2,1)}, bf16[8,512,128]{2,1,0:T(8,128)(2,1)S(1)}) custom-call(bf16[512,256]{1,0:T(8,128)(2,1)S(1)} %feats_one.1.first_ref, bf16[256,128]{1,0:T(8,128)(2,1)S(1)} %get-tuple-element.60.refs_4_.weight_ref, f32[2,128]{1,0:T(2,128)S(1)} %get-tuple-element.61.refs_5_.bias_ref, ...), custom_call_target="tpu_custom_call" | custom-call | flops 1400000000 | bytes 1500000 | tf_op jit(solution)/shard_map/planes/pallas_call | solution.py:233
  39.8 2.7 %collective-permute-done.10.refs_0_ = bf16[8,128,128]{2,1,0:T(8,128)(2,1)S(1)} collective-permute-done((bf16[8,128,128]{2,1,0:T(8,128)(2,1)S(1)}, bf16[8,128,128]{2,1,0:T(8,128)(2,1)S(1)}, u32[]{:S(2)}, u32[]{:S(2)}) %collective-permute-start.10) | collective-permute-done | bytes 262176 | tf_op jit(solution)/shard_map/ppermute | solution.py:278
  42.4 3.7 %collective-permute-start.11 = (bf16[8,128,128]{2,1,0:T(8,128)(2,1)S(1)}, bf16[8,128,128]{2,1,0:T(8,128)(2,1)S(1)}, u32[]{:S(2)}, u32[]{:S(2)}) collective-permute-start(bf16[8,128,128]{2,1,0:T(8,128)(2,1)S(1)} %collective-permute-done.10.refs_0_), channel_id=1, source_target_pairs={{0,32},{4,36},{8,40},{12,44},{16,48},{20,52},{24,56},{28,60},{32,6... | collective-permute-start | bytes 786440 | tf_op jit(solution)/shard_map/ppermute | solution.py:278
  46.1 0.0 collective-permute-done.14.refs_1_
  46.1 0.0 collective-permute-start.15
  46.1 3.5 %planes.6 = (bf16[512,8192]{1,0:T(8,128)(2,1)}, bf16[512,2048]{1,0:T(8,128)(2,1)}, bf16[8,512,128]{2,1,0:T(8,128)(2,1)S(1)}) custom-call(bf16[512,256]{1,0:T(8,128)(2,1)S(1)} %feats_one.1.first_ref, bf16[256,128]{1,0:T(8,128)(2,1)S(1)} %get-tuple-element.60.refs_4_.weight_ref, ...), custom_call_target="tpu_custom_call", output_to_operand_aliasing={{0}: (5, {}), {1}: (6, {}), {2}: (7, {})} | custom-call | flops 2800000000 | bytes 3000000 | tf_op jit(solution)/shard_map/planes/pallas_call | solution.py:233
  49.6 0.4 collective-permute-done.11.refs_0_
  50.0 3.7 %collective-permute-start.12 = (bf16[8,128,128]{2,1,0:T(8,128)(2,1)S(1)}, bf16[8,128,128]{2,1,0:T(8,128)(2,1)S(1)}, u32[]{:S(2)}, u32[]{:S(2)}) collective-permute-start(bf16[8,128,128]{2,1,0:T(8,128)(2,1)S(1)} %collective-permute-done.11.refs_0_), channel_id=1, source_target_pairs={{0,32},{4,36},{8,40},{12,44},{16,48},{20,52},{24,56},{28,60},{32,6... | collective-permute-start | bytes 786440 | tf_op jit(solution)/shard_map/ppermute | solution.py:278
  53.7 0.0 collective-permute-done.15.refs_1_
  53.7 0.0 collective-permute-start.16
  53.7 3.5 %planes.7 = (bf16[512,8192]{1,0:T(8,128)(2,1)}, bf16[512,2048]{1,0:T(8,128)(2,1)}, bf16[8,512,128]{2,1,0:T(8,128)(2,1)S(1)}) custom-call(bf16[512,256]{1,0:T(8,128)(2,1)S(1)} %feats_one.1.first_ref, bf16[256,128]{1,0:T(8,128)(2,1)S(1)} %get-tuple-element.60.refs_4_.weight_ref, ...), custom_call_target="tpu_custom_call", output_to_operand_aliasing={{0}: (5, {}), {1}: (6, {}), {2}: (7, {})} | custom-call | flops 2800000000 | bytes 3000000 | tf_op jit(solution)/shard_map/planes/pallas_call | solution.py:233
  57.2 0.6 collective-permute-done.12.refs_0_
  57.8 3.8 %collective-permute-start.13 = (bf16[4,128,128]{2,1,0:T(8,128)(2,1)S(1)}, bf16[4,128,128]{2,1,0:T(8,128)(2,1)S(1)}, u32[]{:S(2)}, u32[]{:S(2)}) collective-permute-start(bf16[4,128,128]{2,1,0:T(8,128)(2,1)S(1)} %slice.8), channel_id=1, source_target_pairs={{0,32},{4,36},{8,40},{12,44},{16,48},{20,52},{24,56},{28,60},{32,6... | collective-permute-start | bytes 393224 | tf_op jit(solution)/shard_map/ppermute | solution.py:281
  61.6 0.1 collective-permute-done.16.refs_1_
  61.7 0.1 collective-permute-start.17
  61.8 4.3 %planes.8 = (bf16[512,8192]{1,0:T(8,128)(2,1)}, bf16[512,2048]{1,0:T(8,128)(2,1)}, bf16[512,512]{1,0:T(8,128)(2,1)S(1)}, bf16[512,128]{1,0:T(8,128)(2,1)S(1)}) custom-call(bf16[512,256]{1,0:T(8,128)(2,1)S(1)} %feats_one.1.first_ref, bf16[256,128]{1,0:T(8,128)(2,1)S(1)} %get-tuple-element.60.refs_4_.weight_ref, ...), custom_call_target="tpu_custom_call", output_to_operand_aliasing={{0}: (5, {}), {1}: (6, {})} | custom-call | flops 2800000000 | bytes 3000000 | tf_op jit(solution)/shard_map/planes/pallas_call | solution.py:233
  66.1 0.0 collective-permute-done.13.refs_0_
  66.1 1.8 %collective-permute-done.17.refs_1_ = bf16[4,128,128]{2,1,0:T(8,128)(2,1)S(1)} collective-permute-done((bf16[4,128,128]{2,1,0:T(8,128)(2,1)S(1)}, bf16[4,128,128]{2,1,0:T(8,128)(2,1)S(1)}, u32[]{:S(2)}, u32[]{:S(2)}) %collective-permute-start.17) | collective-permute-done | bytes 131104 | tf_op jit(solution)/shard_map/ppermute | solution.py:282
  68.0 2.5 %planes.9 = (bf16[512,8192]{1,0:T(8,128)(2,1)}, bf16[512,2048]{1,0:T(8,128)(2,1)}, bf16[512,512]{1,0:T(8,128)(2,1)}, bf16[512,128]{1,0:T(8,128)(2,1)}) custom-call(bf16[512,256]{1,0:T(8,128)(2,1)S(1)} %feats_one.1.first_ref, bf16[256,128]{1,0:T(8,128)(2,1)S(1)} %get-tuple-element.60.refs_4_.weight_ref, ...), custom_call_target="tpu_custom_call", output_to_operand_aliasing={{0}: (5, {}), {1}: (6, {})} | custom-call | flops 1400000000 | bytes 1500000 | tf_op jit(solution)/shard_map/planes/pallas_call | solution.py:233
  (8 shorter events, 0.1 us)
Async XLA Ops:
  0.6 0.9 %copy-start = (bf16[2,96,4,128]{3,2,1,0:T(4,128)(2,1)S(1)}, bf16[2,96,4,128]{3,2,1,0:T(4,128)(2,1)}, u32[]{:S(2)}) copy-start(bf16[2,96,4,128]{3,2,1,0:T(4,128)(2,1)} %param.5) | copy-start | bytes 589828
  2.0 13.3 %collective-permute-start.1 = (bf16[384,128]{1,0:T(8,128)(2,1)S(1)}, bf16[384,128]{1,0:T(8,128)(2,1)S(1)}, u32[]{:S(2)}, u32[]{:S(2)}) collective-permute-start(bf16[384,128]{1,0:T(8,128)(2,1)S(1)} %get-tuple-element.46), channel_id=1, source_target_pairs={{0,1},{1,2},{2,3},{4,5},{5,6},{6,7},{8,9},{9,10},{10,11},{12,13},{... | collective-permute-start | bytes 294920 | tf_op jit(solution)/shard_map/ppermute | solution.py:255
  3.8 11.5 %collective-permute-start = (bf16[96,256]{1,0:T(8,128)(2,1)S(1)}, bf16[96,256]{1,0:T(8,128)(2,1)S(1)}, u32[]{:S(2)}, u32[]{:S(2)}) collective-permute-start(bf16[96,256]{1,0:T(8,128)(2,1)S(1)} %get-tuple-element.45), channel_id=1, source_target_pairs={{0,4},{4,8},{8,12},{12,16},{16,20},{20,24},{24,28},{28,32},{32,36}... | collective-permute-start | bytes 147464 | tf_op jit(solution)/shard_map/ppermute | solution.py:256
  7.2 8.1 %collective-permute-start.2 = (bf16[96,128]{1,0:T(8,128)(2,1)S(1)}, bf16[96,128]{1,0:T(8,128)(2,1)S(1)}, u32[]{:S(2)}, u32[]{:S(2)}) collective-permute-start(bf16[96,128]{1,0:T(8,128)(2,1)S(1)} %get-tuple-element.47), channel_id=1, source_target_pairs={{0,5},{1,6},{2,7},{4,9},{5,10},{6,11},{8,13},{9,14},{10,15},{12,17... | collective-permute-start | bytes 73736 | tf_op jit(solution)/shard_map/ppermute | solution.py:257
  11.8 0.9 %copy-start.1 = (bf16[128,864]{0,1:T(8,128)(2,1)S(1)}, bf16[128,864]{0,1:T(8,128)(2,1)}, u32[]{:S(2)}) copy-start(bf16[128,864]{0,1:T(8,128)(2,1)} %param.6) | copy-start | bytes 663556
  12.7 0.8 %copy-start.2 = (bf16[256,128]{1,0:T(8,128)(2,1)S(1)}, bf16[256,128]{1,0:T(8,128)(2,1)}, u32[]{:S(2)}) copy-start(bf16[256,128]{1,0:T(8,128)(2,1)} %refs_2_) | copy-start | bytes 196612
  13.6 0.7 copy-start.3
  14.3 0.7 copy-start.4
  16.0 10.2 %collective-permute-start.4 = (bf16[128,128]{1,0:T(8,128)(2,1)S(1)}, bf16[128,128]{1,0:T(8,128)(2,1)S(1)}, u32[]{:S(2)}, u32[]{:S(2)}) collective-permute-start(bf16[128,128]{1,0:T(8,128)(2,1)S(1)} %get-tuple-element.56.refs_0_), channel_id=1, source_target_pairs={{0,1},{1,0},{2,3},{3,2},{4,5},{5,4},{6,7},{7,6},{8,9},{9,8},{10,11... | collective-permute-start | bytes 98312 | tf_op jit(solution)/shard_map/ppermute | solution.py:268
  19.2 6.9 %collective-permute-start.5 = (bf16[128,128]{1,0:T(8,128)(2,1)S(1)}, bf16[128,128]{1,0:T(8,128)(2,1)S(1)}, u32[]{:S(2)}, u32[]{:S(2)}) collective-permute-start(bf16[128,128]{1,0:T(8,128)(2,1)S(1)} %get-tuple-element.56.refs_0_), channel_id=1, source_target_pairs={{0,2},{1,3},{2,0},{3,1},{4,6},{5,7},{6,4},{7,5},{8,10},{9,11},{10,... | collective-permute-start | bytes 98312 | tf_op jit(solution)/shard_map/ppermute | solution.py:268
  19.2 6.9 %collective-permute-start.6 = (bf16[128,128]{1,0:T(8,128)(2,1)S(1)}, bf16[128,128]{1,0:T(8,128)(2,1)S(1)}, u32[]{:S(2)}, u32[]{:S(2)}) collective-permute-start(bf16[128,128]{1,0:T(8,128)(2,1)S(1)} %get-tuple-element.56.refs_0_), channel_id=1, source_target_pairs={{0,3},{1,2},{2,1},{3,0},{4,7},{5,6},{6,5},{7,4},{8,11},{9,10},{10,... | collective-permute-start | bytes 98312 | tf_op jit(solution)/shard_map/ppermute | solution.py:268
  20.6 5.5 %collective-permute-start.3 = (bf16[128,128]{1,0:T(8,128)(2,1)S(1)}, bf16[128,128]{1,0:T(8,128)(2,1)S(1)}, u32[]{:S(2)}, u32[]{:S(2)}) collective-permute-start(bf16[128,128]{1,0:T(8,128)(2,1)S(1)} %get-tuple-element.54), channel_id=1, source_target_pairs={{0,16},{4,20},{8,24},{12,28},{16,0},{20,4},{24,8},{28,12},{32,48},... | collective-permute-start | bytes 98312 | tf_op jit(solution)/shard_map/ppermute | solution.py:266
  26.2 4.5 %collective-permute-start.7 = (bf16[2,128,128]{2,1,0:T(8,128)(2,1)S(1)}, bf16[2,128,128]{2,1,0:T(8,128)(2,1)S(1)}, u32[]{:S(2)}, u32[]{:S(2)}) collective-permute-start(bf16[2,128,128]{2,1,0:T(8,128)(2,1)S(1)} %pad_maximum_fusion), channel_id=1, source_target_pairs={{0,12},{4,0},{8,4},{12,8},{16,28},{20,16},{24,20},{28,24},{32,44},... | collective-permute-start | bytes 196616 | tf_op jit(solution)/shard_map/ppermute | solution.py:271
  27.9 5.8 %collective-permute-start.8 = (bf16[2,128,128]{2,1,0:T(8,128)(2,1)S(1)}, bf16[2,128,128]{2,1,0:T(8,128)(2,1)S(1)}, u32[]{:S(2)}, u32[]{:S(2)}) collective-permute-start(bf16[2,128,128]{2,1,0:T(8,128)(2,1)S(1)} %pad_maximum_fusion), channel_id=1, source_target_pairs={{0,8},{4,12},{8,0},{12,4},{16,24},{20,28},{24,16},{28,20},{32,40},... | collective-permute-start | bytes 196616 | tf_op jit(solution)/shard_map/ppermute | solution.py:271
  28.6 5.8 %collective-permute-start.9 = (bf16[2,128,128]{2,1,0:T(8,128)(2,1)S(1)}, bf16[2,128,128]{2,1,0:T(8,128)(2,1)S(1)}, u32[]{:S(2)}, u32[]{:S(2)}) collective-permute-start(bf16[2,128,128]{2,1,0:T(8,128)(2,1)S(1)} %pad_maximum_fusion), channel_id=1, source_target_pairs={{0,4},{4,8},{8,12},{12,0},{16,20},{20,24},{24,28},{28,16},{32,36},... | collective-permute-start | bytes 196616 | tf_op jit(solution)/shard_map/ppermute | solution.py:271
  34.4 8.0 %collective-permute-start.10 = (bf16[8,128,128]{2,1,0:T(8,128)(2,1)S(1)}, bf16[8,128,128]{2,1,0:T(8,128)(2,1)S(1)}, u32[]{:S(2)}, u32[]{:S(2)}) collective-permute-start(bf16[8,128,128]{2,1,0:T(8,128)(2,1)S(1)} %constant_dynamic-update-slice_fusion.refs_0_), channel_id=1, source_target_pairs={{0,32},{4,36},{8,40},{12,44},{16,48},{20,52},{24,56},{28,60},{32,6... | collective-permute-start | bytes 786440 | tf_op jit(solution)/shard_map/ppermute | solution.py:278
  37.6 8.5 %collective-permute-start.14 = (bf16[8,128,128]{2,1,0:T(8,128)(2,1)S(1)}, bf16[8,128,128]{2,1,0:T(8,128)(2,1)S(1)}, u32[]{:S(2)}, u32[]{:S(2)}) collective-permute-start(bf16[8,128,128]{2,1,0:T(8,128)(2,1)S(1)} %constant_dynamic-update-slice_fusion.refs_0_), channel_id=1, source_target_pairs={{0,224},{4,228},{8,232},{12,236},{16,240},{20,244},{24,248},{28,25... | collective-permute-start | bytes 786440 | tf_op jit(solution)/shard_map/ppermute | solution.py:279
  42.4 7.6 %collective-permute-start.11 = (bf16[8,128,128]{2,1,0:T(8,128)(2,1)S(1)}, bf16[8,128,128]{2,1,0:T(8,128)(2,1)S(1)}, u32[]{:S(2)}, u32[]{:S(2)}) collective-permute-start(bf16[8,128,128]{2,1,0:T(8,128)(2,1)S(1)} %collective-permute-done.10.refs_0_), channel_id=1, source_target_pairs={{0,32},{4,36},{8,40},{12,44},{16,48},{20,52},{24,56},{28,60},{32,6... | collective-permute-start | bytes 786440 | tf_op jit(solution)/shard_map/ppermute | solution.py:278
  46.1 7.6 %collective-permute-start.15 = (bf16[8,128,128]{2,1,0:T(8,128)(2,1)S(1)}, bf16[8,128,128]{2,1,0:T(8,128)(2,1)S(1)}, u32[]{:S(2)}, u32[]{:S(2)}) collective-permute-start(bf16[8,128,128]{2,1,0:T(8,128)(2,1)S(1)} %collective-permute-done.14.refs_1_), channel_id=1, source_target_pairs={{0,224},{4,228},{8,232},{12,236},{16,240},{20,244},{24,248},{28,25... | collective-permute-start | bytes 786440 | tf_op jit(solution)/shard_map/ppermute | solution.py:279
  50.0 7.8 %collective-permute-start.12 = (bf16[8,128,128]{2,1,0:T(8,128)(2,1)S(1)}, bf16[8,128,128]{2,1,0:T(8,128)(2,1)S(1)}, u32[]{:S(2)}, u32[]{:S(2)}) collective-permute-start(bf16[8,128,128]{2,1,0:T(8,128)(2,1)S(1)} %collective-permute-done.11.refs_0_), channel_id=1, source_target_pairs={{0,32},{4,36},{8,40},{12,44},{16,48},{20,52},{24,56},{28,60},{32,6... | collective-permute-start | bytes 786440 | tf_op jit(solution)/shard_map/ppermute | solution.py:278
  53.7 7.9 %collective-permute-start.16 = (bf16[8,128,128]{2,1,0:T(8,128)(2,1)S(1)}, bf16[8,128,128]{2,1,0:T(8,128)(2,1)S(1)}, u32[]{:S(2)}, u32[]{:S(2)}) collective-permute-start(bf16[8,128,128]{2,1,0:T(8,128)(2,1)S(1)} %collective-permute-done.15.refs_1_), channel_id=1, source_target_pairs={{0,224},{4,228},{8,232},{12,236},{16,240},{20,244},{24,248},{28,25... | collective-permute-start | bytes 786440 | tf_op jit(solution)/shard_map/ppermute | solution.py:279
  57.8 8.3 %collective-permute-start.13 = (bf16[4,128,128]{2,1,0:T(8,128)(2,1)S(1)}, bf16[4,128,128]{2,1,0:T(8,128)(2,1)S(1)}, u32[]{:S(2)}, u32[]{:S(2)}) collective-permute-start(bf16[4,128,128]{2,1,0:T(8,128)(2,1)S(1)} %slice.8), channel_id=1, source_target_pairs={{0,32},{4,36},{8,40},{12,44},{16,48},{20,52},{24,56},{28,60},{32,6... | collective-permute-start | bytes 393224 | tf_op jit(solution)/shard_map/ppermute | solution.py:281
  61.7 6.3 %collective-permute-start.17 = (bf16[4,128,128]{2,1,0:T(8,128)(2,1)S(1)}, bf16[4,128,128]{2,1,0:T(8,128)(2,1)S(1)}, u32[]{:S(2)}, u32[]{:S(2)}) collective-permute-start(bf16[4,128,128]{2,1,0:T(8,128)(2,1)S(1)} %slice.9), channel_id=1, source_target_pairs={{0,224},{4,228},{8,232},{12,236},{16,240},{20,244},{24,248},{28,25... | collective-permute-start | bytes 393224 | tf_op jit(solution)/shard_map/ppermute | solution.py:282

commit v5 on v3

--- a/solution.py
+++ b/solution.py
@@ -17,6 +17,14 @@
     return jnp.dot(a, b, preferred_element_type=F32)
 
 
+def dot_nt(a, b):
+    return lax.dot_general(a, b, (((1,), (1,)), ((), ())), preferred_element_type=F32)
+
+
+def dot_tn(a, b):
+    return lax.dot_general(a, b, (((0,), (0,)), ((), ())), preferred_element_type=F32)
+
+
 def iotas(*shape):
     return lax.broadcasted_iota(jnp.int32, shape, 0), lax.broadcasted_iota(jnp.int32, shape, 1)
 
@@ -35,33 +43,53 @@
     return jnp.where(mask, value, 0.0).astype(BF)
 
 
-def split_kernel(tile_ref, main_ref, left_ref):
+def stage_kernel(*refs):
+    count = len(refs) // 2
+    for n in range(count):
+        refs[count + n][...] = refs[n][...]
+
+
+def stage(*params):
+    return pl.pallas_call(
+        stage_kernel,
+        out_shape=[jax.ShapeDtypeStruct(param.shape, param.dtype) for param in params],
+        compiler_params=SMALL,
+        cost_estimate=pl.CostEstimate(flops=1_000_000_000, bytes_accessed=600_000, transcendentals=0),
+        name="stage",
+    )(*params)
+
+
+def split_kernel(tile_ref, main_ref, top_ref, left_ref, corner_ref):
     row, col = iotas(384, 384)
     tap = (row >= 96).astype(jnp.int32) + (row >= 192).astype(jnp.int32) + (row >= 288).astype(jnp.int32)
     order = one_hot(col == (row - 96 * tap) * 4 + tap)
+    row, col = iotas(16, 256)
+    rim = one_hot((row < 2) & (col == row * 128 + 127))
     main = dot(order, jnp.concatenate([tile_ref[0], tile_ref[1]], axis=1)).astype(BF)
-    row, col = iotas(256, 128)
-    rim = one_hot(((row == 127) & (col == 0)) | ((row == 255) & (col == 64)))
     main_ref[...] = main
-    left_ref[...] = dot(main, rim).astype(BF)
+    top_ref[...] = main[288:384]
+    left_ref[...] = dot_nt(rim, main).astype(BF)
+    corner_ref[...] = dot_nt(rim, main[288:384]).astype(BF)
 
 
 def split_tile(images):
     return pl.pallas_call(
         split_kernel,
-        out_shape=[jax.ShapeDtypeStruct((384, 256), BF), jax.ShapeDtypeStruct((384, 128), BF)],
+        out_shape=[jax.ShapeDtypeStruct(shape, BF) for shape in ((384, 256), (96, 256), (16, 384), (16, 96))],
         compiler_params=SMALL,
         name="split_tile",
     )(images.reshape(2, 384, 128))
 
 
-def hidden_kernel(main_ref, top_ref, left_ref, weight_ref, bias_ref, one_ref, two_ref):
-    rows = jnp.concatenate([top_ref[:, :256], main_ref[...]], axis=0)
+def hidden_kernel(main_ref, top_ref, left_ref, corner_ref, weight_ref, bias_ref, one_ref, two_ref):
+    rows = jnp.concatenate([top_ref[...], main_ref[...]], axis=0)
     row, col = iotas(256, 384)
     source = 2 * (col & 63) - 1 + (col >> 7) + jnp.where((col & 64) != 0, 128, 0)
     valid = ((col & 63) != 0) | (col >= 128)
     taps = dot(rows, one_hot((row == source) & valid))
-    rim = jnp.concatenate([top_ref[:, 256:], left_ref[...]], axis=0).astype(F32)
+    row, col = iotas(16, 128)
+    place = one_hot((row < 2) & (col == row * 64))
+    rim = jnp.concatenate([dot_tn(corner_ref[...], place), dot_tn(left_ref[...], place)], axis=0)
     first = (taps[:, :128] + rim).astype(BF)
     parts = [first, taps[:, 128:256].astype(BF), taps[:, 256:384].astype(BF)]
     stacked = jnp.concatenate(
@@ -73,7 +101,7 @@
         ],
         axis=1,
     )
-    pre = lax.dot_general(weight_ref[...], stacked, (((0,), (0,)), ((), ())), preferred_element_type=F32)
+    pre = dot_tn(weight_ref[...], stacked)
     bias = jnp.transpose(jnp.broadcast_to(bias_ref[...], (128, 128)))
     hidden = [jnp.maximum(pre[:, i * 128 : (i + 1) * 128] + bias, 0.0) for i in range(2)]
     lane = lax.broadcasted_iota(jnp.int32, (128, 128), 1)
@@ -81,23 +109,24 @@
     two_ref[...] = jnp.where(lane < 64, pltpu.roll(hidden[0], 64, 1), hidden[1]).astype(BF)
 
 
-def hidden_of(main, top, left, conv_weight, conv_bias):
+def hidden_of(main, top, left, corner, conv_weight, conv_bias):
     return pl.pallas_call(
         hidden_kernel,
         out_shape=[jax.ShapeDtypeStruct((128, 128), BF)] * 2,
         compiler_params=SMALL,
         name="hidden",
-    )(main, top, left, conv_weight.T, conv_bias[None, :])
-
-
-def feats_one_kernel(*refs):
-    hid_refs, (weight_ref, bias_ref, out_ref) = refs[:4], refs[4:]
+    )(main, top, left, corner, conv_weight, conv_bias)
+
+
+def feats_one_kernel(own_ref, swapped_ref, far_ref, weight_ref, bias_ref, out_ref):
+    hidden = [own_ref[...], swapped_ref[...], far_ref[0], far_ref[1]]
     for m in range(4):
         k = lax.axis_index("cols") ^ m
         feats = lax.dot_general(
-            hid_refs[m][...], weight_ref[...], (((0,), (1,)), ((), ())), preferred_element_type=F32
+            hidden[m], weight_ref[...], (((0,), (1,)), ((), ())), preferred_element_type=F32
         )
-        feats = (feats + bias_ref[...]).astype(BF) * jnp.bfloat16(0.0625)
+        bias = jnp.concatenate([bias_ref[0:1, :], bias_ref[1:2, :]], axis=1)
+        feats = (feats + bias).astype(BF) * jnp.bfloat16(0.0625)
         for i in range(2):
             out_ref[pl.ds(pl.multiple_of(i * 256 + k * 64, 64), 64), :] = feats[i * 64 : (i + 1) * 64, :]
 
@@ -108,24 +137,21 @@
         out_shape=jax.ShapeDtypeStruct((512, 256), BF),
         compiler_params=SMALL,
         name="feats_one",
-    )(*hidden, proj_weight, proj_bias[None, :])
+    )(*hidden, proj_weight, proj_bias)
 
 
 def planes_kernel(offsets, last, n_alias, first_ref, weight_ref, bias_ref, *refs):
     n_hid = 2 if last else len(offsets)
     hid_refs, rest = refs[:n_hid], refs[n_hid + n_alias :]
     if last:
-        small_ref, zero_out, one_out, two_out, three_out, zero_buf, one_buf, two_buf, three_buf, hid_buf, sems = rest
+        small_ref, zero_out, one_out, two_out, three_out = rest[:5]
+        zero_buf, one_buf, two_buf, three_buf, hid_buf, sems = rest[5:]
     else:
         zero_out, one_out, small_out, zero_buf, one_buf, small_buf, sems = rest
     z, yh, x = position()
     order = [((j % X - x) & (X - 1)) * 2 + (yh ^ (j // X)) for j in range(PLANE)]
     row, col = iotas(512, 128)
     pool1 = one_hot(col == (row >> 7) * 32 + ((row & 63) >> 1), 0.25)
-    row, col = iotas(256, 64)
-    pool2 = one_hot(col == (row >> 6) * 16 + ((row & 31) >> 1), 0.25)
-    row, col = iotas(64, 64)
-    pool3 = one_hot(col == (row >> 5) * 8 + ((row & 15) >> 1), 0.25)
     bias = jnp.concatenate(
         [jnp.transpose(jnp.broadcast_to(bias_ref[n : n + 1, :], (128, 128))) for n in range(2)], axis=0
     )
@@ -156,18 +182,25 @@
         one = jnp.concatenate(ones, axis=1)
         one_buf[n] = one
         send(one_buf.at[n], one_out.at[:, pl.ds(pl.multiple_of(place * 256, 256), 256)])
-        two = dot(one, pool2).astype(BF)
-        three = dot(two, pool3).astype(BF)
-        small = jnp.concatenate([two, three], axis=1)
+        side = place & 1
+        row, col = iotas(256, 128)
+        two = dot(one, one_hot(col == side * 64 + (row >> 6) * 16 + ((row & 31) >> 1), 0.25)).astype(BF)
+        row, col = iotas(128, 128)
+        cell = ((row & 63) >> 5) * 8 + ((row & 15) >> 1)
+        three = dot(two, one_hot(((row >> 6) == side) & (col == place * 16 + cell), 0.25)).astype(BF)
         if not last:
-            small_buf[n] = small
+            small_buf[n, :, :128] = two
+            small_buf[n, :, 128:] = three
             send(small_buf.at[n], small_out.at[place])
     if last:
-        for m in range(Z):
-            piece = jnp.where(place == m, small, small_ref[m])
-            two_buf[:, m * 64 : (m + 1) * 64] = piece[:, 0:64]
-            three_buf[:, m * 16 : (m + 1) * 16] = piece[:, 64:80]
+        for m in range(Z // 2):
+            parts = [jnp.where(place == k, two, small_ref[k, :, :128]) for k in (2 * m, 2 * m + 1)]
+            two_buf[:, m * 128 : (m + 1) * 128] = parts[0] + parts[1]
         send(two_buf, two_out)
+        total = three
+        for k in range(Z):
+            total = total + jnp.where(place == k, jnp.zeros_like(three), small_ref[k, :, 128:])
+        three_buf[...] = total
         send(three_buf, three_out)
     for copy in copies:
         copy.wait()
@@ -175,17 +208,18 @@
 
 def planes_call(offsets, hidden, first, proj_weight, proj_bias, outs, last=False):
     count = len(offsets)
-    args = [first, proj_weight, proj_bias.reshape(2, 128), *hidden]
+    args = [first, proj_weight, proj_bias, *hidden]
     in_specs = [VMEM] * len(args)
     aliases = {}
     if outs is not None:
         shared = 2 if last else 3
         aliases = {len(args) + n: n for n in range(shared)}
         args += list(outs)
-        in_specs += [ANYWHERE] * shared + [VMEM] * (3 - shared)
-    shapes = [(512, 8192), (512, 2048)] + ([(512, 512), (512, 128)] if last else [(8, 512, 128)])
+        in_specs += [ANYWHERE] * shared + [VMEM] * (len(outs) - shared)
+    small = [(512, 512), (512, 128)] if last else [(Z, 512, 256)]
+    shapes = [(512, 8192), (512, 2048)] + small
     scratch = [(2 * count, 512, 512), (count, 512, 256)]
-    scratch += [(512, 512), (512, 128), (8, 128, 128)] if last else [(count, 512, 128)]
+    scratch += small + [(8, 128, 128)] if last else [(count, 512, 256)]
     return pl.pallas_call(
         functools.partial(planes_kernel, offsets, last, len(aliases)),
         in_specs=in_specs,
@@ -204,23 +238,32 @@
 def per_device(images, conv_weight, conv_bias, proj_weight, proj_bias):
     right = [(c, c + 1) for c in range(COLS - 1)]
     down = [(r, r + 1) for r in range(ROWS - 1)]
-    main, left = split_tile(images)
+    diagonal = [(r * COLS + c, (r + 1) * COLS + c + 1) for r in range(ROWS - 1) for c in range(COLS - 1)]
+    main, top, left, corner = split_tile(images)
+    params = (conv_weight.T, conv_bias[None, :])
+    main, top, left, corner, params = lax.optimization_barrier((main, top, left, corner, params))
+    top = lax.ppermute(top, "rows", down)
+    corner = lax.ppermute(corner, ("rows", "cols"), diagonal)
     left = lax.ppermute(left, "cols", right)
-    top = lax.ppermute(jnp.concatenate([main[288:], left[288:]], axis=1), "rows", down)
-    hidden_one, hidden_two = hidden_of(main, top, left, conv_weight, conv_bias)
+    conv_weight, conv_bias = stage(*params)
+    hidden_one, hidden_two = hidden_of(main, top, left, corner, conv_weight, conv_bias)
 
     def along(axis, steps):
         size, stride = {"z": (Z, PLANE), "yh": (YH, X), "x": (X, 1)}[axis]
         target = lambda r: r + ((r // stride + steps) % size - (r // stride) % size) * stride
         return [(r, target(r)) for r in range(ROWS)]
 
+    params = (proj_weight, proj_bias.reshape(2, 128))
+    hidden_one, hidden_two, params = lax.optimization_barrier((hidden_one, hidden_two, params))
     other = lax.ppermute(hidden_two, "rows", along("yh", 1))
+    proj_weight, proj_bias = stage(*params)
+    swapped = lax.ppermute(hidden_one, "cols", [(k, k ^ 1) for k in range(COLS)])
+    other, swapped, proj_weight, proj_bias = lax.optimization_barrier((other, swapped, proj_weight, proj_bias))
     pair = jnp.stack([hidden_two, other])
-    ones = [hidden_one]
-    ones += [lax.ppermute(hidden_one, "cols", [(k, k ^ m) for k in range(COLS)]) for m in range(1, 4)]
+    far = lax.ppermute(jnp.stack([hidden_one, swapped]), "cols", [(k, k ^ 2) for k in range(COLS)])
     mine = jnp.concatenate([pair] + [lax.ppermute(pair, "rows", along("x", -s)) for s in range(1, X)])
-    mine, ones = lax.optimization_barrier((mine, ones))
-    first = feats_one(ones, proj_weight, proj_bias)
+    mine, far = lax.optimization_barrier((mine, far))
+    first = feats_one((hidden_one, swapped, far), proj_weight, proj_bias)
 
     call = functools.partial(planes_call, first=first, proj_weight=proj_weight, proj_bias=proj_bias)
     below, above = mine, mine

time: 78.4 us -> 70.1 us (0.89)
  the two profiles are of different devices: /device:TPU:104 before, /device:TPU:96 now
where the time goes in v5:
time: 70.1 us; the launch traced here: 69.8 us
  starting transfers between devices  35.6 us (51%)
  Pallas kernels  15.4 us (22%)
  waiting for transfers between devices  15.3 us (22%)
  local copies, waits for them, and re-layouts  2.58 us (4%)
  between operations  0.97 us (1%)
    pallas_call x5, Pallas kernels, planes_call(): pl.pallas_call(functools.partial(planes_kernel, offsets, last, len(aliase...  13.9 us
    ppermute x3, starting transfers between devices, per_device(): below = lax.ppermute(below, 'rows', along('z', 1))  11 us
    ppermute x3, waiting for transfers between devices, per_device(): below = lax.ppermute(below, 'rows', along('z', 1))  6.61 us
    ppermute x1, starting transfers between devices, per_device(): corner = lax.ppermute(corner, ('rows', 'cols'), diagonal)  5.14 us
    ppermute x3, waiting for transfers between devices, per_device(): lax.ppermute(pair, 'rows', along('x', -s))  4.96 us
    ppermute x3, starting transfers between devices, per_device(): lax.ppermute(pair, 'rows', along('x', -s))  3.88 us
    ppermute x1, starting transfers between devices, per_device(): below = lax.ppermute(below[:4], 'rows', along('z', 1))  3.77 us
    ppermute x1, starting transfers between devices, per_device(): lax.ppermute(hidden_one, 'cols', [(k, k ^ 1) for k in range(COLS)])  3.62 us
  transfers between devices with their start and end apart: 17, of which 8 were waited for; matrix products, arithmetic and copies ran while one was open for 0% of the time, Pallas kernels for 17%

profile of v5, /device:TPU:96, one launch (start us, length us, event | category | flops | bytes accessed | tf_op | source)
XLA Modules:
  0.0 69.8 jit_solution(6661546552114303702)
XLA Ops:
  0.6 0.0 copy-start
  0.6 0.9 %copy-done = bf16[2,96,4,128]{3,2,1,0:T(4,128)(2,1)S(1)} copy-done((bf16[2,96,4,128]{3,2,1,0:T(4,128)(2,1)S(1)}, bf16[2,96,4,128]{3,2,1,0:T(4,128)(2,1)}, u32[]{:S(2)}) %copy-start) | copy-done | bytes 196632
  1.6 0.5 split_tile.1
  2.0 0.0 copy-start.3
  2.0 3.6 %collective-permute-start = (bf16[96,256]{1,0:T(8,128)(2,1)S(1)}, bf16[96,256]{1,0:T(8,128)(2,1)S(1)}, u32[]{:S(2)}, u32[]{:S(2)}) collective-permute-start(bf16[96,256]{1,0:T(8,128)(2,1)S(1)} %get-tuple-element.47), channel_id=1, source_target_pairs={{0,4},{4,8},{8,12},{12,16},{16,20},{20,24},{24,28},{28,32},{32,36}... | collective-permute-start | bytes 147464 | tf_op jit(solution)/shard_map/ppermute | solution.py:245
  5.6 1.5 %collective-permute-start.1 = (bf16[16,384]{1,0:T(8,128)(2,1)S(1)}, bf16[16,384]{1,0:T(8,128)(2,1)S(1)}, u32[]{:S(2)}, u32[]{:S(2)}) collective-permute-start(bf16[16,384]{1,0:T(8,128)(2,1)S(1)} %get-tuple-element.48), channel_id=1, source_target_pairs={{0,1},{1,2},{2,3},{4,5},{5,6},{6,7},{8,9},{9,10},{10,11},{12,13},{... | collective-permute-start | bytes 36872 | tf_op jit(solution)/shard_map/ppermute | solution.py:247
  7.1 5.1 %collective-permute-start.2 = (bf16[16,96]{1,0:T(8,128)(2,1)S(1)}, bf16[16,96]{1,0:T(8,128)(2,1)S(1)}, u32[]{:S(2)}, u32[]{:S(2)}) collective-permute-start(bf16[16,96]{1,0:T(8,128)(2,1)S(1)} %get-tuple-element.49), channel_id=1, source_target_pairs={{0,5},{1,6},{2,7},{4,9},{5,10},{6,11},{8,13},{9,14},{10,15},{12,17... | collective-permute-start | bytes 9224 | tf_op jit(solution)/shard_map/ppermute | solution.py:246
  12.2 0.0 copy-start.1
  12.2 0.9 %copy-done.1 = bf16[128,864]{0,1:T(8,128)(2,1)S(1)} copy-done((bf16[128,864]{0,1:T(8,128)(2,1)S(1)}, bf16[128,864]{0,1:T(8,128)(2,1)}, u32[]{:S(2)}) %copy-start.1) | copy-done | bytes 221208
  13.1 0.0 copy-start.4
  13.2 0.7 copy-done.4
  13.8 0.0 copy-start.2
  13.8 0.0 collective-permute-done.2.corner_ref
  13.8 0.0 collective-permute-done.1.left_ref
  13.8 0.0 collective-permute-done.top_ref
  13.9 0.8 %hidden.1 = (bf16[128,128]{1,0:T(8,128)(2,1)S(1)}, bf16[128,128]{1,0:T(8,128)(2,1)S(1)}) custom-call(bf16[384,256]{1,0:T(8,128)(2,1)S(1)} %get-tuple-element.46.main_ref, bf16[96,256]{1,0:T(8,128)(2,1)S(1)} %collective-permute-done.top_ref, bf16[16,384]{1,0:T(8,128)(2,1)S(1)} %collective-permute-done.1.left_ref, ...), custom_call_target="tpu_custom_call" | custom-call | tf_op jit(solution)/shard_map/hidden/pallas_call | solution.py:113
  14.6 3.0 %collective-permute-start.3 = (bf16[128,128]{1,0:T(8,128)(2,1)S(1)}, bf16[128,128]{1,0:T(8,128)(2,1)S(1)}, u32[]{:S(2)}, u32[]{:S(2)}) collective-permute-start(bf16[128,128]{1,0:T(8,128)(2,1)S(1)} %get-tuple-element.57), channel_id=1, source_target_pairs={{0,16},{4,20},{8,24},{12,28},{16,0},{20,4},{24,8},{28,12},{32,48},... | collective-permute-start | bytes 98312 | tf_op jit(solution)/shard_map/ppermute | solution.py:258
  17.6 3.6 %collective-permute-start.4 = (bf16[128,128]{1,0:T(8,128)(2,1)S(1)}, bf16[128,128]{1,0:T(8,128)(2,1)S(1)}, u32[]{:S(2)}, u32[]{:S(2)}) collective-permute-start(bf16[128,128]{1,0:T(8,128)(2,1)S(1)} %get-tuple-element.56.own_ref), channel_id=1, source_target_pairs={{0,1},{1,0},{2,3},{3,2},{4,5},{5,4},{6,7},{7,6},{8,9},{9,8},{10,11... | collective-permute-start | bytes 98312 | tf_op jit(solution)/shard_map/ppermute | solution.py:260
  21.2 0.0 copy-done.3
  21.2 0.0 copy-done.2
  21.2 0.0 collective-permute-done.3
  21.2 0.8 %collective-permute-done.4.swapped_ref = bf16[128,128]{1,0:T(8,128)(2,1)S(1)} collective-permute-done((bf16[128,128]{1,0:T(8,128)(2,1)S(1)}, bf16[128,128]{1,0:T(8,128)(2,1)S(1)}, u32[]{:S(2)}, u32[]{:S(2)}) %collective-permute-start.4) | collective-permute-done | bytes 32800 | tf_op jit(solution)/shard_map/ppermute | solution.py:260
  22.1 2.4 %collective-permute-start.5 = (bf16[2,128,128]{2,1,0:T(8,128)(2,1)S(1)}, bf16[2,128,128]{2,1,0:T(8,128)(2,1)S(1)}, u32[]{:S(2)}, u32[]{:S(2)}) collective-permute-start(bf16[2,128,128]{2,1,0:T(8,128)(2,1)S(1)} %pad_maximum_fusion), channel_id=1, source_target_pairs={{0,12},{4,0},{8,4},{12,8},{16,28},{20,16},{24,20},{28,24},{32,44},... | collective-permute-start | bytes 196616 | tf_op jit(solution)/shard_map/ppermute | solution.py:264
  24.5 0.1 collective-permute-start.6
  24.6 1.3 %collective-permute-start.7 = (bf16[2,128,128]{2,1,0:T(8,128)(2,1)S(1)}, bf16[2,128,128]{2,1,0:T(8,128)(2,1)S(1)}, u32[]{:S(2)}, u32[]{:S(2)}) collective-permute-start(bf16[2,128,128]{2,1,0:T(8,128)(2,1)S(1)} %pad_maximum_fusion), channel_id=1, source_target_pairs={{0,4},{4,8},{8,12},{12,0},{16,20},{20,24},{24,28},{28,16},{32,36},... | collective-permute-start | bytes 196616 | tf_op jit(solution)/shard_map/ppermute | solution.py:264
  26.0 0.1 collective-permute-start.8
  26.1 0.3 collective-permute-done.5
  26.4 4.2 %collective-permute-done.6 = bf16[2,128,128]{2,1,0:T(8,128)(2,1)S(1)} collective-permute-done((bf16[2,128,128]{2,1,0:T(8,128)(2,1)S(1)}, bf16[2,128,128]{2,1,0:T(8,128)(2,1)S(1)}, u32[]{:S(2)}, u32[]{:S(2)}) %collective-permute-start.6) | collective-permute-done | bytes 65568 | tf_op jit(solution)/shard_map/ppermute | solution.py:264
  30.6 0.5 collective-permute-done.7
  31.1 0.0 collective-permute-done.8.far_ref
  31.1 3.6 %collective-permute-start.9 = (bf16[8,128,128]{2,1,0:T(8,128)(2,1)S(1)}, bf16[8,128,128]{2,1,0:T(8,128)(2,1)S(1)}, u32[]{:S(2)}, u32[]{:S(2)}) collective-permute-start(bf16[8,128,128]{2,1,0:T(8,128)(2,1)S(1)} %constant_dynamic-update-slice_fusion.refs_0_), channel_id=1, source_target_pairs={{0,32},{4,36},{8,40},{12,44},{16,48},{20,52},{24,56},{28,60},{32,6... | collective-permute-start | bytes 786440 | tf_op jit(solution)/shard_map/ppermute | solution.py:272
  34.7 0.0 collective-permute-start.13
  34.7 0.3 feats_one.1.first_ref
  35.0 1.9 %planes.5 = (bf16[512,8192]{1,0:T(8,128)(2,1)}, bf16[512,2048]{1,0:T(8,128)(2,1)}, bf16[8,512,256]{2,1,0:T(8,128)(2,1)S(1)}) custom-call(bf16[512,256]{1,0:T(8,128)(2,1)S(1)} %feats_one.1.first_ref, bf16[256,128]{1,0:T(8,128)(2,1)S(1)} %get-tuple-element.65.weight_ref, f32[2,128]{1,0:T(2,128)S(1)} %get-tuple-element.66.bias_ref, ...), custom_call_target="tpu_custom_call" | custom-call | flops 1400000000 | bytes 1500000 | tf_op jit(solution)/shard_map/planes/pallas_call | solution.py:223
  36.9 3.8 %collective-permute-done.9.refs_0_ = bf16[8,128,128]{2,1,0:T(8,128)(2,1)S(1)} collective-permute-done((bf16[8,128,128]{2,1,0:T(8,128)(2,1)S(1)}, bf16[8,128,128]{2,1,0:T(8,128)(2,1)S(1)}, u32[]{:S(2)}, u32[]{:S(2)}) %collective-permute-start.9) | collective-permute-done | bytes 262176 | tf_op jit(solution)/shard_map/ppermute | solution.py:272
  40.7 3.7 %collective-permute-start.10 = (bf16[8,128,128]{2,1,0:T(8,128)(2,1)S(1)}, bf16[8,128,128]{2,1,0:T(8,128)(2,1)S(1)}, u32[]{:S(2)}, u32[]{:S(2)}) collective-permute-start(bf16[8,128,128]{2,1,0:T(8,128)(2,1)S(1)} %collective-permute-done.9.refs_0_), channel_id=1, source_target_pairs={{0,32},{4,36},{8,40},{12,44},{16,48},{20,52},{24,56},{28,60},{32,6... | collective-permute-start | bytes 786440 | tf_op jit(solution)/shard_map/ppermute | solution.py:272
  44.4 0.0 collective-permute-done.13.refs_1_
  44.4 0.0 collective-permute-start.14
  44.4 3.2 %planes.6 = (bf16[512,8192]{1,0:T(8,128)(2,1)}, bf16[512,2048]{1,0:T(8,128)(2,1)}, bf16[8,512,256]{2,1,0:T(8,128)(2,1)S(1)}) custom-call(bf16[512,256]{1,0:T(8,128)(2,1)S(1)} %feats_one.1.first_ref, bf16[256,128]{1,0:T(8,128)(2,1)S(1)} %get-tuple-element.65.weight_ref, ...), custom_call_target="tpu_custom_call", output_to_operand_aliasing={{0}: (5, {}), {1}: (6, {}), {2}: (7, {})} | custom-call | flops 2800000000 | bytes 3000000 | tf_op jit(solution)/shard_map/planes/pallas_call | solution.py:223
  47.6 1.9 %collective-permute-done.10.refs_0_ = bf16[8,128,128]{2,1,0:T(8,128)(2,1)S(1)} collective-permute-done((bf16[8,128,128]{2,1,0:T(8,128)(2,1)S(1)}, bf16[8,128,128]{2,1,0:T(8,128)(2,1)S(1)}, u32[]{:S(2)}, u32[]{:S(2)}) %collective-permute-start.10) | collective-permute-done | bytes 262176 | tf_op jit(solution)/shard_map/ppermute | solution.py:272
  49.5 3.7 %collective-permute-start.11 = (bf16[8,128,128]{2,1,0:T(8,128)(2,1)S(1)}, bf16[8,128,128]{2,1,0:T(8,128)(2,1)S(1)}, u32[]{:S(2)}, u32[]{:S(2)}) collective-permute-start(bf16[8,128,128]{2,1,0:T(8,128)(2,1)S(1)} %collective-permute-done.10.refs_0_), channel_id=1, source_target_pairs={{0,32},{4,36},{8,40},{12,44},{16,48},{20,52},{24,56},{28,60},{32,6... | collective-permute-start | bytes 786440 | tf_op jit(solution)/shard_map/ppermute | solution.py:272
  53.2 0.0 collective-permute-done.14.refs_1_
  53.2 0.0 collective-permute-start.15
  53.2 3.2 %planes.7 = (bf16[512,8192]{1,0:T(8,128)(2,1)}, bf16[512,2048]{1,0:T(8,128)(2,1)}, bf16[8,512,256]{2,1,0:T(8,128)(2,1)S(1)}) custom-call(bf16[512,256]{1,0:T(8,128)(2,1)S(1)} %feats_one.1.first_ref, bf16[256,128]{1,0:T(8,128)(2,1)S(1)} %get-tuple-element.65.weight_ref, ...), custom_call_target="tpu_custom_call", output_to_operand_aliasing={{0}: (5, {}), {1}: (6, {}), {2}: (7, {})} | custom-call | flops 2800000000 | bytes 3000000 | tf_op jit(solution)/shard_map/planes/pallas_call | solution.py:223
  56.4 0.9 %collective-permute-done.11.refs_0_ = bf16[8,128,128]{2,1,0:T(8,128)(2,1)S(1)} collective-permute-done((bf16[8,128,128]{2,1,0:T(8,128)(2,1)S(1)}, bf16[8,128,128]{2,1,0:T(8,128)(2,1)S(1)}, u32[]{:S(2)}, u32[]{:S(2)}) %collective-permute-start.11) | collective-permute-done | bytes 262176 | tf_op jit(solution)/shard_map/ppermute | solution.py:272
  57.4 3.8 %collective-permute-start.12 = (bf16[4,128,128]{2,1,0:T(8,128)(2,1)S(1)}, bf16[4,128,128]{2,1,0:T(8,128)(2,1)S(1)}, u32[]{:S(2)}, u32[]{:S(2)}) collective-permute-start(bf16[4,128,128]{2,1,0:T(8,128)(2,1)S(1)} %slice.8), channel_id=1, source_target_pairs={{0,32},{4,36},{8,40},{12,44},{16,48},{20,52},{24,56},{28,60},{32,6... | collective-permute-start | bytes 393224 | tf_op jit(solution)/shard_map/ppermute | solution.py:275
  61.2 0.0 collective-permute-done.15.refs_1_
  61.2 0.1 collective-permute-start.16
  61.3 3.3 %planes.8 = (bf16[512,8192]{1,0:T(8,128)(2,1)}, bf16[512,2048]{1,0:T(8,128)(2,1)}, bf16[8,512,256]{2,1,0:T(8,128)(2,1)S(1)}) custom-call(bf16[512,256]{1,0:T(8,128)(2,1)S(1)} %feats_one.1.first_ref, bf16[256,128]{1,0:T(8,128)(2,1)S(1)} %get-tuple-element.65.weight_ref, ...), custom_call_target="tpu_custom_call", output_to_operand_aliasing={{0}: (5, {}), {1}: (6, {}), {2}: (7, {})} | custom-call | flops 2800000000 | bytes 3000000 | tf_op jit(solution)/shard_map/planes/pallas_call | solution.py:223
  64.5 0.0 collective-permute-done.12.refs_0_
  64.6 2.9 %collective-permute-done.16.refs_1_ = bf16[4,128,128]{2,1,0:T(8,128)(2,1)S(1)} collective-permute-done((bf16[4,128,128]{2,1,0:T(8,128)(2,1)S(1)}, bf16[4,128,128]{2,1,0:T(8,128)(2,1)S(1)}, u32[]{:S(2)}, u32[]{:S(2)}) %collective-permute-start.16) | collective-permute-done | bytes 131104 | tf_op jit(solution)/shard_map/ppermute | solution.py:276
  67.4 2.2 %planes.9 = (bf16[512,8192]{1,0:T(8,128)(2,1)}, bf16[512,2048]{1,0:T(8,128)(2,1)}, bf16[512,512]{1,0:T(8,128)(2,1)}, bf16[512,128]{1,0:T(8,128)(2,1)}) custom-call(bf16[512,256]{1,0:T(8,128)(2,1)S(1)} %feats_one.1.first_ref, bf16[256,128]{1,0:T(8,128)(2,1)S(1)} %get-tuple-element.65.weight_ref, ...), custom_call_target="tpu_custom_call", output_to_operand_aliasing={{0}: (5, {}), {1}: (6, {})} | custom-call | flops 1400000000 | bytes 1500000 | tf_op jit(solution)/shard_map/planes/pallas_call | solution.py:223
  (11 shorter events, 0.1 us)
Async XLA Ops:
  0.6 0.9 %copy-start = (bf16[2,96,4,128]{3,2,1,0:T(4,128)(2,1)S(1)}, bf16[2,96,4,128]{3,2,1,0:T(4,128)(2,1)}, u32[]{:S(2)}) copy-start(bf16[2,96,4,128]{3,2,1,0:T(4,128)(2,1)} %param.5) | copy-start | bytes 589828
  2.0 19.2 %copy-start.3 = (f32[256]{0:T(256)S(1)}, f32[256]{0:T(256)}, u32[]{:S(2)}) copy-start(f32[256]{0:T(256)} %param.9) | copy-start | bytes 3076
  2.0 11.8 %collective-permute-start = (bf16[96,256]{1,0:T(8,128)(2,1)S(1)}, bf16[96,256]{1,0:T(8,128)(2,1)S(1)}, u32[]{:S(2)}, u32[]{:S(2)}) collective-permute-start(bf16[96,256]{1,0:T(8,128)(2,1)S(1)} %get-tuple-element.47), channel_id=1, source_target_pairs={{0,4},{4,8},{8,12},{12,16},{16,20},{20,24},{24,28},{28,32},{32,36}... | collective-permute-start | bytes 147464 | tf_op jit(solution)/shard_map/ppermute | solution.py:245
  5.6 8.2 %collective-permute-start.1 = (bf16[16,384]{1,0:T(8,128)(2,1)S(1)}, bf16[16,384]{1,0:T(8,128)(2,1)S(1)}, u32[]{:S(2)}, u32[]{:S(2)}) collective-permute-start(bf16[16,384]{1,0:T(8,128)(2,1)S(1)} %get-tuple-element.48), channel_id=1, source_target_pairs={{0,1},{1,2},{2,3},{4,5},{5,6},{6,7},{8,9},{9,10},{10,11},{12,13},{... | collective-permute-start | bytes 36872 | tf_op jit(solution)/shard_map/ppermute | solution.py:247
  7.1 6.8 %collective-permute-start.2 = (bf16[16,96]{1,0:T(8,128)(2,1)S(1)}, bf16[16,96]{1,0:T(8,128)(2,1)S(1)}, u32[]{:S(2)}, u32[]{:S(2)}) collective-permute-start(bf16[16,96]{1,0:T(8,128)(2,1)S(1)} %get-tuple-element.49), channel_id=1, source_target_pairs={{0,5},{1,6},{2,7},{4,9},{5,10},{6,11},{8,13},{9,14},{10,15},{12,17... | collective-permute-start | bytes 9224 | tf_op jit(solution)/shard_map/ppermute | solution.py:246
  12.2 0.9 %copy-start.1 = (bf16[128,864]{0,1:T(8,128)(2,1)S(1)}, bf16[128,864]{0,1:T(8,128)(2,1)}, u32[]{:S(2)}) copy-start(bf16[128,864]{0,1:T(8,128)(2,1)} %param.6) | copy-start | bytes 663556
  13.1 0.7 copy-start.4
  13.8 7.4 %copy-start.2 = (bf16[256,128]{1,0:T(8,128)(2,1)S(1)}, bf16[256,128]{1,0:T(8,128)(2,1)}, u32[]{:S(2)}) copy-start(bf16[256,128]{1,0:T(8,128)(2,1)} %refs_0_) | copy-start | bytes 196612
  14.6 6.6 %collective-permute-start.3 = (bf16[128,128]{1,0:T(8,128)(2,1)S(1)}, bf16[128,128]{1,0:T(8,128)(2,1)S(1)}, u32[]{:S(2)}, u32[]{:S(2)}) collective-permute-start(bf16[128,128]{1,0:T(8,128)(2,1)S(1)} %get-tuple-element.57), channel_id=1, source_target_pairs={{0,16},{4,20},{8,24},{12,28},{16,0},{20,4},{24,8},{28,12},{32,48},... | collective-permute-start | bytes 98312 | tf_op jit(solution)/shard_map/ppermute | solution.py:258
  17.6 4.5 %collective-permute-start.4 = (bf16[128,128]{1,0:T(8,128)(2,1)S(1)}, bf16[128,128]{1,0:T(8,128)(2,1)S(1)}, u32[]{:S(2)}, u32[]{:S(2)}) collective-permute-start(bf16[128,128]{1,0:T(8,128)(2,1)S(1)} %get-tuple-element.56.own_ref), channel_id=1, source_target_pairs={{0,1},{1,0},{2,3},{3,2},{4,5},{5,4},{6,7},{7,6},{8,9},{9,8},{10,11... | collective-permute-start | bytes 98312 | tf_op jit(solution)/shard_map/ppermute | solution.py:260
  22.1 4.3 %collective-permute-start.5 = (bf16[2,128,128]{2,1,0:T(8,128)(2,1)S(1)}, bf16[2,128,128]{2,1,0:T(8,128)(2,1)S(1)}, u32[]{:S(2)}, u32[]{:S(2)}) collective-permute-start(bf16[2,128,128]{2,1,0:T(8,128)(2,1)S(1)} %pad_maximum_fusion), channel_id=1, source_target_pairs={{0,12},{4,0},{8,4},{12,8},{16,28},{20,16},{24,20},{28,24},{32,44},... | collective-permute-start | bytes 196616 | tf_op jit(solution)/shard_map/ppermute | solution.py:264
  24.5 6.1 %collective-permute-start.6 = (bf16[2,128,128]{2,1,0:T(8,128)(2,1)S(1)}, bf16[2,128,128]{2,1,0:T(8,128)(2,1)S(1)}, u32[]{:S(2)}, u32[]{:S(2)}) collective-permute-start(bf16[2,128,128]{2,1,0:T(8,128)(2,1)S(1)} %pad_maximum_fusion), channel_id=1, source_target_pairs={{0,8},{4,12},{8,0},{12,4},{16,24},{20,28},{24,16},{28,20},{32,40},... | collective-permute-start | bytes 196616 | tf_op jit(solution)/shard_map/ppermute | solution.py:264
  24.6 6.5 %collective-permute-start.7 = (bf16[2,128,128]{2,1,0:T(8,128)(2,1)S(1)}, bf16[2,128,128]{2,1,0:T(8,128)(2,1)S(1)}, u32[]{:S(2)}, u32[]{:S(2)}) collective-permute-start(bf16[2,128,128]{2,1,0:T(8,128)(2,1)S(1)} %pad_maximum_fusion), channel_id=1, source_target_pairs={{0,4},{4,8},{8,12},{12,0},{16,20},{20,24},{24,28},{28,16},{32,36},... | collective-permute-start | bytes 196616 | tf_op jit(solution)/shard_map/ppermute | solution.py:264
  26.0 5.1 %collective-permute-start.8 = (bf16[2,128,128]{2,1,0:T(8,128)(2,1)S(1)}, bf16[2,128,128]{2,1,0:T(8,128)(2,1)S(1)}, u32[]{:S(2)}, u32[]{:S(2)}) collective-permute-start(bf16[2,128,128]{2,1,0:T(8,128)(2,1)S(1)} %pad_maximum_fusion.1), channel_id=1, source_target_pairs={{0,2},{1,3},{2,0},{3,1},{4,6},{5,7},{6,4},{7,5},{8,10},{9,11},{10,... | collective-permute-start | bytes 196616 | tf_op jit(solution)/shard_map/ppermute | solution.py:263
  31.1 9.5 %collective-permute-start.9 = (bf16[8,128,128]{2,1,0:T(8,128)(2,1)S(1)}, bf16[8,128,128]{2,1,0:T(8,128)(2,1)S(1)}, u32[]{:S(2)}, u32[]{:S(2)}) collective-permute-start(bf16[8,128,128]{2,1,0:T(8,128)(2,1)S(1)} %constant_dynamic-update-slice_fusion.refs_0_), channel_id=1, source_target_pairs={{0,32},{4,36},{8,40},{12,44},{16,48},{20,52},{24,56},{28,60},{32,6... | collective-permute-start | bytes 786440 | tf_op jit(solution)/shard_map/ppermute | solution.py:272
  34.7 9.6 %collective-permute-start.13 = (bf16[8,128,128]{2,1,0:T(8,128)(2,1)S(1)}, bf16[8,128,128]{2,1,0:T(8,128)(2,1)S(1)}, u32[]{:S(2)}, u32[]{:S(2)}) collective-permute-start(bf16[8,128,128]{2,1,0:T(8,128)(2,1)S(1)} %constant_dynamic-update-slice_fusion.refs_0_), channel_id=1, source_target_pairs={{0,224},{4,228},{8,232},{12,236},{16,240},{20,244},{24,248},{28,25... | collective-permute-start | bytes 786440 | tf_op jit(solution)/shard_map/ppermute | solution.py:273
  40.7 8.8 %collective-permute-start.10 = (bf16[8,128,128]{2,1,0:T(8,128)(2,1)S(1)}, bf16[8,128,128]{2,1,0:T(8,128)(2,1)S(1)}, u32[]{:S(2)}, u32[]{:S(2)}) collective-permute-start(bf16[8,128,128]{2,1,0:T(8,128)(2,1)S(1)} %collective-permute-done.9.refs_0_), channel_id=1, source_target_pairs={{0,32},{4,36},{8,40},{12,44},{16,48},{20,52},{24,56},{28,60},{32,6... | collective-permute-start | bytes 786440 | tf_op jit(solution)/shard_map/ppermute | solution.py:272
  44.4 8.8 %collective-permute-start.14 = (bf16[8,128,128]{2,1,0:T(8,128)(2,1)S(1)}, bf16[8,128,128]{2,1,0:T(8,128)(2,1)S(1)}, u32[]{:S(2)}, u32[]{:S(2)}) collective-permute-start(bf16[8,128,128]{2,1,0:T(8,128)(2,1)S(1)} %collective-permute-done.13.refs_1_), channel_id=1, source_target_pairs={{0,224},{4,228},{8,232},{12,236},{16,240},{20,244},{24,248},{28,25... | collective-permute-start | bytes 786440 | tf_op jit(solution)/shard_map/ppermute | solution.py:273
  49.5 7.9 %collective-permute-start.11 = (bf16[8,128,128]{2,1,0:T(8,128)(2,1)S(1)}, bf16[8,128,128]{2,1,0:T(8,128)(2,1)S(1)}, u32[]{:S(2)}, u32[]{:S(2)}) collective-permute-start(bf16[8,128,128]{2,1,0:T(8,128)(2,1)S(1)} %collective-permute-done.10.refs_0_), channel_id=1, source_target_pairs={{0,32},{4,36},{8,40},{12,44},{16,48},{20,52},{24,56},{28,60},{32,6... | collective-permute-start | bytes 786440 | tf_op jit(solution)/shard_map/ppermute | solution.py:272
  53.2 8.0 %collective-permute-start.15 = (bf16[8,128,128]{2,1,0:T(8,128)(2,1)S(1)}, bf16[8,128,128]{2,1,0:T(8,128)(2,1)S(1)}, u32[]{:S(2)}, u32[]{:S(2)}) collective-permute-start(bf16[8,128,128]{2,1,0:T(8,128)(2,1)S(1)} %collective-permute-done.14.refs_1_), channel_id=1, source_target_pairs={{0,224},{4,228},{8,232},{12,236},{16,240},{20,244},{24,248},{28,25... | collective-permute-start | bytes 786440 | tf_op jit(solution)/shard_map/ppermute | solution.py:273
  57.4 7.1 %collective-permute-start.12 = (bf16[4,128,128]{2,1,0:T(8,128)(2,1)S(1)}, bf16[4,128,128]{2,1,0:T(8,128)(2,1)S(1)}, u32[]{:S(2)}, u32[]{:S(2)}) collective-permute-start(bf16[4,128,128]{2,1,0:T(8,128)(2,1)S(1)} %slice.8), channel_id=1, source_target_pairs={{0,32},{4,36},{8,40},{12,44},{16,48},{20,52},{24,56},{28,60},{32,6... | collective-permute-start | bytes 393224 | tf_op jit(solution)/shard_map/ppermute | solution.py:275
  61.2 6.3 %collective-permute-start.16 = (bf16[4,128,128]{2,1,0:T(8,128)(2,1)S(1)}, bf16[4,128,128]{2,1,0:T(8,128)(2,1)S(1)}, u32[]{:S(2)}, u32[]{:S(2)}) collective-permute-start(bf16[4,128,128]{2,1,0:T(8,128)(2,1)S(1)} %slice.9), channel_id=1, source_target_pairs={{0,224},{4,228},{8,232},{12,236},{16,240},{20,244},{24,248},{28,25... | collective-permute-start | bytes 393224 | tf_op jit(solution)/shard_map/ppermute | solution.py:276

commit v6 on v5

--- a/solution.py
+++ b/solution.py
@@ -59,7 +59,7 @@
     )(*params)
 
 
-def split_kernel(tile_ref, main_ref, top_ref, left_ref, corner_ref):
+def split_kernel(tile_ref, main_ref, top_ref, left_ref):
     row, col = iotas(384, 384)
     tap = (row >= 96).astype(jnp.int32) + (row >= 192).astype(jnp.int32) + (row >= 288).astype(jnp.int32)
     order = one_hot(col == (row - 96 * tap) * 4 + tap)
@@ -69,13 +69,12 @@
     main_ref[...] = main
     top_ref[...] = main[288:384]
     left_ref[...] = dot_nt(rim, main).astype(BF)
-    corner_ref[...] = dot_nt(rim, main[288:384]).astype(BF)
 
 
 def split_tile(images):
     return pl.pallas_call(
         split_kernel,
-        out_shape=[jax.ShapeDtypeStruct(shape, BF) for shape in ((384, 256), (96, 256), (16, 384), (16, 96))],
+        out_shape=[jax.ShapeDtypeStruct(shape, BF) for shape in ((384, 256), (96, 256), (16, 384))],
         compiler_params=SMALL,
         name="split_tile",
     )(images.reshape(2, 384, 128))
@@ -89,7 +88,9 @@
     taps = dot(rows, one_hot((row == source) & valid))
     row, col = iotas(16, 128)
     place = one_hot((row < 2) & (col == row * 64))
-    rim = jnp.concatenate([dot_tn(corner_ref[...], place), dot_tn(left_ref[...], place)], axis=0)
+    row, col = iotas(256, 128)
+    last = one_hot(((row & 127) == 127) & (col == (row >> 7) * 64))
+    rim = jnp.concatenate([dot(corner_ref[...], last), dot_tn(left_ref[...], place)], axis=0)
     first = (taps[:, :128] + rim).astype(BF)
     parts = [first, taps[:, 128:256].astype(BF), taps[:, 256:384].astype(BF)]
     stacked = jnp.concatenate(
@@ -239,11 +240,11 @@
     right = [(c, c + 1) for c in range(COLS - 1)]
     down = [(r, r + 1) for r in range(ROWS - 1)]
     diagonal = [(r * COLS + c, (r + 1) * COLS + c + 1) for r in range(ROWS - 1) for c in range(COLS - 1)]
-    main, top, left, corner = split_tile(images)
+    main, top, left = split_tile(images)
     params = (conv_weight.T, conv_bias[None, :])
-    main, top, left, corner, params = lax.optimization_barrier((main, top, left, corner, params))
+    main, top, left, params = lax.optimization_barrier((main, top, left, params))
+    corner = lax.ppermute(top, ("rows", "cols"), diagonal)
     top = lax.ppermute(top, "rows", down)
-    corner = lax.ppermute(corner, ("rows", "cols"), diagonal)
     left = lax.ppermute(left, "cols", right)
     conv_weight, conv_bias = stage(*params)
     hidden_one, hidden_two = hidden_of(main, top, left, corner, conv_weight, conv_bias)

time: 70.1 us -> 68.1 us (0.971); the launches traced: 69.8 us -> 66.8 us
  starting transfers between devices: 35.6 us -> 34 us
  waiting for transfers between devices: 15.3 us -> 13.9 us
    ppermute x1, starting transfers between devices: 3.62 us -> 0.94 us  [per_device(): lax.ppermute(hidden_one, 'cols', [(k, k ^ 1) for k in range(COLS)])]
    ppermute x1, starting transfers between devices: 5.14 us -> 2.56 us  [per_device(): corner = lax.ppermute(top, ('rows', 'cols'), diagonal)]
    ppermute x1, starting transfers between devices: 1.46 us -> 3.87 us  [per_device(): left = lax.ppermute(left, 'cols', right)]
    ppermute x3, starting transfers between devices: 3.88 us -> 5.83 us  [per_device(): lax.ppermute(pair, 'rows', along('x', -s))]
    ppermute x1, waiting for transfers between devices: 0.01 us -> 1.56 us  [per_device(): other = lax.ppermute(hidden_two, 'rows', along('yh', 1))]
    ppermute x3, waiting for transfers between devices: 4.96 us -> 3.42 us  [per_device(): lax.ppermute(pair, 'rows', along('x', -s))]
    ppermute x3, starting transfers between devices: 11 us -> 9.59 us  [per_device(): below = lax.ppermute(below, 'rows', along('z', 1))]
    ppermute x3, waiting for transfers between devices: 6.61 us -> 5.6 us  [per_device(): below = lax.ppermute(below, 'rows', along('z', 1))]
  transfers between devices with their start and end apart: 17 -> 17, of which waited for: 8 -> 9; matrix products, arithmetic and copies ran while one was open for 0% -> 0% of each run, Pallas kernels for 17% -> 18%
where the time goes in v6:
time: 68.1 us; the launch traced here: 66.8 us
  starting transfers between devices  34 us (50%)
  Pallas kernels  15.3 us (22%)
  waiting for transfers between devices  13.9 us (20%)
  local copies, waits for them, and re-layouts  2.58 us (4%)
  between operations  0.96 us (1%)
    pallas_call x5, Pallas kernels, planes_call(): pl.pallas_call(functools.partial(planes_kernel, offsets, last, len(aliase...  13.8 us
    ppermute x3, starting transfers between devices, per_device(): below = lax.ppermute(below, 'rows', along('z', 1))  9.59 us
    ppermute x3, starting transfers between devices, per_device(): lax.ppermute(pair, 'rows', along('x', -s))  5.83 us
    ppermute x3, waiting for transfers between devices, per_device(): below = lax.ppermute(below, 'rows', along('z', 1))  5.6 us
    ppermute x1, starting transfers between devices, per_device(): left = lax.ppermute(left, 'cols', right)  3.87 us
    ppermute x1, starting transfers between devices, per_device(): below = lax.ppermute(below[:4], 'rows', along('z', 1))  3.77 us
    ppermute x1, starting transfers between devices, per_device(): top = lax.ppermute(top, 'rows', down)  3.56 us
    ppermute x3, waiting for transfers between devices, per_device(): lax.ppermute(pair, 'rows', along('x', -s))  3.42 us
  transfers between devices with their start and end apart: 17, of which 9 were waited for; matrix products, arithmetic and copies ran while one was open for 0% of the time, Pallas kernels for 18%

profile of v6, /device:TPU:96, one launch (start us, length us, event | category | flops | bytes accessed | tf_op | source)
XLA Modules:
  0.0 66.8 jit_solution(6150241581894154280)
XLA Ops:
  0.6 0.0 copy-start
  0.6 0.9 %copy-done = bf16[2,96,4,128]{3,2,1,0:T(4,128)(2,1)S(1)} copy-done((bf16[2,96,4,128]{3,2,1,0:T(4,128)(2,1)S(1)}, bf16[2,96,4,128]{3,2,1,0:T(4,128)(2,1)}, u32[]{:S(2)}) %copy-start) | copy-done | bytes 196632
  1.6 0.4 split_tile.1
  2.0 0.0 copy-start.3
  2.0 3.6 %collective-permute-start = (bf16[96,256]{1,0:T(8,128)(2,1)S(1)}, bf16[96,256]{1,0:T(8,128)(2,1)S(1)}, u32[]{:S(2)}, u32[]{:S(2)}) collective-permute-start(bf16[96,256]{1,0:T(8,128)(2,1)S(1)} %get-tuple-element.44), channel_id=1, source_target_pairs={{0,4},{4,8},{8,12},{12,16},{16,20},{20,24},{24,28},{28,32},{32,36}... | collective-permute-start | bytes 147464 | tf_op jit(solution)/shard_map/ppermute | solution.py:247
  5.6 2.6 %collective-permute-start.2 = (bf16[96,256]{1,0:T(8,128)(2,1)S(1)}, bf16[96,256]{1,0:T(8,128)(2,1)S(1)}, u32[]{:S(2)}, u32[]{:S(2)}) collective-permute-start(bf16[96,256]{1,0:T(8,128)(2,1)S(1)} %get-tuple-element.44), channel_id=1, source_target_pairs={{0,5},{1,6},{2,7},{4,9},{5,10},{6,11},{8,13},{9,14},{10,15},{12,17... | collective-permute-start | bytes 147464 | tf_op jit(solution)/shard_map/ppermute | solution.py:246
  8.1 3.9 %collective-permute-start.1 = (bf16[16,384]{1,0:T(8,128)(2,1)S(1)}, bf16[16,384]{1,0:T(8,128)(2,1)S(1)}, u32[]{:S(2)}, u32[]{:S(2)}) collective-permute-start(bf16[16,384]{1,0:T(8,128)(2,1)S(1)} %get-tuple-element.45), channel_id=1, source_target_pairs={{0,1},{1,2},{2,3},{4,5},{5,6},{6,7},{8,9},{9,10},{10,11},{12,13},{... | collective-permute-start | bytes 36872 | tf_op jit(solution)/shard_map/ppermute | solution.py:248
  12.0 0.0 copy-start.1
  12.0 0.9 %copy-done.1 = bf16[128,864]{0,1:T(8,128)(2,1)S(1)} copy-done((bf16[128,864]{0,1:T(8,128)(2,1)S(1)}, bf16[128,864]{0,1:T(8,128)(2,1)}, u32[]{:S(2)}) %copy-start.1) | copy-done | bytes 221208
  13.0 0.0 copy-start.4
  13.0 0.7 copy-done.4
  13.6 0.0 copy-start.2
  13.6 0.0 collective-permute-done.1.left_ref
  13.6 0.0 collective-permute-done.top_ref
  13.7 0.0 collective-permute-done.2.corner_ref
  13.7 0.7 %hidden.1 = (bf16[128,128]{1,0:T(8,128)(2,1)S(1)}, bf16[128,128]{1,0:T(8,128)(2,1)S(1)}) custom-call(bf16[384,256]{1,0:T(8,128)(2,1)S(1)} %get-tuple-element.43.main_ref, bf16[96,256]{1,0:T(8,128)(2,1)S(1)} %collective-permute-done.top_ref, bf16[16,384]{1,0:T(8,128)(2,1)S(1)} %collective-permute-done.1.left_ref, ...), custom_call_target="tpu_custom_call" | custom-call | tf_op jit(solution)/shard_map/hidden/pallas_call | solution.py:114
  14.4 3.0 %collective-permute-start.3 = (bf16[128,128]{1,0:T(8,128)(2,1)S(1)}, bf16[128,128]{1,0:T(8,128)(2,1)S(1)}, u32[]{:S(2)}, u32[]{:S(2)}) collective-permute-start(bf16[128,128]{1,0:T(8,128)(2,1)S(1)} %get-tuple-element.53), channel_id=1, source_target_pairs={{0,16},{4,20},{8,24},{12,28},{16,0},{20,4},{24,8},{28,12},{32,48},... | collective-permute-start | bytes 98312 | tf_op jit(solution)/shard_map/ppermute | solution.py:259
  17.4 0.9 %collective-permute-start.4 = (bf16[128,128]{1,0:T(8,128)(2,1)S(1)}, bf16[128,128]{1,0:T(8,128)(2,1)S(1)}, u32[]{:S(2)}, u32[]{:S(2)}) collective-permute-start(bf16[128,128]{1,0:T(8,128)(2,1)S(1)} %get-tuple-element.52.own_ref), channel_id=1, source_target_pairs={{0,1},{1,0},{2,3},{3,2},{4,5},{5,4},{6,7},{7,6},{8,9},{9,8},{10,11... | collective-permute-start | bytes 98312 | tf_op jit(solution)/shard_map/ppermute | solution.py:261
  18.4 0.0 copy-done.3
  18.4 0.0 copy-done.2
  18.4 1.6 %collective-permute-done.3 = bf16[128,128]{1,0:T(8,128)(2,1)S(1)} collective-permute-done((bf16[128,128]{1,0:T(8,128)(2,1)S(1)}, bf16[128,128]{1,0:T(8,128)(2,1)S(1)}, u32[]{:S(2)}, u32[]{:S(2)}) %collective-permute-start.3) | collective-permute-done | bytes 32800 | tf_op jit(solution)/shard_map/ppermute | solution.py:259
  19.9 0.0 collective-permute-done.4.swapped_ref
  19.9 3.4 %collective-permute-start.5 = (bf16[2,128,128]{2,1,0:T(8,128)(2,1)S(1)}, bf16[2,128,128]{2,1,0:T(8,128)(2,1)S(1)}, u32[]{:S(2)}, u32[]{:S(2)}) collective-permute-start(bf16[2,128,128]{2,1,0:T(8,128)(2,1)S(1)} %pad_maximum_fusion), channel_id=1, source_target_pairs={{0,12},{4,0},{8,4},{12,8},{16,28},{20,16},{24,20},{28,24},{32,44},... | collective-permute-start | bytes 196616 | tf_op jit(solution)/shard_map/ppermute | solution.py:265
  23.3 1.1 %collective-permute-start.6 = (bf16[2,128,128]{2,1,0:T(8,128)(2,1)S(1)}, bf16[2,128,128]{2,1,0:T(8,128)(2,1)S(1)}, u32[]{:S(2)}, u32[]{:S(2)}) collective-permute-start(bf16[2,128,128]{2,1,0:T(8,128)(2,1)S(1)} %pad_maximum_fusion), channel_id=1, source_target_pairs={{0,8},{4,12},{8,0},{12,4},{16,24},{20,28},{24,16},{28,20},{32,40},... | collective-permute-start | bytes 196616 | tf_op jit(solution)/shard_map/ppermute | solution.py:265
  24.4 1.3 %collective-permute-start.7 = (bf16[2,128,128]{2,1,0:T(8,128)(2,1)S(1)}, bf16[2,128,128]{2,1,0:T(8,128)(2,1)S(1)}, u32[]{:S(2)}, u32[]{:S(2)}) collective-permute-start(bf16[2,128,128]{2,1,0:T(8,128)(2,1)S(1)} %pad_maximum_fusion), channel_id=1, source_target_pairs={{0,4},{4,8},{8,12},{12,0},{16,20},{20,24},{24,28},{28,16},{32,36},... | collective-permute-start | bytes 196616 | tf_op jit(solution)/shard_map/ppermute | solution.py:265
  25.8 0.8 %collective-permute-start.8 = (bf16[2,128,128]{2,1,0:T(8,128)(2,1)S(1)}, bf16[2,128,128]{2,1,0:T(8,128)(2,1)S(1)}, u32[]{:S(2)}, u32[]{:S(2)}) collective-permute-start(bf16[2,128,128]{2,1,0:T(8,128)(2,1)S(1)} %pad_maximum_fusion.1), channel_id=1, source_target_pairs={{0,2},{1,3},{2,0},{3,1},{4,6},{5,7},{6,4},{7,5},{8,10},{9,11},{10,... | collective-permute-start | bytes 196616 | tf_op jit(solution)/shard_map/ppermute | solution.py:264
  26.6 0.0 collective-permute-done.5
  26.6 2.8 %collective-permute-done.6 = bf16[2,128,128]{2,1,0:T(8,128)(2,1)S(1)} collective-permute-done((bf16[2,128,128]{2,1,0:T(8,128)(2,1)S(1)}, bf16[2,128,128]{2,1,0:T(8,128)(2,1)S(1)}, u32[]{:S(2)}, u32[]{:S(2)}) %collective-permute-start.6) | collective-permute-done | bytes 65568 | tf_op jit(solution)/shard_map/ppermute | solution.py:265
  29.4 0.7 %collective-permute-done.7 = bf16[2,128,128]{2,1,0:T(8,128)(2,1)S(1)} collective-permute-done((bf16[2,128,128]{2,1,0:T(8,128)(2,1)S(1)}, bf16[2,128,128]{2,1,0:T(8,128)(2,1)S(1)}, u32[]{:S(2)}, u32[]{:S(2)}) %collective-permute-start.7) | collective-permute-done | bytes 65568 | tf_op jit(solution)/shard_map/ppermute | solution.py:265
  30.1 0.0 collective-permute-done.8.far_ref
  30.1 2.8 %collective-permute-start.9 = (bf16[8,128,128]{2,1,0:T(8,128)(2,1)S(1)}, bf16[8,128,128]{2,1,0:T(8,128)(2,1)S(1)}, u32[]{:S(2)}, u32[]{:S(2)}) collective-permute-start(bf16[8,128,128]{2,1,0:T(8,128)(2,1)S(1)} %constant_dynamic-update-slice_fusion.refs_0_), channel_id=1, source_target_pairs={{0,32},{4,36},{8,40},{12,44},{16,48},{20,52},{24,56},{28,60},{32,6... | collective-permute-start | bytes 786440 | tf_op jit(solution)/shard_map/ppermute | solution.py:273
  32.9 0.0 collective-permute-start.13
  32.9 0.3 feats_one.1.first_ref
  33.2 1.9 %planes.5 = (bf16[512,8192]{1,0:T(8,128)(2,1)}, bf16[512,2048]{1,0:T(8,128)(2,1)}, bf16[8,512,256]{2,1,0:T(8,128)(2,1)S(1)}) custom-call(bf16[512,256]{1,0:T(8,128)(2,1)S(1)} %feats_one.1.first_ref, bf16[256,128]{1,0:T(8,128)(2,1)S(1)} %get-tuple-element.61.weight_ref, f32[2,128]{1,0:T(2,128)S(1)} %get-tuple-element.62.bias_ref, ...), custom_call_target="tpu_custom_call" | custom-call | flops 1400000000 | bytes 1500000 | tf_op jit(solution)/shard_map/planes/pallas_call | solution.py:224
  35.1 2.3 %collective-permute-done.9.refs_0_ = bf16[8,128,128]{2,1,0:T(8,128)(2,1)S(1)} collective-permute-done((bf16[8,128,128]{2,1,0:T(8,128)(2,1)S(1)}, bf16[8,128,128]{2,1,0:T(8,128)(2,1)S(1)}, u32[]{:S(2)}, u32[]{:S(2)}) %collective-permute-start.9) | collective-permute-done | bytes 262176 | tf_op jit(solution)/shard_map/ppermute | solution.py:273
  37.4 3.1 %collective-permute-start.10 = (bf16[8,128,128]{2,1,0:T(8,128)(2,1)S(1)}, bf16[8,128,128]{2,1,0:T(8,128)(2,1)S(1)}, u32[]{:S(2)}, u32[]{:S(2)}) collective-permute-start(bf16[8,128,128]{2,1,0:T(8,128)(2,1)S(1)} %collective-permute-done.9.refs_0_), channel_id=1, source_target_pairs={{0,32},{4,36},{8,40},{12,44},{16,48},{20,52},{24,56},{28,60},{32,6... | collective-permute-start | bytes 786440 | tf_op jit(solution)/shard_map/ppermute | solution.py:273
  40.5 0.0 collective-permute-done.13.refs_1_
  40.5 0.0 collective-permute-start.14
  40.5 3.2 %planes.6 = (bf16[512,8192]{1,0:T(8,128)(2,1)}, bf16[512,2048]{1,0:T(8,128)(2,1)}, bf16[8,512,256]{2,1,0:T(8,128)(2,1)S(1)}) custom-call(bf16[512,256]{1,0:T(8,128)(2,1)S(1)} %feats_one.1.first_ref, bf16[256,128]{1,0:T(8,128)(2,1)S(1)} %get-tuple-element.61.weight_ref, ...), custom_call_target="tpu_custom_call", output_to_operand_aliasing={{0}: (5, {}), {1}: (6, {}), {2}: (7, {})} | custom-call | flops 2800000000 | bytes 3000000 | tf_op jit(solution)/shard_map/planes/pallas_call | solution.py:224
  43.8 1.5 %collective-permute-done.10.refs_0_ = bf16[8,128,128]{2,1,0:T(8,128)(2,1)S(1)} collective-permute-done((bf16[8,128,128]{2,1,0:T(8,128)(2,1)S(1)}, bf16[8,128,128]{2,1,0:T(8,128)(2,1)S(1)}, u32[]{:S(2)}, u32[]{:S(2)}) %collective-permute-start.10) | collective-permute-done | bytes 262176 | tf_op jit(solution)/shard_map/ppermute | solution.py:273
  45.3 3.7 %collective-permute-start.11 = (bf16[8,128,128]{2,1,0:T(8,128)(2,1)S(1)}, bf16[8,128,128]{2,1,0:T(8,128)(2,1)S(1)}, u32[]{:S(2)}, u32[]{:S(2)}) collective-permute-start(bf16[8,128,128]{2,1,0:T(8,128)(2,1)S(1)} %collective-permute-done.10.refs_0_), channel_id=1, source_target_pairs={{0,32},{4,36},{8,40},{12,44},{16,48},{20,52},{24,56},{28,60},{32,6... | collective-permute-start | bytes 786440 | tf_op jit(solution)/shard_map/ppermute | solution.py:273
  49.0 0.2 collective-permute-done.14.refs_1_
  49.2 0.0 collective-permute-start.15
  49.2 3.2 %planes.7 = (bf16[512,8192]{1,0:T(8,128)(2,1)}, bf16[512,2048]{1,0:T(8,128)(2,1)}, bf16[8,512,256]{2,1,0:T(8,128)(2,1)S(1)}) custom-call(bf16[512,256]{1,0:T(8,128)(2,1)S(1)} %feats_one.1.first_ref, bf16[256,128]{1,0:T(8,128)(2,1)S(1)} %get-tuple-element.61.weight_ref, ...), custom_call_target="tpu_custom_call", output_to_operand_aliasing={{0}: (5, {}), {1}: (6, {}), {2}: (7, {})} | custom-call | flops 2800000000 | bytes 3000000 | tf_op jit(solution)/shard_map/planes/pallas_call | solution.py:224
  52.4 1.8 %collective-permute-done.11.refs_0_ = bf16[8,128,128]{2,1,0:T(8,128)(2,1)S(1)} collective-permute-done((bf16[8,128,128]{2,1,0:T(8,128)(2,1)S(1)}, bf16[8,128,128]{2,1,0:T(8,128)(2,1)S(1)}, u32[]{:S(2)}, u32[]{:S(2)}) %collective-permute-start.11) | collective-permute-done | bytes 262176 | tf_op jit(solution)/shard_map/ppermute | solution.py:273
  54.3 3.8 %collective-permute-start.12 = (bf16[4,128,128]{2,1,0:T(8,128)(2,1)S(1)}, bf16[4,128,128]{2,1,0:T(8,128)(2,1)S(1)}, u32[]{:S(2)}, u32[]{:S(2)}) collective-permute-start(bf16[4,128,128]{2,1,0:T(8,128)(2,1)S(1)} %slice.8), channel_id=1, source_target_pairs={{0,32},{4,36},{8,40},{12,44},{16,48},{20,52},{24,56},{28,60},{32,6... | collective-permute-start | bytes 393224 | tf_op jit(solution)/shard_map/ppermute | solution.py:276
  58.0 0.1 collective-permute-done.15.refs_1_
  58.2 0.1 collective-permute-start.16
  58.3 3.2 %planes.8 = (bf16[512,8192]{1,0:T(8,128)(2,1)}, bf16[512,2048]{1,0:T(8,128)(2,1)}, bf16[8,512,256]{2,1,0:T(8,128)(2,1)S(1)}) custom-call(bf16[512,256]{1,0:T(8,128)(2,1)S(1)} %feats_one.1.first_ref, bf16[256,128]{1,0:T(8,128)(2,1)S(1)} %get-tuple-element.61.weight_ref, ...), custom_call_target="tpu_custom_call", output_to_operand_aliasing={{0}: (5, {}), {1}: (6, {}), {2}: (7, {})} | custom-call | flops 2800000000 | bytes 3000000 | tf_op jit(solution)/shard_map/planes/pallas_call | solution.py:224
  61.5 0.0 collective-permute-done.12.refs_0_
  61.6 2.9 %collective-permute-done.16.refs_1_ = bf16[4,128,128]{2,1,0:T(8,128)(2,1)S(1)} collective-permute-done((bf16[4,128,128]{2,1,0:T(8,128)(2,1)S(1)}, bf16[4,128,128]{2,1,0:T(8,128)(2,1)S(1)}, u32[]{:S(2)}, u32[]{:S(2)}) %collective-permute-start.16) | collective-permute-done | bytes 131104 | tf_op jit(solution)/shard_map/ppermute | solution.py:277
  64.5 2.2 %planes.9 = (bf16[512,8192]{1,0:T(8,128)(2,1)}, bf16[512,2048]{1,0:T(8,128)(2,1)}, bf16[512,512]{1,0:T(8,128)(2,1)}, bf16[512,128]{1,0:T(8,128)(2,1)}) custom-call(bf16[512,256]{1,0:T(8,128)(2,1)S(1)} %feats_one.1.first_ref, bf16[256,128]{1,0:T(8,128)(2,1)S(1)} %get-tuple-element.61.weight_ref, ...), custom_call_target="tpu_custom_call", output_to_operand_aliasing={{0}: (5, {}), {1}: (6, {})} | custom-call | flops 1400000000 | bytes 1500000 | tf_op jit(solution)/shard_map/planes/pallas_call | solution.py:224
  (11 shorter events, 0.1 us)
Async XLA Ops:
  0.6 0.9 %copy-start = (bf16[2,96,4,128]{3,2,1,0:T(4,128)(2,1)S(1)}, bf16[2,96,4,128]{3,2,1,0:T(4,128)(2,1)}, u32[]{:S(2)}) copy-start(bf16[2,96,4,128]{3,2,1,0:T(4,128)(2,1)} %param.5) | copy-start | bytes 589828
  2.0 16.3 %copy-start.3 = (f32[256]{0:T(256)S(1)}, f32[256]{0:T(256)}, u32[]{:S(2)}) copy-start(f32[256]{0:T(256)} %param.9) | copy-start | bytes 3076
  2.0 11.6 %collective-permute-start = (bf16[96,256]{1,0:T(8,128)(2,1)S(1)}, bf16[96,256]{1,0:T(8,128)(2,1)S(1)}, u32[]{:S(2)}, u32[]{:S(2)}) collective-permute-start(bf16[96,256]{1,0:T(8,128)(2,1)S(1)} %get-tuple-element.44), channel_id=1, source_target_pairs={{0,4},{4,8},{8,12},{12,16},{16,20},{20,24},{24,28},{28,32},{32,36}... | collective-permute-start | bytes 147464 | tf_op jit(solution)/shard_map/ppermute | solution.py:247
  5.6 8.1 %collective-permute-start.2 = (bf16[96,256]{1,0:T(8,128)(2,1)S(1)}, bf16[96,256]{1,0:T(8,128)(2,1)S(1)}, u32[]{:S(2)}, u32[]{:S(2)}) collective-permute-start(bf16[96,256]{1,0:T(8,128)(2,1)S(1)} %get-tuple-element.44), channel_id=1, source_target_pairs={{0,5},{1,6},{2,7},{4,9},{5,10},{6,11},{8,13},{9,14},{10,15},{12,17... | collective-permute-start | bytes 147464 | tf_op jit(solution)/shard_map/ppermute | solution.py:246
  8.1 5.5 %collective-permute-start.1 = (bf16[16,384]{1,0:T(8,128)(2,1)S(1)}, bf16[16,384]{1,0:T(8,128)(2,1)S(1)}, u32[]{:S(2)}, u32[]{:S(2)}) collective-permute-start(bf16[16,384]{1,0:T(8,128)(2,1)S(1)} %get-tuple-element.45), channel_id=1, source_target_pairs={{0,1},{1,2},{2,3},{4,5},{5,6},{6,7},{8,9},{9,10},{10,11},{12,13},{... | collective-permute-start | bytes 36872 | tf_op jit(solution)/shard_map/ppermute | solution.py:248
  12.0 0.9 %copy-start.1 = (bf16[128,864]{0,1:T(8,128)(2,1)S(1)}, bf16[128,864]{0,1:T(8,128)(2,1)}, u32[]{:S(2)}) copy-start(bf16[128,864]{0,1:T(8,128)(2,1)} %param.6) | copy-start | bytes 663556
  13.0 0.7 copy-start.4
  13.6 4.7 %copy-start.2 = (bf16[256,128]{1,0:T(8,128)(2,1)S(1)}, bf16[256,128]{1,0:T(8,128)(2,1)}, u32[]{:S(2)}) copy-start(bf16[256,128]{1,0:T(8,128)(2,1)} %refs_0_) | copy-start | bytes 196612
  14.4 5.5 %collective-permute-start.3 = (bf16[128,128]{1,0:T(8,128)(2,1)S(1)}, bf16[128,128]{1,0:T(8,128)(2,1)S(1)}, u32[]{:S(2)}, u32[]{:S(2)}) collective-permute-start(bf16[128,128]{1,0:T(8,128)(2,1)S(1)} %get-tuple-element.53), channel_id=1, source_target_pairs={{0,16},{4,20},{8,24},{12,28},{16,0},{20,4},{24,8},{28,12},{32,48},... | collective-permute-start | bytes 98312 | tf_op jit(solution)/shard_map/ppermute | solution.py:259
  17.4 2.5 %collective-permute-start.4 = (bf16[128,128]{1,0:T(8,128)(2,1)S(1)}, bf16[128,128]{1,0:T(8,128)(2,1)S(1)}, u32[]{:S(2)}, u32[]{:S(2)}) collective-permute-start(bf16[128,128]{1,0:T(8,128)(2,1)S(1)} %get-tuple-element.52.own_ref), channel_id=1, source_target_pairs={{0,1},{1,0},{2,3},{3,2},{4,5},{5,4},{6,7},{7,6},{8,9},{9,8},{10,11... | collective-permute-start | bytes 98312 | tf_op jit(solution)/shard_map/ppermute | solution.py:261
  19.9 6.7 %collective-permute-start.5 = (bf16[2,128,128]{2,1,0:T(8,128)(2,1)S(1)}, bf16[2,128,128]{2,1,0:T(8,128)(2,1)S(1)}, u32[]{:S(2)}, u32[]{:S(2)}) collective-permute-start(bf16[2,128,128]{2,1,0:T(8,128)(2,1)S(1)} %pad_maximum_fusion), channel_id=1, source_target_pairs={{0,12},{4,0},{8,4},{12,8},{16,28},{20,16},{24,20},{28,24},{32,44},... | collective-permute-start | bytes 196616 | tf_op jit(solution)/shard_map/ppermute | solution.py:265
  23.3 6.1 %collective-permute-start.6 = (bf16[2,128,128]{2,1,0:T(8,128)(2,1)S(1)}, bf16[2,128,128]{2,1,0:T(8,128)(2,1)S(1)}, u32[]{:S(2)}, u32[]{:S(2)}) collective-permute-start(bf16[2,128,128]{2,1,0:T(8,128)(2,1)S(1)} %pad_maximum_fusion), channel_id=1, source_target_pairs={{0,8},{4,12},{8,0},{12,4},{16,24},{20,28},{24,16},{28,20},{32,40},... | collective-permute-start | bytes 196616 | tf_op jit(solution)/shard_map/ppermute | solution.py:265
  24.4 5.6 %collective-permute-start.7 = (bf16[2,128,128]{2,1,0:T(8,128)(2,1)S(1)}, bf16[2,128,128]{2,1,0:T(8,128)(2,1)S(1)}, u32[]{:S(2)}, u32[]{:S(2)}) collective-permute-start(bf16[2,128,128]{2,1,0:T(8,128)(2,1)S(1)} %pad_maximum_fusion), channel_id=1, source_target_pairs={{0,4},{4,8},{8,12},{12,0},{16,20},{20,24},{24,28},{28,16},{32,36},... | collective-permute-start | bytes 196616 | tf_op jit(solution)/shard_map/ppermute | solution.py:265
  25.8 4.4 %collective-permute-start.8 = (bf16[2,128,128]{2,1,0:T(8,128)(2,1)S(1)}, bf16[2,128,128]{2,1,0:T(8,128)(2,1)S(1)}, u32[]{:S(2)}, u32[]{:S(2)}) collective-permute-start(bf16[2,128,128]{2,1,0:T(8,128)(2,1)S(1)} %pad_maximum_fusion.1), channel_id=1, source_target_pairs={{0,2},{1,3},{2,0},{3,1},{4,6},{5,7},{6,4},{7,5},{8,10},{9,11},{10,... | collective-permute-start | bytes 196616 | tf_op jit(solution)/shard_map/ppermute | solution.py:264
  30.1 7.2 %collective-permute-start.9 = (bf16[8,128,128]{2,1,0:T(8,128)(2,1)S(1)}, bf16[8,128,128]{2,1,0:T(8,128)(2,1)S(1)}, u32[]{:S(2)}, u32[]{:S(2)}) collective-permute-start(bf16[8,128,128]{2,1,0:T(8,128)(2,1)S(1)} %constant_dynamic-update-slice_fusion.refs_0_), channel_id=1, source_target_pairs={{0,32},{4,36},{8,40},{12,44},{16,48},{20,52},{24,56},{28,60},{32,6... | collective-permute-start | bytes 786440 | tf_op jit(solution)/shard_map/ppermute | solution.py:273
  32.9 7.6 %collective-permute-start.13 = (bf16[8,128,128]{2,1,0:T(8,128)(2,1)S(1)}, bf16[8,128,128]{2,1,0:T(8,128)(2,1)S(1)}, u32[]{:S(2)}, u32[]{:S(2)}) collective-permute-start(bf16[8,128,128]{2,1,0:T(8,128)(2,1)S(1)} %constant_dynamic-update-slice_fusion.refs_0_), channel_id=1, source_target_pairs={{0,224},{4,228},{8,232},{12,236},{16,240},{20,244},{24,248},{28,25... | collective-permute-start | bytes 786440 | tf_op jit(solution)/shard_map/ppermute | solution.py:274
  37.4 7.9 %collective-permute-start.10 = (bf16[8,128,128]{2,1,0:T(8,128)(2,1)S(1)}, bf16[8,128,128]{2,1,0:T(8,128)(2,1)S(1)}, u32[]{:S(2)}, u32[]{:S(2)}) collective-permute-start(bf16[8,128,128]{2,1,0:T(8,128)(2,1)S(1)} %collective-permute-done.9.refs_0_), channel_id=1, source_target_pairs={{0,32},{4,36},{8,40},{12,44},{16,48},{20,52},{24,56},{28,60},{32,6... | collective-permute-start | bytes 786440 | tf_op jit(solution)/shard_map/ppermute | solution.py:273
  40.5 8.7 %collective-permute-start.14 = (bf16[8,128,128]{2,1,0:T(8,128)(2,1)S(1)}, bf16[8,128,128]{2,1,0:T(8,128)(2,1)S(1)}, u32[]{:S(2)}, u32[]{:S(2)}) collective-permute-start(bf16[8,128,128]{2,1,0:T(8,128)(2,1)S(1)} %collective-permute-done.13.refs_1_), channel_id=1, source_target_pairs={{0,224},{4,228},{8,232},{12,236},{16,240},{20,244},{24,248},{28,25... | collective-permute-start | bytes 786440 | tf_op jit(solution)/shard_map/ppermute | solution.py:274
  45.3 9.0 %collective-permute-start.11 = (bf16[8,128,128]{2,1,0:T(8,128)(2,1)S(1)}, bf16[8,128,128]{2,1,0:T(8,128)(2,1)S(1)}, u32[]{:S(2)}, u32[]{:S(2)}) collective-permute-start(bf16[8,128,128]{2,1,0:T(8,128)(2,1)S(1)} %collective-permute-done.10.refs_0_), channel_id=1, source_target_pairs={{0,32},{4,36},{8,40},{12,44},{16,48},{20,52},{24,56},{28,60},{32,6... | collective-permute-start | bytes 786440 | tf_op jit(solution)/shard_map/ppermute | solution.py:273
  49.2 9.0 %collective-permute-start.15 = (bf16[8,128,128]{2,1,0:T(8,128)(2,1)S(1)}, bf16[8,128,128]{2,1,0:T(8,128)(2,1)S(1)}, u32[]{:S(2)}, u32[]{:S(2)}) collective-permute-start(bf16[8,128,128]{2,1,0:T(8,128)(2,1)S(1)} %collective-permute-done.14.refs_1_), channel_id=1, source_target_pairs={{0,224},{4,228},{8,232},{12,236},{16,240},{20,244},{24,248},{28,25... | collective-permute-start | bytes 786440 | tf_op jit(solution)/shard_map/ppermute | solution.py:274
  54.3 7.3 %collective-permute-start.12 = (bf16[4,128,128]{2,1,0:T(8,128)(2,1)S(1)}, bf16[4,128,128]{2,1,0:T(8,128)(2,1)S(1)}, u32[]{:S(2)}, u32[]{:S(2)}) collective-permute-start(bf16[4,128,128]{2,1,0:T(8,128)(2,1)S(1)} %slice.8), channel_id=1, source_target_pairs={{0,32},{4,36},{8,40},{12,44},{16,48},{20,52},{24,56},{28,60},{32,6... | collective-permute-start | bytes 393224 | tf_op jit(solution)/shard_map/ppermute | solution.py:276
  58.2 6.3 %collective-permute-start.16 = (bf16[4,128,128]{2,1,0:T(8,128)(2,1)S(1)}, bf16[4,128,128]{2,1,0:T(8,128)(2,1)S(1)}, u32[]{:S(2)}, u32[]{:S(2)}) collective-permute-start(bf16[4,128,128]{2,1,0:T(8,128)(2,1)S(1)} %slice.9), channel_id=1, source_target_pairs={{0,224},{4,228},{8,232},{12,236},{16,240},{20,244},{24,248},{28,25... | collective-permute-start | bytes 393224 | tf_op jit(solution)/shard_map/ppermute | solution.py:277

commit v7 on v6

--- a/solution.py
+++ b/solution.py
@@ -141,22 +141,56 @@
     )(*hidden, proj_weight, proj_bias)
 
 
+def pool_one():
+    row, col = iotas(512, 128)
+    return one_hot(col == (row >> 7) * 32 + ((row & 63) >> 1), 0.25)
+
+
+def bias_lanes(bias_ref):
+    bias = jnp.concatenate(
+        [jnp.transpose(jnp.broadcast_to(bias_ref[n : n + 1, :], (128, 128))) for n in range(2)], axis=0
+    )
+    return jnp.concatenate([bias] * 4, axis=1)
+
+
+def half_kernel(first_ref, weight_ref, bias_ref, hid_ref, _, zero_out, part_ref, zero_buf, sem):
+    z, yh, x = position()
+    start = ((z + Z // 2) & (Z - 1)) * 1024 + yh * 512
+    hid = jnp.concatenate([hid_ref[(j - x) & (X - 1)] for j in range(X)], axis=1)
+    feats = (dot(weight_ref[...], hid) + bias_lanes(bias_ref)).astype(BF)
+    zero = dot(first_ref[...], feats).astype(BF)
+    zero_buf[...] = zero
+    copy = pltpu.make_async_copy(zero_buf, zero_out.at[:, pl.ds(pl.multiple_of(start, 512), 512)], sem)
+    copy.start()
+    part_ref[...] = dot(zero, pool_one()).astype(BF)
+    copy.wait()
+
+
+def half_call(hidden, first, proj_weight, proj_bias, zero):
+    return pl.pallas_call(
+        half_kernel,
+        in_specs=[VMEM] * 4 + [ANYWHERE],
+        out_specs=[ANYWHERE, VMEM],
+        out_shape=[jax.ShapeDtypeStruct((512, 8192), BF), jax.ShapeDtypeStruct((512, 128), BF)],
+        scratch_shapes=[pltpu.VMEM((512, 512), BF), pltpu.SemaphoreType.DMA],
+        input_output_aliases={4: 0},
+        compiler_params=SMALL,
+        cost_estimate=pl.CostEstimate(flops=700_000_000, bytes_accessed=750_000, transcendentals=0),
+        name="half_plane",
+    )(first, proj_weight, proj_bias, hidden, zero)
+
+
 def planes_kernel(offsets, last, n_alias, first_ref, weight_ref, bias_ref, *refs):
-    n_hid = 2 if last else len(offsets)
+    n_hid = len(offsets)
     hid_refs, rest = refs[:n_hid], refs[n_hid + n_alias :]
     if last:
-        small_ref, zero_out, one_out, two_out, three_out = rest[:5]
-        zero_buf, one_buf, two_buf, three_buf, hid_buf, sems = rest[5:]
+        small_ref, part_ref, zero_out, one_out, two_out, three_out = rest[:6]
+        zero_buf, one_buf, two_buf, three_buf, sems = rest[6:]
     else:
         zero_out, one_out, small_out, zero_buf, one_buf, small_buf, sems = rest
     z, yh, x = position()
-    order = [((j % X - x) & (X - 1)) * 2 + (yh ^ (j // X)) for j in range(PLANE)]
-    row, col = iotas(512, 128)
-    pool1 = one_hot(col == (row >> 7) * 32 + ((row & 63) >> 1), 0.25)
-    bias = jnp.concatenate(
-        [jnp.transpose(jnp.broadcast_to(bias_ref[n : n + 1, :], (128, 128))) for n in range(2)], axis=0
-    )
-    bias = jnp.concatenate([bias] * 4, axis=1)
+    order = [(yh ^ (j // X)) * X + ((j % X - x) & (X - 1)) for j in range(PLANE)]
+    pool1, bias = pool_one(), bias_lanes(bias_ref)
     copies = []
 
     def send(source, target):
@@ -165,21 +199,20 @@
 
     for n, offset in enumerate(offsets):
         place = (z + (offset + Z)) & (Z - 1)
-        if last:
-            hid_buf[0:4] = hid_refs[0][...]
-            hid_buf[4:8] = hid_refs[1][...]
-            hid_ref = hid_buf
-        else:
-            hid_ref = hid_refs[n]
+        hid_ref = hid_refs[n]
         ones = []
-        for half in range(2):
-            hid = jnp.concatenate([hid_ref[order[4 * half + j]] for j in range(4)], axis=1)
+        for half in (1 - yh,) if last else (0, 1):
+            blocks = order[:X] if last else order[X * half : X * (half + 1)]
+            hid = jnp.concatenate([hid_ref[block & (X - 1) if last else block] for block in blocks], axis=1)
             feats = (dot(weight_ref[...], hid) + bias).astype(BF)
             zero = dot(first_ref[...], feats).astype(BF)
-            slot = 2 * n + half
+            slot = 2 * n + len(ones)
             zero_buf[slot] = zero
             send(zero_buf.at[slot], zero_out.at[:, pl.ds(pl.multiple_of(place * 1024 + half * 512, 512), 512)])
             ones.append(dot(zero, pool1).astype(BF))
+        if last:
+            part = part_ref[...]
+            ones = [jnp.where(yh == 0, part, ones[0]), jnp.where(yh == 0, ones[0], part)]
         one = jnp.concatenate(ones, axis=1)
         one_buf[n] = one
         send(one_buf.at[n], one_out.at[:, pl.ds(pl.multiple_of(place * 256, 256), 256)])
@@ -220,7 +253,7 @@
     small = [(512, 512), (512, 128)] if last else [(Z, 512, 256)]
     shapes = [(512, 8192), (512, 2048)] + small
     scratch = [(2 * count, 512, 512), (count, 512, 256)]
-    scratch += small + [(8, 128, 128)] if last else [(count, 512, 256)]
+    scratch += small if last else [(count, 512, 256)]
     return pl.pallas_call(
         functools.partial(planes_kernel, offsets, last, len(aliases)),
         in_specs=in_specs,
@@ -262,7 +295,8 @@
     other, swapped, proj_weight, proj_bias = lax.optimization_barrier((other, swapped, proj_weight, proj_bias))
     pair = jnp.stack([hidden_two, other])
     far = lax.ppermute(jnp.stack([hidden_one, swapped]), "cols", [(k, k ^ 2) for k in range(COLS)])
-    mine = jnp.concatenate([pair] + [lax.ppermute(pair, "rows", along("x", -s)) for s in range(1, X)])
+    pairs = [pair] + [lax.ppermute(pair, "rows", along("x", -s)) for s in range(1, X)]
+    mine = jnp.concatenate([p[n : n + 1] for n in range(YH) for p in pairs])
     mine, far = lax.optimization_barrier((mine, far))
     first = feats_one((hidden_one, swapped, far), proj_weight, proj_bias)
 
@@ -275,7 +309,8 @@
         outs = call((-step, step), [below, above], outs=outs)
     below = lax.ppermute(below[:4], "rows", along("z", 1))
     above = lax.ppermute(above[4:], "rows", along("z", -1))
-    return tuple(call((Z // 2,), [below, above], outs=outs, last=True))
+    zero, part = half_call(below, first, proj_weight, proj_bias, outs[0])
+    return tuple(call((Z // 2,), [above], outs=[zero, outs[1], outs[2], part], last=True))
 
 
 def solution(mesh):

time: 68.1 us -> 72.6 us (1.066)
  the two profiles are of different devices: /device:TPU:96 before, /device:TPU:8 now
where the time goes in v7:
time: 72.6 us; the launch traced here: 72.4 us
  starting transfers between devices  34 us (47%)
  waiting for transfers between devices  18.2 us (25%)
  Pallas kernels  16.6 us (23%)
  local copies, waits for them, and re-layouts  2.6 us (4%)
  between operations  0.99 us (1%)
    pallas_call x5, Pallas kernels, planes_call(): pl.pallas_call(functools.partial(planes_kernel, offsets, last, len(aliase...  13.6 us
    ppermute x3, starting transfers between devices, per_device(): above = lax.ppermute(above, 'rows', along('z', -1))  13.3 us
    ppermute x3, waiting for transfers between devices, per_device(): below = lax.ppermute(below, 'rows', along('z', 1))  6.52 us
    ppermute x3, starting transfers between devices, per_device(): lax.ppermute(pair, 'rows', along('x', -s))  4.79 us
    ppermute x3, waiting for transfers between devices, per_device(): lax.ppermute(pair, 'rows', along('x', -s))  4.01 us
    ppermute x3, waiting for transfers between devices, per_device(): above = lax.ppermute(above, 'rows', along('z', -1))  3.99 us
    ppermute x1, starting transfers between devices, per_device(): other = lax.ppermute(hidden_two, 'rows', along('yh', 1))  3.78 us
    ppermute x1, starting transfers between devices, per_device(): top = lax.ppermute(top, 'rows', down)  3.55 us
  transfers between devices with their start and end apart: 17, of which 9 were waited for; matrix products, arithmetic and copies ran while one was open for 0% of the time, Pallas kernels for 18%

profile of v7, /device:TPU:8, one launch (start us, length us, event | category | flops | bytes accessed | tf_op | source)
XLA Modules:
  0.0 72.4 jit_solution(14872479693924623069)
XLA Ops:
  0.6 0.0 copy-start
  0.6 0.9 %copy-done = bf16[2,96,4,128]{3,2,1,0:T(4,128)(2,1)S(1)} copy-done((bf16[2,96,4,128]{3,2,1,0:T(4,128)(2,1)S(1)}, bf16[2,96,4,128]{3,2,1,0:T(4,128)(2,1)}, u32[]{:S(2)}) %copy-start) | copy-done | bytes 196632
  1.6 0.5 split_tile.1
  2.0 0.0 copy-start.3
  2.0 3.5 %collective-permute-start = (bf16[96,256]{1,0:T(8,128)(2,1)S(1)}, bf16[96,256]{1,0:T(8,128)(2,1)S(1)}, u32[]{:S(2)}, u32[]{:S(2)}) collective-permute-start(bf16[96,256]{1,0:T(8,128)(2,1)S(1)} %get-tuple-element.46), channel_id=1, source_target_pairs={{0,4},{4,8},{8,12},{12,16},{16,20},{20,24},{24,28},{28,32},{32,36}... | collective-permute-start | bytes 147464 | tf_op jit(solution)/shard_map/ppermute | solution.py:280
  5.6 2.6 %collective-permute-start.2 = (bf16[96,256]{1,0:T(8,128)(2,1)S(1)}, bf16[96,256]{1,0:T(8,128)(2,1)S(1)}, u32[]{:S(2)}, u32[]{:S(2)}) collective-permute-start(bf16[96,256]{1,0:T(8,128)(2,1)S(1)} %get-tuple-element.46), channel_id=1, source_target_pairs={{0,5},{1,6},{2,7},{4,9},{5,10},{6,11},{8,13},{9,14},{10,15},{12,17... | collective-permute-start | bytes 147464 | tf_op jit(solution)/shard_map/ppermute | solution.py:279
  8.1 1.9 %collective-permute-start.1 = (bf16[16,384]{1,0:T(8,128)(2,1)S(1)}, bf16[16,384]{1,0:T(8,128)(2,1)S(1)}, u32[]{:S(2)}, u32[]{:S(2)}) collective-permute-start(bf16[16,384]{1,0:T(8,128)(2,1)S(1)} %get-tuple-element.47), channel_id=1, source_target_pairs={{0,1},{1,2},{2,3},{4,5},{5,6},{6,7},{8,9},{9,10},{10,11},{12,13},{... | collective-permute-start | bytes 36872 | tf_op jit(solution)/shard_map/ppermute | solution.py:281
  10.1 0.0 copy-start.1
  10.1 0.9 %copy-done.1 = bf16[128,864]{0,1:T(8,128)(2,1)S(1)} copy-done((bf16[128,864]{0,1:T(8,128)(2,1)S(1)}, bf16[128,864]{0,1:T(8,128)(2,1)}, u32[]{:S(2)}) %copy-start.1) | copy-done | bytes 221208
  11.0 0.0 copy-start.4
  11.0 0.7 copy-done.4
  11.7 0.0 copy-start.2
  11.7 1.8 %collective-permute-done.1.left_ref = bf16[16,384]{1,0:T(8,128)(2,1)S(1)} collective-permute-done((bf16[16,384]{1,0:T(8,128)(2,1)S(1)}, bf16[16,384]{1,0:T(8,128)(2,1)S(1)}, u32[]{:S(2)}, u32[]{:S(2)}) %collective-permute-start.1) | collective-permute-done | bytes 12320 | tf_op jit(solution)/shard_map/ppermute | solution.py:281
  13.4 0.0 collective-permute-done.top_ref
  13.4 0.0 collective-permute-done.2.corner_ref
  13.4 0.7 %hidden.1 = (bf16[128,128]{1,0:T(8,128)(2,1)S(1)}, bf16[128,128]{1,0:T(8,128)(2,1)S(1)}) custom-call(bf16[384,256]{1,0:T(8,128)(2,1)S(1)} %get-tuple-element.45.main_ref, bf16[96,256]{1,0:T(8,128)(2,1)S(1)} %collective-permute-done.top_ref, bf16[16,384]{1,0:T(8,128)(2,1)S(1)} %collective-permute-done.1.left_ref, ...), custom_call_target="tpu_custom_call" | custom-call | tf_op jit(solution)/shard_map/hidden/pallas_call | solution.py:114
  14.2 3.8 %collective-permute-start.3 = (bf16[128,128]{1,0:T(8,128)(2,1)S(1)}, bf16[128,128]{1,0:T(8,128)(2,1)S(1)}, u32[]{:S(2)}, u32[]{:S(2)}) collective-permute-start(bf16[128,128]{1,0:T(8,128)(2,1)S(1)} %get-tuple-element.55), channel_id=1, source_target_pairs={{0,16},{4,20},{8,24},{12,28},{16,0},{20,4},{24,8},{28,12},{32,48},... | collective-permute-start | bytes 98312 | tf_op jit(solution)/shard_map/ppermute | solution.py:292
  18.0 0.0 collective-permute-start.4
  18.0 0.0 copy-done.3
  18.0 0.0 copy-done.2
  18.0 1.9 %collective-permute-done.3 = bf16[128,128]{1,0:T(8,128)(2,1)S(1)} collective-permute-done((bf16[128,128]{1,0:T(8,128)(2,1)S(1)}, bf16[128,128]{1,0:T(8,128)(2,1)S(1)}, u32[]{:S(2)}, u32[]{:S(2)}) %collective-permute-start.3) | collective-permute-done | bytes 32800 | tf_op jit(solution)/shard_map/ppermute | solution.py:292
  19.9 0.0 collective-permute-done.4.swapped_ref
  19.9 3.1 %collective-permute-start.5 = (bf16[2,128,128]{2,1,0:T(8,128)(2,1)S(1)}, bf16[2,128,128]{2,1,0:T(8,128)(2,1)S(1)}, u32[]{:S(2)}, u32[]{:S(2)}) collective-permute-start(bf16[2,128,128]{2,1,0:T(8,128)(2,1)S(1)} %pad_maximum_fusion), channel_id=1, source_target_pairs={{0,12},{4,0},{8,4},{12,8},{16,28},{20,16},{24,20},{28,24},{32,44},... | collective-permute-start | bytes 196616 | tf_op jit(solution)/shard_map/ppermute | solution.py:298
  23.0 0.4 collective-permute-start.6
  23.4 1.3 %collective-permute-start.7 = (bf16[2,128,128]{2,1,0:T(8,128)(2,1)S(1)}, bf16[2,128,128]{2,1,0:T(8,128)(2,1)S(1)}, u32[]{:S(2)}, u32[]{:S(2)}) collective-permute-start(bf16[2,128,128]{2,1,0:T(8,128)(2,1)S(1)} %pad_maximum_fusion), channel_id=1, source_target_pairs={{0,4},{4,8},{8,12},{12,0},{16,20},{20,24},{24,28},{28,16},{32,36},... | collective-permute-start | bytes 196616 | tf_op jit(solution)/shard_map/ppermute | solution.py:298
  24.7 0.8 %collective-permute-start.8 = (bf16[2,128,128]{2,1,0:T(8,128)(2,1)S(1)}, bf16[2,128,128]{2,1,0:T(8,128)(2,1)S(1)}, u32[]{:S(2)}, u32[]{:S(2)}) collective-permute-start(bf16[2,128,128]{2,1,0:T(8,128)(2,1)S(1)} %pad_maximum_fusion.1), channel_id=1, source_target_pairs={{0,2},{1,3},{2,0},{3,1},{4,6},{5,7},{6,4},{7,5},{8,10},{9,11},{10,... | collective-permute-start | bytes 196616 | tf_op jit(solution)/shard_map/ppermute | solution.py:297
  25.4 0.0 collective-permute-done.5
  25.4 3.4 %collective-permute-done.6 = bf16[2,128,128]{2,1,0:T(8,128)(2,1)S(1)} collective-permute-done((bf16[2,128,128]{2,1,0:T(8,128)(2,1)S(1)}, bf16[2,128,128]{2,1,0:T(8,128)(2,1)S(1)}, u32[]{:S(2)}, u32[]{:S(2)}) %collective-permute-start.6) | collective-permute-done | bytes 65568 | tf_op jit(solution)/shard_map/ppermute | solution.py:298
  28.8 0.6 collective-permute-done.7
  29.5 0.0 collective-permute-done.8.far_ref
  29.5 5.9 %collective-permute-start.9 = (bf16[8,128,128]{2,1,0:T(8,128)(2,1)S(1)}, bf16[8,128,128]{2,1,0:T(8,128)(2,1)S(1)}, u32[]{:S(2)}, u32[]{:S(2)}) collective-permute-start(bf16[8,128,128]{2,1,0:T(8,128)(2,1)S(1)} %slice_dynamic-update-slice_fusion.refs_0_), channel_id=1, source_target_pairs={{0,224},{4,228},{8,232},{12,236},{16,240},{20,244},{24,248},{28,25... | collective-permute-start | bytes 786440 | tf_op jit(solution)/shard_map/ppermute | solution.py:308
  35.5 0.0 collective-permute-start.13
  35.5 0.3 feats_one.1.first_ref
  35.7 1.9 %planes.5 = (bf16[512,8192]{1,0:T(8,128)(2,1)}, bf16[512,2048]{1,0:T(8,128)(2,1)}, bf16[8,512,256]{2,1,0:T(8,128)(2,1)S(1)}) custom-call(bf16[512,256]{1,0:T(8,128)(2,1)S(1)} %feats_one.1.first_ref, bf16[256,128]{1,0:T(8,128)(2,1)S(1)} %get-tuple-element.63.weight_ref, f32[2,128]{1,0:T(2,128)S(1)} %get-tuple-element.64.bias_ref, ...), custom_call_target="tpu_custom_call" | custom-call | flops 1400000000 | bytes 1500000 | tf_op jit(solution)/shard_map/planes/pallas_call | solution.py:257
  37.6 2.1 %collective-permute-done.9.refs_1_ = bf16[8,128,128]{2,1,0:T(8,128)(2,1)S(1)} collective-permute-done((bf16[8,128,128]{2,1,0:T(8,128)(2,1)S(1)}, bf16[8,128,128]{2,1,0:T(8,128)(2,1)S(1)}, u32[]{:S(2)}, u32[]{:S(2)}) %collective-permute-start.9) | collective-permute-done | bytes 262176 | tf_op jit(solution)/shard_map/ppermute | solution.py:308
  39.8 3.7 %collective-permute-start.10 = (bf16[8,128,128]{2,1,0:T(8,128)(2,1)S(1)}, bf16[8,128,128]{2,1,0:T(8,128)(2,1)S(1)}, u32[]{:S(2)}, u32[]{:S(2)}) collective-permute-start(bf16[8,128,128]{2,1,0:T(8,128)(2,1)S(1)} %collective-permute-done.9.refs_1_), channel_id=1, source_target_pairs={{0,224},{4,228},{8,232},{12,236},{16,240},{20,244},{24,248},{28,25... | collective-permute-start | bytes 786440 | tf_op jit(solution)/shard_map/ppermute | solution.py:308
  43.4 0.3 collective-permute-done.13.refs_0_
  43.7 0.0 collective-permute-start.14
  43.7 3.2 %planes.6 = (bf16[512,8192]{1,0:T(8,128)(2,1)}, bf16[512,2048]{1,0:T(8,128)(2,1)}, bf16[8,512,256]{2,1,0:T(8,128)(2,1)S(1)}) custom-call(bf16[512,256]{1,0:T(8,128)(2,1)S(1)} %feats_one.1.first_ref, bf16[256,128]{1,0:T(8,128)(2,1)S(1)} %get-tuple-element.63.weight_ref, ...), custom_call_target="tpu_custom_call", output_to_operand_aliasing={{0}: (5, {}), {1}: (6, {}), {2}: (7, {})} | custom-call | flops 2800000000 | bytes 3000000 | tf_op jit(solution)/shard_map/planes/pallas_call | solution.py:257
  47.0 1.9 %collective-permute-done.10.refs_1_ = bf16[8,128,128]{2,1,0:T(8,128)(2,1)S(1)} collective-permute-done((bf16[8,128,128]{2,1,0:T(8,128)(2,1)S(1)}, bf16[8,128,128]{2,1,0:T(8,128)(2,1)S(1)}, u32[]{:S(2)}, u32[]{:S(2)}) %collective-permute-start.10) | collective-permute-done | bytes 262176 | tf_op jit(solution)/shard_map/ppermute | solution.py:308
  48.8 3.7 %collective-permute-start.11 = (bf16[8,128,128]{2,1,0:T(8,128)(2,1)S(1)}, bf16[8,128,128]{2,1,0:T(8,128)(2,1)S(1)}, u32[]{:S(2)}, u32[]{:S(2)}) collective-permute-start(bf16[8,128,128]{2,1,0:T(8,128)(2,1)S(1)} %collective-permute-done.10.refs_1_), channel_id=1, source_target_pairs={{0,224},{4,228},{8,232},{12,236},{16,240},{20,244},{24,248},{28,25... | collective-permute-start | bytes 786440 | tf_op jit(solution)/shard_map/ppermute | solution.py:308
  52.5 0.6 collective-permute-done.14.refs_0_
  53.1 0.0 collective-permute-start.15
  53.1 3.2 %planes.7 = (bf16[512,8192]{1,0:T(8,128)(2,1)}, bf16[512,2048]{1,0:T(8,128)(2,1)}, bf16[8,512,256]{2,1,0:T(8,128)(2,1)S(1)}) custom-call(bf16[512,256]{1,0:T(8,128)(2,1)S(1)} %feats_one.1.first_ref, bf16[256,128]{1,0:T(8,128)(2,1)S(1)} %get-tuple-element.63.weight_ref, ...), custom_call_target="tpu_custom_call", output_to_operand_aliasing={{0}: (5, {}), {1}: (6, {}), {2}: (7, {})} | custom-call | flops 2800000000 | bytes 3000000 | tf_op jit(solution)/shard_map/planes/pallas_call | solution.py:257
  56.4 5.7 %collective-permute-done.15.refs_0_ = bf16[8,128,128]{2,1,0:T(8,128)(2,1)S(1)} collective-permute-done((bf16[8,128,128]{2,1,0:T(8,128)(2,1)S(1)}, bf16[8,128,128]{2,1,0:T(8,128)(2,1)S(1)}, u32[]{:S(2)}, u32[]{:S(2)}) %collective-permute-start.15) | collective-permute-done | bytes 262176 | tf_op jit(solution)/shard_map/ppermute | solution.py:307
  62.1 0.1 collective-permute-start.16
  62.1 0.0 collective-permute-done.11.refs_1_
  62.2 3.3 %collective-permute-start.12 = (bf16[4,128,128]{2,1,0:T(8,128)(2,1)S(1)}, bf16[4,128,128]{2,1,0:T(8,128)(2,1)S(1)}, u32[]{:S(2)}, u32[]{:S(2)}) collective-permute-start(bf16[4,128,128]{2,1,0:T(8,128)(2,1)S(1)} %slice.38), channel_id=1, source_target_pairs={{0,224},{4,228},{8,232},{12,236},{16,240},{20,244},{24,248},{28,25... | collective-permute-start | bytes 393224 | tf_op jit(solution)/shard_map/ppermute | solution.py:311
  65.5 3.2 %planes.8 = (bf16[512,8192]{1,0:T(8,128)(2,1)}, bf16[512,2048]{1,0:T(8,128)(2,1)}, bf16[8,512,256]{2,1,0:T(8,128)(2,1)S(1)}) custom-call(bf16[512,256]{1,0:T(8,128)(2,1)S(1)} %feats_one.1.first_ref, bf16[256,128]{1,0:T(8,128)(2,1)S(1)} %get-tuple-element.63.weight_ref, ...), custom_call_target="tpu_custom_call", output_to_operand_aliasing={{0}: (5, {}), {1}: (6, {}), {2}: (7, {})} | custom-call | flops 2800000000 | bytes 3000000 | tf_op jit(solution)/shard_map/planes/pallas_call | solution.py:257
  68.7 0.0 collective-permute-done.16.hid_ref
  68.7 1.4 %half_plane.1 = (bf16[512,8192]{1,0:T(8,128)(2,1)}, bf16[512,128]{1,0:T(8,128)(2,1)S(1)}) custom-call(bf16[512,256]{1,0:T(8,128)(2,1)S(1)} %feats_one.1.first_ref, bf16[256,128]{1,0:T(8,128)(2,1)S(1)} %get-tuple-element.63.weight_ref, f32[2,128]{1,0:T(2,128)S(1)} %get-tuple-element.64.bias_ref, ...), custom_call_target="tpu_custom_call", output_to_operand_aliasing={{0}: (4, {})} | custom-call | flops 700000000 | bytes 750000 | tf_op jit(solution)/shard_map/half_plane/pallas_call | solution.py:170
  70.2 0.0 collective-permute-done.12.refs_0_
  70.2 2.0 %planes.9 = (bf16[512,8192]{1,0:T(8,128)(2,1)}, bf16[512,2048]{1,0:T(8,128)(2,1)}, bf16[512,512]{1,0:T(8,128)(2,1)}, bf16[512,128]{1,0:T(8,128)(2,1)}) custom-call(bf16[512,256]{1,0:T(8,128)(2,1)S(1)} %feats_one.1.first_ref, bf16[256,128]{1,0:T(8,128)(2,1)S(1)} %get-tuple-element.63.weight_ref, ...), custom_call_target="tpu_custom_call", output_to_operand_aliasing={{0}: (4, {}), {1}: (5, {})} | custom-call | flops 1400000000 | bytes 1500000 | tf_op jit(solution)/shard_map/planes/pallas_call | solution.py:257
  (14 shorter events, 0.1 us)
Async XLA Ops:
  0.6 0.9 %copy-start = (bf16[2,96,4,128]{3,2,1,0:T(4,128)(2,1)S(1)}, bf16[2,96,4,128]{3,2,1,0:T(4,128)(2,1)}, u32[]{:S(2)}) copy-start(bf16[2,96,4,128]{3,2,1,0:T(4,128)(2,1)} %param.5) | copy-start | bytes 589828
  2.0 16.0 %copy-start.3 = (f32[256]{0:T(256)S(1)}, f32[256]{0:T(256)}, u32[]{:S(2)}) copy-start(f32[256]{0:T(256)} %param.9) | copy-start | bytes 3076
  2.0 11.4 %collective-permute-start = (bf16[96,256]{1,0:T(8,128)(2,1)S(1)}, bf16[96,256]{1,0:T(8,128)(2,1)S(1)}, u32[]{:S(2)}, u32[]{:S(2)}) collective-permute-start(bf16[96,256]{1,0:T(8,128)(2,1)S(1)} %get-tuple-element.46), channel_id=1, source_target_pairs={{0,4},{4,8},{8,12},{12,16},{16,20},{20,24},{24,28},{28,32},{32,36}... | collective-permute-start | bytes 147464 | tf_op jit(solution)/shard_map/ppermute | solution.py:280
  5.6 7.9 %collective-permute-start.2 = (bf16[96,256]{1,0:T(8,128)(2,1)S(1)}, bf16[96,256]{1,0:T(8,128)(2,1)S(1)}, u32[]{:S(2)}, u32[]{:S(2)}) collective-permute-start(bf16[96,256]{1,0:T(8,128)(2,1)S(1)} %get-tuple-element.46), channel_id=1, source_target_pairs={{0,5},{1,6},{2,7},{4,9},{5,10},{6,11},{8,13},{9,14},{10,15},{12,17... | collective-permute-start | bytes 147464 | tf_op jit(solution)/shard_map/ppermute | solution.py:279
  8.1 5.3 %collective-permute-start.1 = (bf16[16,384]{1,0:T(8,128)(2,1)S(1)}, bf16[16,384]{1,0:T(8,128)(2,1)S(1)}, u32[]{:S(2)}, u32[]{:S(2)}) collective-permute-start(bf16[16,384]{1,0:T(8,128)(2,1)S(1)} %get-tuple-element.47), channel_id=1, source_target_pairs={{0,1},{1,2},{2,3},{4,5},{5,6},{6,7},{8,9},{9,10},{10,11},{12,13},{... | collective-permute-start | bytes 36872 | tf_op jit(solution)/shard_map/ppermute | solution.py:281
  10.1 0.9 %copy-start.1 = (bf16[128,864]{0,1:T(8,128)(2,1)S(1)}, bf16[128,864]{0,1:T(8,128)(2,1)}, u32[]{:S(2)}) copy-start(bf16[128,864]{0,1:T(8,128)(2,1)} %param.6) | copy-start | bytes 663556
  11.0 0.7 copy-start.4
  11.7 6.3 %copy-start.2 = (bf16[256,128]{1,0:T(8,128)(2,1)S(1)}, bf16[256,128]{1,0:T(8,128)(2,1)}, u32[]{:S(2)}) copy-start(bf16[256,128]{1,0:T(8,128)(2,1)} %refs_0_) | copy-start | bytes 196612
  14.2 5.7 %collective-permute-start.3 = (bf16[128,128]{1,0:T(8,128)(2,1)S(1)}, bf16[128,128]{1,0:T(8,128)(2,1)S(1)}, u32[]{:S(2)}, u32[]{:S(2)}) collective-permute-start(bf16[128,128]{1,0:T(8,128)(2,1)S(1)} %get-tuple-element.55), channel_id=1, source_target_pairs={{0,16},{4,20},{8,24},{12,28},{16,0},{20,4},{24,8},{28,12},{32,48},... | collective-permute-start | bytes 98312 | tf_op jit(solution)/shard_map/ppermute | solution.py:292
  18.0 1.9 %collective-permute-start.4 = (bf16[128,128]{1,0:T(8,128)(2,1)S(1)}, bf16[128,128]{1,0:T(8,128)(2,1)S(1)}, u32[]{:S(2)}, u32[]{:S(2)}) collective-permute-start(bf16[128,128]{1,0:T(8,128)(2,1)S(1)} %get-tuple-element.54.own_ref), channel_id=1, source_target_pairs={{0,1},{1,0},{2,3},{3,2},{4,5},{5,4},{6,7},{7,6},{8,9},{9,8},{10,11... | collective-permute-start | bytes 98312 | tf_op jit(solution)/shard_map/ppermute | solution.py:294
  19.9 5.5 %collective-permute-start.5 = (bf16[2,128,128]{2,1,0:T(8,128)(2,1)S(1)}, bf16[2,128,128]{2,1,0:T(8,128)(2,1)S(1)}, u32[]{:S(2)}, u32[]{:S(2)}) collective-permute-start(bf16[2,128,128]{2,1,0:T(8,128)(2,1)S(1)} %pad_maximum_fusion), channel_id=1, source_target_pairs={{0,12},{4,0},{8,4},{12,8},{16,28},{20,16},{24,20},{28,24},{32,44},... | collective-permute-start | bytes 196616 | tf_op jit(solution)/shard_map/ppermute | solution.py:298
  23.0 5.8 %collective-permute-start.6 = (bf16[2,128,128]{2,1,0:T(8,128)(2,1)S(1)}, bf16[2,128,128]{2,1,0:T(8,128)(2,1)S(1)}, u32[]{:S(2)}, u32[]{:S(2)}) collective-permute-start(bf16[2,128,128]{2,1,0:T(8,128)(2,1)S(1)} %pad_maximum_fusion), channel_id=1, source_target_pairs={{0,8},{4,12},{8,0},{12,4},{16,24},{20,28},{24,16},{28,20},{32,40},... | collective-permute-start | bytes 196616 | tf_op jit(solution)/shard_map/ppermute | solution.py:298
  23.4 6.1 %collective-permute-start.7 = (bf16[2,128,128]{2,1,0:T(8,128)(2,1)S(1)}, bf16[2,128,128]{2,1,0:T(8,128)(2,1)S(1)}, u32[]{:S(2)}, u32[]{:S(2)}) collective-permute-start(bf16[2,128,128]{2,1,0:T(8,128)(2,1)S(1)} %pad_maximum_fusion), channel_id=1, source_target_pairs={{0,4},{4,8},{8,12},{12,0},{16,20},{20,24},{24,28},{28,16},{32,36},... | collective-permute-start | bytes 196616 | tf_op jit(solution)/shard_map/ppermute | solution.py:298
  24.7 4.8 %collective-permute-start.8 = (bf16[2,128,128]{2,1,0:T(8,128)(2,1)S(1)}, bf16[2,128,128]{2,1,0:T(8,128)(2,1)S(1)}, u32[]{:S(2)}, u32[]{:S(2)}) collective-permute-start(bf16[2,128,128]{2,1,0:T(8,128)(2,1)S(1)} %pad_maximum_fusion.1), channel_id=1, source_target_pairs={{0,2},{1,3},{2,0},{3,1},{4,6},{5,7},{6,4},{7,5},{8,10},{9,11},{10,... | collective-permute-start | bytes 196616 | tf_op jit(solution)/shard_map/ppermute | solution.py:297
  29.5 10.2 %collective-permute-start.9 = (bf16[8,128,128]{2,1,0:T(8,128)(2,1)S(1)}, bf16[8,128,128]{2,1,0:T(8,128)(2,1)S(1)}, u32[]{:S(2)}, u32[]{:S(2)}) collective-permute-start(bf16[8,128,128]{2,1,0:T(8,128)(2,1)S(1)} %slice_dynamic-update-slice_fusion.refs_0_), channel_id=1, source_target_pairs={{0,224},{4,228},{8,232},{12,236},{16,240},{20,244},{24,248},{28,25... | collective-permute-start | bytes 786440 | tf_op jit(solution)/shard_map/ppermute | solution.py:308
  35.5 8.3 %collective-permute-start.13 = (bf16[8,128,128]{2,1,0:T(8,128)(2,1)S(1)}, bf16[8,128,128]{2,1,0:T(8,128)(2,1)S(1)}, u32[]{:S(2)}, u32[]{:S(2)}) collective-permute-start(bf16[8,128,128]{2,1,0:T(8,128)(2,1)S(1)} %slice_dynamic-update-slice_fusion.refs_0_), channel_id=1, source_target_pairs={{0,32},{4,36},{8,40},{12,44},{16,48},{20,52},{24,56},{28,60},{32,6... | collective-permute-start | bytes 786440 | tf_op jit(solution)/shard_map/ppermute | solution.py:307
  39.8 9.1 %collective-permute-start.10 = (bf16[8,128,128]{2,1,0:T(8,128)(2,1)S(1)}, bf16[8,128,128]{2,1,0:T(8,128)(2,1)S(1)}, u32[]{:S(2)}, u32[]{:S(2)}) collective-permute-start(bf16[8,128,128]{2,1,0:T(8,128)(2,1)S(1)} %collective-permute-done.9.refs_1_), channel_id=1, source_target_pairs={{0,224},{4,228},{8,232},{12,236},{16,240},{20,244},{24,248},{28,25... | collective-permute-start | bytes 786440 | tf_op jit(solution)/shard_map/ppermute | solution.py:308
  43.7 9.4 %collective-permute-start.14 = (bf16[8,128,128]{2,1,0:T(8,128)(2,1)S(1)}, bf16[8,128,128]{2,1,0:T(8,128)(2,1)S(1)}, u32[]{:S(2)}, u32[]{:S(2)}) collective-permute-start(bf16[8,128,128]{2,1,0:T(8,128)(2,1)S(1)} %collective-permute-done.13.refs_0_), channel_id=1, source_target_pairs={{0,32},{4,36},{8,40},{12,44},{16,48},{20,52},{24,56},{28,60},{32,6... | collective-permute-start | bytes 786440 | tf_op jit(solution)/shard_map/ppermute | solution.py:307
  48.8 13.3 %collective-permute-start.11 = (bf16[8,128,128]{2,1,0:T(8,128)(2,1)S(1)}, bf16[8,128,128]{2,1,0:T(8,128)(2,1)S(1)}, u32[]{:S(2)}, u32[]{:S(2)}) collective-permute-start(bf16[8,128,128]{2,1,0:T(8,128)(2,1)S(1)} %collective-permute-done.10.refs_1_), channel_id=1, source_target_pairs={{0,224},{4,228},{8,232},{12,236},{16,240},{20,244},{24,248},{28,25... | collective-permute-start | bytes 786440 | tf_op jit(solution)/shard_map/ppermute | solution.py:308
  53.1 8.9 %collective-permute-start.15 = (bf16[8,128,128]{2,1,0:T(8,128)(2,1)S(1)}, bf16[8,128,128]{2,1,0:T(8,128)(2,1)S(1)}, u32[]{:S(2)}, u32[]{:S(2)}) collective-permute-start(bf16[8,128,128]{2,1,0:T(8,128)(2,1)S(1)} %collective-permute-done.14.refs_0_), channel_id=1, source_target_pairs={{0,32},{4,36},{8,40},{12,44},{16,48},{20,52},{24,56},{28,60},{32,6... | collective-permute-start | bytes 786440 | tf_op jit(solution)/shard_map/ppermute | solution.py:307
  62.1 6.7 %collective-permute-start.16 = (bf16[4,128,128]{2,1,0:T(8,128)(2,1)S(1)}, bf16[4,128,128]{2,1,0:T(8,128)(2,1)S(1)}, u32[]{:S(2)}, u32[]{:S(2)}) collective-permute-start(bf16[4,128,128]{2,1,0:T(8,128)(2,1)S(1)} %slice.39), channel_id=1, source_target_pairs={{0,32},{4,36},{8,40},{12,44},{16,48},{20,52},{24,56},{28,60},{32,6... | collective-permute-start | bytes 393224 | tf_op jit(solution)/shard_map/ppermute | solution.py:310
  62.2 8.0 %collective-permute-start.12 = (bf16[4,128,128]{2,1,0:T(8,128)(2,1)S(1)}, bf16[4,128,128]{2,1,0:T(8,128)(2,1)S(1)}, u32[]{:S(2)}, u32[]{:S(2)}) collective-permute-start(bf16[4,128,128]{2,1,0:T(8,128)(2,1)S(1)} %slice.38), channel_id=1, source_target_pairs={{0,224},{4,228},{8,232},{12,236},{16,240},{20,244},{24,248},{28,25... | collective-permute-start | bytes 393224 | tf_op jit(solution)/shard_map/ppermute | solution.py:311

commit v8 on v6

--- a/solution.py
+++ b/solution.py
@@ -259,11 +259,10 @@
     other = lax.ppermute(hidden_two, "rows", along("yh", 1))
     proj_weight, proj_bias = stage(*params)
     swapped = lax.ppermute(hidden_one, "cols", [(k, k ^ 1) for k in range(COLS)])
-    other, swapped, proj_weight, proj_bias = lax.optimization_barrier((other, swapped, proj_weight, proj_bias))
+    far = lax.ppermute(jnp.stack([hidden_one, swapped]), "cols", [(k, k ^ 2) for k in range(COLS)])
+    other, far, proj_weight, proj_bias = lax.optimization_barrier((other, far, proj_weight, proj_bias))
     pair = jnp.stack([hidden_two, other])
-    far = lax.ppermute(jnp.stack([hidden_one, swapped]), "cols", [(k, k ^ 2) for k in range(COLS)])
     mine = jnp.concatenate([pair] + [lax.ppermute(pair, "rows", along("x", -s)) for s in range(1, X)])
-    mine, far = lax.optimization_barrier((mine, far))
     first = feats_one((hidden_one, swapped, far), proj_weight, proj_bias)
 
     call = functools.partial(planes_call, first=first, proj_weight=proj_weight, proj_bias=proj_bias)

time: 68.1 us -> 68.4 us (level); the launches traced: 66.8 us -> 68.1 us
  waiting for transfers between devices: 13.9 us -> 20.1 us
  starting transfers between devices: 34 us -> 29.2 us
    ppermute x3, starting transfers between devices: 9.59 us -> 3.4 us  [per_device(): below = lax.ppermute(below, 'rows', along('z', 1))]
    ppermute x3, waiting for transfers between devices: 5.6 us -> 8.85 us  [per_device(): below = lax.ppermute(below, 'rows', along('z', 1))]
    ppermute x3, starting transfers between devices: 0.01 us -> 2.48 us  [per_device(): above = lax.ppermute(above, 'rows', along('z', -1))]
    ppermute x1, waiting for transfers between devices: 0.05 us -> 1.46 us  [per_device(): lax.ppermute(jnp.stack([hidden_one, swapped]), 'cols', [(k, k ^ 2) for k...]
    ppermute x3, waiting for transfers between devices: 3.42 us -> 4.67 us  [per_device(): lax.ppermute(pair, 'rows', along('x', -s))]
    ppermute x1, starting transfers between devices: 3.77 us -> 2.57 us  [per_device(): below = lax.ppermute(below[:4], 'rows', along('z', 1))]
    ppermute x1, starting transfers between devices: 0.94 us -> 1.69 us  [per_device(): lax.ppermute(hidden_one, 'cols', [(k, k ^ 1) for k in range(COLS)])]
  transfers between devices with their start and end apart: 17 -> 17, of which waited for: 9 -> 11; matrix products, arithmetic and copies ran while one was open for 0% -> 0% of each run, Pallas kernels for 18% -> 17%
where the time goes in v8:
time: 68.4 us; the launch traced here: 68.1 us
  starting transfers between devices  29.2 us (43%)
  waiting for transfers between devices  20.1 us (29%)
  Pallas kernels  15.3 us (22%)
  local copies, waits for them, and re-layouts  2.58 us (4%)
  between operations  0.96 us (1%)
    pallas_call x5, Pallas kernels, planes_call(): pl.pallas_call(functools.partial(planes_kernel, offsets, last, len(aliase...  13.8 us
    ppermute x3, waiting for transfers between devices, per_device(): below = lax.ppermute(below, 'rows', along('z', 1))  8.85 us
    ppermute x3, starting transfers between devices, per_device(): lax.ppermute(pair, 'rows', along('x', -s))  5.33 us
    ppermute x3, waiting for transfers between devices, per_device(): lax.ppermute(pair, 'rows', along('x', -s))  4.67 us
    ppermute x1, starting transfers between devices, per_device(): left = lax.ppermute(left, 'cols', right)  3.87 us
    ppermute x1, starting transfers between devices, per_device(): top = lax.ppermute(top, 'rows', down)  3.56 us
    ppermute x3, starting transfers between devices, per_device(): below = lax.ppermute(below, 'rows', along('z', 1))  3.4 us
    ppermute x1, waiting for transfers between devices, per_device(): above = lax.ppermute(above[4:], 'rows', along('z', -1))  2.9 us
  transfers between devices with their start and end apart: 17, of which 11 were waited for; matrix products, arithmetic and copies ran while one was open for 0% of the time, Pallas kernels for 17%

profile of v8, /device:TPU:96, one launch (start us, length us, event | category | flops | bytes accessed | tf_op | source)
XLA Modules:
  0.0 68.1 jit_solution(7365555674108293531)
XLA Ops:
  0.6 0.0 copy-start
  0.6 0.9 %copy-done = bf16[2,96,4,128]{3,2,1,0:T(4,128)(2,1)S(1)} copy-done((bf16[2,96,4,128]{3,2,1,0:T(4,128)(2,1)S(1)}, bf16[2,96,4,128]{3,2,1,0:T(4,128)(2,1)}, u32[]{:S(2)}) %copy-start) | copy-done | bytes 196632
  1.6 0.4 split_tile.1
  2.0 0.0 copy-start.3
  2.0 3.6 %collective-permute-start = (bf16[96,256]{1,0:T(8,128)(2,1)S(1)}, bf16[96,256]{1,0:T(8,128)(2,1)S(1)}, u32[]{:S(2)}, u32[]{:S(2)}) collective-permute-start(bf16[96,256]{1,0:T(8,128)(2,1)S(1)} %get-tuple-element.42), channel_id=1, source_target_pairs={{0,4},{4,8},{8,12},{12,16},{16,20},{20,24},{24,28},{28,32},{32,36}... | collective-permute-start | bytes 147464 | tf_op jit(solution)/shard_map/ppermute | solution.py:247
  5.6 2.6 %collective-permute-start.2 = (bf16[96,256]{1,0:T(8,128)(2,1)S(1)}, bf16[96,256]{1,0:T(8,128)(2,1)S(1)}, u32[]{:S(2)}, u32[]{:S(2)}) collective-permute-start(bf16[96,256]{1,0:T(8,128)(2,1)S(1)} %get-tuple-element.42), channel_id=1, source_target_pairs={{0,5},{1,6},{2,7},{4,9},{5,10},{6,11},{8,13},{9,14},{10,15},{12,17... | collective-permute-start | bytes 147464 | tf_op jit(solution)/shard_map/ppermute | solution.py:246
  8.1 3.9 %collective-permute-start.1 = (bf16[16,384]{1,0:T(8,128)(2,1)S(1)}, bf16[16,384]{1,0:T(8,128)(2,1)S(1)}, u32[]{:S(2)}, u32[]{:S(2)}) collective-permute-start(bf16[16,384]{1,0:T(8,128)(2,1)S(1)} %get-tuple-element.43), channel_id=1, source_target_pairs={{0,1},{1,2},{2,3},{4,5},{5,6},{6,7},{8,9},{9,10},{10,11},{12,13},{... | collective-permute-start | bytes 36872 | tf_op jit(solution)/shard_map/ppermute | solution.py:248
  12.0 0.0 copy-start.1
  12.0 0.9 %copy-done.1 = bf16[128,864]{0,1:T(8,128)(2,1)S(1)} copy-done((bf16[128,864]{0,1:T(8,128)(2,1)S(1)}, bf16[128,864]{0,1:T(8,128)(2,1)}, u32[]{:S(2)}) %copy-start.1) | copy-done | bytes 221208
  13.0 0.0 copy-start.4
  13.0 0.7 copy-done.4
  13.6 0.0 copy-start.2
  13.6 0.0 collective-permute-done.1.left_ref
  13.6 0.0 collective-permute-done.top_ref
  13.7 0.0 collective-permute-done.2.corner_ref
  13.7 0.7 %hidden.1 = (bf16[128,128]{1,0:T(8,128)(2,1)S(1)}, bf16[128,128]{1,0:T(8,128)(2,1)S(1)}) custom-call(bf16[384,256]{1,0:T(8,128)(2,1)S(1)} %get-tuple-element.41.main_ref, bf16[96,256]{1,0:T(8,128)(2,1)S(1)} %collective-permute-done.top_ref, bf16[16,384]{1,0:T(8,128)(2,1)S(1)} %collective-permute-done.1.left_ref, ...), custom_call_target="tpu_custom_call" | custom-call | tf_op jit(solution)/shard_map/hidden/pallas_call | solution.py:114
  14.4 1.7 %collective-permute-start.3 = (bf16[128,128]{1,0:T(8,128)(2,1)S(1)}, bf16[128,128]{1,0:T(8,128)(2,1)S(1)}, u32[]{:S(2)}, u32[]{:S(2)}) collective-permute-start(bf16[128,128]{1,0:T(8,128)(2,1)S(1)} %get-tuple-element.50.own_ref), channel_id=1, source_target_pairs={{0,1},{1,0},{2,3},{3,2},{4,5},{5,4},{6,7},{7,6},{8,9},{9,8},{10,11... | collective-permute-start | bytes 98312 | tf_op jit(solution)/shard_map/ppermute | solution.py:261
  16.1 2.5 %collective-permute-start.4 = (bf16[128,128]{1,0:T(8,128)(2,1)S(1)}, bf16[128,128]{1,0:T(8,128)(2,1)S(1)}, u32[]{:S(2)}, u32[]{:S(2)}) collective-permute-start(bf16[128,128]{1,0:T(8,128)(2,1)S(1)} %get-tuple-element.51), channel_id=1, source_target_pairs={{0,16},{4,20},{8,24},{12,28},{16,0},{20,4},{24,8},{28,12},{32,48},... | collective-permute-start | bytes 98312 | tf_op jit(solution)/shard_map/ppermute | solution.py:259
  18.6 0.0 collective-permute-done.3.swapped_ref
  18.6 1.1 %collective-permute-start.5 = (bf16[2,128,128]{2,1,0:T(8,128)(2,1)S(1)}, bf16[2,128,128]{2,1,0:T(8,128)(2,1)S(1)}, u32[]{:S(2)}, u32[]{:S(2)}) collective-permute-start(bf16[2,128,128]{2,1,0:T(8,128)(2,1)S(1)} %pad_maximum_fusion), channel_id=1, source_target_pairs={{0,2},{1,3},{2,0},{3,1},{4,6},{5,7},{6,4},{7,5},{8,10},{9,11},{10,... | collective-permute-start | bytes 196616 | tf_op jit(solution)/shard_map/ppermute | solution.py:262
  19.8 0.0 copy-done.3
  19.8 0.0 copy-done.2
  19.8 1.8 %collective-permute-done.4 = bf16[128,128]{1,0:T(8,128)(2,1)S(1)} collective-permute-done((bf16[128,128]{1,0:T(8,128)(2,1)S(1)}, bf16[128,128]{1,0:T(8,128)(2,1)S(1)}, u32[]{:S(2)}, u32[]{:S(2)}) %collective-permute-start.4) | collective-permute-done | bytes 32800 | tf_op jit(solution)/shard_map/ppermute | solution.py:259
  21.5 1.5 %collective-permute-done.5.far_ref = bf16[2,128,128]{2,1,0:T(8,128)(2,1)S(1)} collective-permute-done((bf16[2,128,128]{2,1,0:T(8,128)(2,1)S(1)}, bf16[2,128,128]{2,1,0:T(8,128)(2,1)S(1)}, u32[]{:S(2)}, u32[]{:S(2)}) %collective-permute-start.5) | collective-permute-done | bytes 65568 | tf_op jit(solution)/shard_map/ppermute | solution.py:262
  23.0 3.6 %collective-permute-start.6 = (bf16[2,128,128]{2,1,0:T(8,128)(2,1)S(1)}, bf16[2,128,128]{2,1,0:T(8,128)(2,1)S(1)}, u32[]{:S(2)}, u32[]{:S(2)}) collective-permute-start(bf16[2,128,128]{2,1,0:T(8,128)(2,1)S(1)} %pad_maximum_fusion.1), channel_id=1, source_target_pairs={{0,12},{4,0},{8,4},{12,8},{16,28},{20,16},{24,20},{28,24},{32,44},... | collective-permute-start | bytes 196616 | tf_op jit(solution)/shard_map/ppermute | solution.py:265
  26.6 0.4 collective-permute-start.7
  27.0 1.3 %collective-permute-start.8 = (bf16[2,128,128]{2,1,0:T(8,128)(2,1)S(1)}, bf16[2,128,128]{2,1,0:T(8,128)(2,1)S(1)}, u32[]{:S(2)}, u32[]{:S(2)}) collective-permute-start(bf16[2,128,128]{2,1,0:T(8,128)(2,1)S(1)} %pad_maximum_fusion.1), channel_id=1, source_target_pairs={{0,4},{4,8},{8,12},{12,0},{16,20},{20,24},{24,28},{28,16},{32,36},... | collective-permute-start | bytes 196616 | tf_op jit(solution)/shard_map/ppermute | solution.py:265
  28.3 0.1 collective-permute-done.6
  28.5 3.9 %collective-permute-done.7 = bf16[2,128,128]{2,1,0:T(8,128)(2,1)S(1)} collective-permute-done((bf16[2,128,128]{2,1,0:T(8,128)(2,1)S(1)}, bf16[2,128,128]{2,1,0:T(8,128)(2,1)S(1)}, u32[]{:S(2)}, u32[]{:S(2)}) %collective-permute-start.7) | collective-permute-done | bytes 65568 | tf_op jit(solution)/shard_map/ppermute | solution.py:265
  32.4 0.6 collective-permute-done.8
  33.1 1.1 %collective-permute-start.9 = (bf16[8,128,128]{2,1,0:T(8,128)(2,1)S(1)}, bf16[8,128,128]{2,1,0:T(8,128)(2,1)S(1)}, u32[]{:S(2)}, u32[]{:S(2)}) collective-permute-start(bf16[8,128,128]{2,1,0:T(8,128)(2,1)S(1)} %constant_dynamic-update-slice_fusion.refs_0_), channel_id=1, source_target_pairs={{0,32},{4,36},{8,40},{12,44},{16,48},{20,52},{24,56},{28,60},{32,6... | collective-permute-start | bytes 786440 | tf_op jit(solution)/shard_map/ppermute | solution.py:272
  34.2 1.0 %collective-permute-start.13 = (bf16[8,128,128]{2,1,0:T(8,128)(2,1)S(1)}, bf16[8,128,128]{2,1,0:T(8,128)(2,1)S(1)}, u32[]{:S(2)}, u32[]{:S(2)}) collective-permute-start(bf16[8,128,128]{2,1,0:T(8,128)(2,1)S(1)} %constant_dynamic-update-slice_fusion.refs_0_), channel_id=1, source_target_pairs={{0,224},{4,228},{8,232},{12,236},{16,240},{20,244},{24,248},{28,25... | collective-permute-start | bytes 786440 | tf_op jit(solution)/shard_map/ppermute | solution.py:273
  35.2 0.3 feats_one.1.first_ref
  35.4 1.9 %planes.5 = (bf16[512,8192]{1,0:T(8,128)(2,1)}, bf16[512,2048]{1,0:T(8,128)(2,1)}, bf16[8,512,256]{2,1,0:T(8,128)(2,1)S(1)}) custom-call(bf16[512,256]{1,0:T(8,128)(2,1)S(1)} %feats_one.1.first_ref, bf16[256,128]{1,0:T(8,128)(2,1)S(1)} %get-tuple-element.57.weight_ref, f32[2,128]{1,0:T(2,128)S(1)} %get-tuple-element.58.bias_ref, ...), custom_call_target="tpu_custom_call" | custom-call | flops 1400000000 | bytes 1500000 | tf_op jit(solution)/shard_map/planes/pallas_call | solution.py:224
  37.3 3.2 %collective-permute-done.9.refs_0_ = bf16[8,128,128]{2,1,0:T(8,128)(2,1)S(1)} collective-permute-done((bf16[8,128,128]{2,1,0:T(8,128)(2,1)S(1)}, bf16[8,128,128]{2,1,0:T(8,128)(2,1)S(1)}, u32[]{:S(2)}, u32[]{:S(2)}) %collective-permute-start.9) | collective-permute-done | bytes 262176 | tf_op jit(solution)/shard_map/ppermute | solution.py:272
  40.5 1.2 %collective-permute-start.10 = (bf16[8,128,128]{2,1,0:T(8,128)(2,1)S(1)}, bf16[8,128,128]{2,1,0:T(8,128)(2,1)S(1)}, u32[]{:S(2)}, u32[]{:S(2)}) collective-permute-start(bf16[8,128,128]{2,1,0:T(8,128)(2,1)S(1)} %collective-permute-done.9.refs_0_), channel_id=1, source_target_pairs={{0,32},{4,36},{8,40},{12,44},{16,48},{20,52},{24,56},{28,60},{32,6... | collective-permute-start | bytes 786440 | tf_op jit(solution)/shard_map/ppermute | solution.py:272
  41.7 0.0 collective-permute-done.13.refs_1_
  41.8 0.8 %collective-permute-start.14 = (bf16[8,128,128]{2,1,0:T(8,128)(2,1)S(1)}, bf16[8,128,128]{2,1,0:T(8,128)(2,1)S(1)}, u32[]{:S(2)}, u32[]{:S(2)}) collective-permute-start(bf16[8,128,128]{2,1,0:T(8,128)(2,1)S(1)} %collective-permute-done.13.refs_1_), channel_id=1, source_target_pairs={{0,224},{4,228},{8,232},{12,236},{16,240},{20,244},{24,248},{28,25... | collective-permute-start | bytes 786440 | tf_op jit(solution)/shard_map/ppermute | solution.py:273
  42.6 3.2 %planes.6 = (bf16[512,8192]{1,0:T(8,128)(2,1)}, bf16[512,2048]{1,0:T(8,128)(2,1)}, bf16[8,512,256]{2,1,0:T(8,128)(2,1)S(1)}) custom-call(bf16[512,256]{1,0:T(8,128)(2,1)S(1)} %feats_one.1.first_ref, bf16[256,128]{1,0:T(8,128)(2,1)S(1)} %get-tuple-element.57.weight_ref, ...), custom_call_target="tpu_custom_call", output_to_operand_aliasing={{0}: (5, {}), {1}: (6, {}), {2}: (7, {})} | custom-call | flops 2800000000 | bytes 3000000 | tf_op jit(solution)/shard_map/planes/pallas_call | solution.py:224
  45.8 3.3 %collective-permute-done.10.refs_0_ = bf16[8,128,128]{2,1,0:T(8,128)(2,1)S(1)} collective-permute-done((bf16[8,128,128]{2,1,0:T(8,128)(2,1)S(1)}, bf16[8,128,128]{2,1,0:T(8,128)(2,1)S(1)}, u32[]{:S(2)}, u32[]{:S(2)}) %collective-permute-start.10) | collective-permute-done | bytes 262176 | tf_op jit(solution)/shard_map/ppermute | solution.py:272
  49.2 1.1 %collective-permute-start.11 = (bf16[8,128,128]{2,1,0:T(8,128)(2,1)S(1)}, bf16[8,128,128]{2,1,0:T(8,128)(2,1)S(1)}, u32[]{:S(2)}, u32[]{:S(2)}) collective-permute-start(bf16[8,128,128]{2,1,0:T(8,128)(2,1)S(1)} %collective-permute-done.10.refs_0_), channel_id=1, source_target_pairs={{0,32},{4,36},{8,40},{12,44},{16,48},{20,52},{24,56},{28,60},{32,6... | collective-permute-start | bytes 786440 | tf_op jit(solution)/shard_map/ppermute | solution.py:272
  50.2 0.2 collective-permute-done.14.refs_1_
  50.5 0.7 %collective-permute-start.15 = (bf16[8,128,128]{2,1,0:T(8,128)(2,1)S(1)}, bf16[8,128,128]{2,1,0:T(8,128)(2,1)S(1)}, u32[]{:S(2)}, u32[]{:S(2)}) collective-permute-start(bf16[8,128,128]{2,1,0:T(8,128)(2,1)S(1)} %collective-permute-done.14.refs_1_), channel_id=1, source_target_pairs={{0,224},{4,228},{8,232},{12,236},{16,240},{20,244},{24,248},{28,25... | collective-permute-start | bytes 786440 | tf_op jit(solution)/shard_map/ppermute | solution.py:273
  51.2 3.2 %planes.7 = (bf16[512,8192]{1,0:T(8,128)(2,1)}, bf16[512,2048]{1,0:T(8,128)(2,1)}, bf16[8,512,256]{2,1,0:T(8,128)(2,1)S(1)}) custom-call(bf16[512,256]{1,0:T(8,128)(2,1)S(1)} %feats_one.1.first_ref, bf16[256,128]{1,0:T(8,128)(2,1)S(1)} %get-tuple-element.57.weight_ref, ...), custom_call_target="tpu_custom_call", output_to_operand_aliasing={{0}: (5, {}), {1}: (6, {}), {2}: (7, {})} | custom-call | flops 2800000000 | bytes 3000000 | tf_op jit(solution)/shard_map/planes/pallas_call | solution.py:224
  54.4 2.3 %collective-permute-done.11.refs_0_ = bf16[8,128,128]{2,1,0:T(8,128)(2,1)S(1)} collective-permute-done((bf16[8,128,128]{2,1,0:T(8,128)(2,1)S(1)}, bf16[8,128,128]{2,1,0:T(8,128)(2,1)S(1)}, u32[]{:S(2)}, u32[]{:S(2)}) %collective-permute-start.11) | collective-permute-done | bytes 262176 | tf_op jit(solution)/shard_map/ppermute | solution.py:272
  56.8 2.6 %collective-permute-start.12 = (bf16[4,128,128]{2,1,0:T(8,128)(2,1)S(1)}, bf16[4,128,128]{2,1,0:T(8,128)(2,1)S(1)}, u32[]{:S(2)}, u32[]{:S(2)}) collective-permute-start(bf16[4,128,128]{2,1,0:T(8,128)(2,1)S(1)} %slice.8), channel_id=1, source_target_pairs={{0,32},{4,36},{8,40},{12,44},{16,48},{20,52},{24,56},{28,60},{32,6... | collective-permute-start | bytes 393224 | tf_op jit(solution)/shard_map/ppermute | solution.py:275
  59.3 0.1 collective-permute-done.15.refs_1_
  59.5 0.1 collective-permute-start.16
  59.6 3.3 %planes.8 = (bf16[512,8192]{1,0:T(8,128)(2,1)}, bf16[512,2048]{1,0:T(8,128)(2,1)}, bf16[8,512,256]{2,1,0:T(8,128)(2,1)S(1)}) custom-call(bf16[512,256]{1,0:T(8,128)(2,1)S(1)} %feats_one.1.first_ref, bf16[256,128]{1,0:T(8,128)(2,1)S(1)} %get-tuple-element.57.weight_ref, ...), custom_call_target="tpu_custom_call", output_to_operand_aliasing={{0}: (5, {}), {1}: (6, {}), {2}: (7, {})} | custom-call | flops 2800000000 | bytes 3000000 | tf_op jit(solution)/shard_map/planes/pallas_call | solution.py:224
  62.8 0.0 collective-permute-done.12.refs_0_
  62.9 2.9 %collective-permute-done.16.refs_1_ = bf16[4,128,128]{2,1,0:T(8,128)(2,1)S(1)} collective-permute-done((bf16[4,128,128]{2,1,0:T(8,128)(2,1)S(1)}, bf16[4,128,128]{2,1,0:T(8,128)(2,1)S(1)}, u32[]{:S(2)}, u32[]{:S(2)}) %collective-permute-start.16) | collective-permute-done | bytes 131104 | tf_op jit(solution)/shard_map/ppermute | solution.py:276
  65.7 2.2 %planes.9 = (bf16[512,8192]{1,0:T(8,128)(2,1)}, bf16[512,2048]{1,0:T(8,128)(2,1)}, bf16[512,512]{1,0:T(8,128)(2,1)}, bf16[512,128]{1,0:T(8,128)(2,1)}) custom-call(bf16[512,256]{1,0:T(8,128)(2,1)S(1)} %feats_one.1.first_ref, bf16[256,128]{1,0:T(8,128)(2,1)S(1)} %get-tuple-element.57.weight_ref, ...), custom_call_target="tpu_custom_call", output_to_operand_aliasing={{0}: (5, {}), {1}: (6, {})} | custom-call | flops 1400000000 | bytes 1500000 | tf_op jit(solution)/shard_map/planes/pallas_call | solution.py:224
  (11 shorter events, 0.1 us)
Async XLA Ops:
  0.6 0.9 %copy-start = (bf16[2,96,4,128]{3,2,1,0:T(4,128)(2,1)S(1)}, bf16[2,96,4,128]{3,2,1,0:T(4,128)(2,1)}, u32[]{:S(2)}) copy-start(bf16[2,96,4,128]{3,2,1,0:T(4,128)(2,1)} %param.5) | copy-start | bytes 589828
  2.0 17.8 %copy-start.3 = (f32[256]{0:T(256)S(1)}, f32[256]{0:T(256)}, u32[]{:S(2)}) copy-start(f32[256]{0:T(256)} %param.9) | copy-start | bytes 3076
  2.0 11.6 %collective-permute-start = (bf16[96,256]{1,0:T(8,128)(2,1)S(1)}, bf16[96,256]{1,0:T(8,128)(2,1)S(1)}, u32[]{:S(2)}, u32[]{:S(2)}) collective-permute-start(bf16[96,256]{1,0:T(8,128)(2,1)S(1)} %get-tuple-element.42), channel_id=1, source_target_pairs={{0,4},{4,8},{8,12},{12,16},{16,20},{20,24},{24,28},{28,32},{32,36}... | collective-permute-start | bytes 147464 | tf_op jit(solution)/shard_map/ppermute | solution.py:247
  5.6 8.1 %collective-permute-start.2 = (bf16[96,256]{1,0:T(8,128)(2,1)S(1)}, bf16[96,256]{1,0:T(8,128)(2,1)S(1)}, u32[]{:S(2)}, u32[]{:S(2)}) collective-permute-start(bf16[96,256]{1,0:T(8,128)(2,1)S(1)} %get-tuple-element.42), channel_id=1, source_target_pairs={{0,5},{1,6},{2,7},{4,9},{5,10},{6,11},{8,13},{9,14},{10,15},{12,17... | collective-permute-start | bytes 147464 | tf_op jit(solution)/shard_map/ppermute | solution.py:246
  8.1 5.5 %collective-permute-start.1 = (bf16[16,384]{1,0:T(8,128)(2,1)S(1)}, bf16[16,384]{1,0:T(8,128)(2,1)S(1)}, u32[]{:S(2)}, u32[]{:S(2)}) collective-permute-start(bf16[16,384]{1,0:T(8,128)(2,1)S(1)} %get-tuple-element.43), channel_id=1, source_target_pairs={{0,1},{1,2},{2,3},{4,5},{5,6},{6,7},{8,9},{9,10},{10,11},{12,13},{... | collective-permute-start | bytes 36872 | tf_op jit(solution)/shard_map/ppermute | solution.py:248
  12.0 0.9 %copy-start.1 = (bf16[128,864]{0,1:T(8,128)(2,1)S(1)}, bf16[128,864]{0,1:T(8,128)(2,1)}, u32[]{:S(2)}) copy-start(bf16[128,864]{0,1:T(8,128)(2,1)} %param.6) | copy-start | bytes 663556
  13.0 0.7 copy-start.4
  13.6 6.1 %copy-start.2 = (bf16[256,128]{1,0:T(8,128)(2,1)S(1)}, bf16[256,128]{1,0:T(8,128)(2,1)}, u32[]{:S(2)}) copy-start(bf16[256,128]{1,0:T(8,128)(2,1)} %refs_0_) | copy-start | bytes 196612
  14.4 4.2 %collective-permute-start.3 = (bf16[128,128]{1,0:T(8,128)(2,1)S(1)}, bf16[128,128]{1,0:T(8,128)(2,1)S(1)}, u32[]{:S(2)}, u32[]{:S(2)}) collective-permute-start(bf16[128,128]{1,0:T(8,128)(2,1)S(1)} %get-tuple-element.50.own_ref), channel_id=1, source_target_pairs={{0,1},{1,0},{2,3},{3,2},{4,5},{5,4},{6,7},{7,6},{8,9},{9,8},{10,11... | collective-permute-start | bytes 98312 | tf_op jit(solution)/shard_map/ppermute | solution.py:261
  16.1 5.4 %collective-permute-start.4 = (bf16[128,128]{1,0:T(8,128)(2,1)S(1)}, bf16[128,128]{1,0:T(8,128)(2,1)S(1)}, u32[]{:S(2)}, u32[]{:S(2)}) collective-permute-start(bf16[128,128]{1,0:T(8,128)(2,1)S(1)} %get-tuple-element.51), channel_id=1, source_target_pairs={{0,16},{4,20},{8,24},{12,28},{16,0},{20,4},{24,8},{28,12},{32,48},... | collective-permute-start | bytes 98312 | tf_op jit(solution)/shard_map/ppermute | solution.py:259
  18.6 4.4 %collective-permute-start.5 = (bf16[2,128,128]{2,1,0:T(8,128)(2,1)S(1)}, bf16[2,128,128]{2,1,0:T(8,128)(2,1)S(1)}, u32[]{:S(2)}, u32[]{:S(2)}) collective-permute-start(bf16[2,128,128]{2,1,0:T(8,128)(2,1)S(1)} %pad_maximum_fusion), channel_id=1, source_target_pairs={{0,2},{1,3},{2,0},{3,1},{4,6},{5,7},{6,4},{7,5},{8,10},{9,11},{10,... | collective-permute-start | bytes 196616 | tf_op jit(solution)/shard_map/ppermute | solution.py:262
  23.0 5.5 %collective-permute-start.6 = (bf16[2,128,128]{2,1,0:T(8,128)(2,1)S(1)}, bf16[2,128,128]{2,1,0:T(8,128)(2,1)S(1)}, u32[]{:S(2)}, u32[]{:S(2)}) collective-permute-start(bf16[2,128,128]{2,1,0:T(8,128)(2,1)S(1)} %pad_maximum_fusion.1), channel_id=1, source_target_pairs={{0,12},{4,0},{8,4},{12,8},{16,28},{20,16},{24,20},{28,24},{32,44},... | collective-permute-start | bytes 196616 | tf_op jit(solution)/shard_map/ppermute | solution.py:265
  26.6 5.8 %collective-permute-start.7 = (bf16[2,128,128]{2,1,0:T(8,128)(2,1)S(1)}, bf16[2,128,128]{2,1,0:T(8,128)(2,1)S(1)}, u32[]{:S(2)}, u32[]{:S(2)}) collective-permute-start(bf16[2,128,128]{2,1,0:T(8,128)(2,1)S(1)} %pad_maximum_fusion.1), channel_id=1, source_target_pairs={{0,8},{4,12},{8,0},{12,4},{16,24},{20,28},{24,16},{28,20},{32,40},... | collective-permute-start | bytes 196616 | tf_op jit(solution)/shard_map/ppermute | solution.py:265
  27.0 6.0 %collective-permute-start.8 = (bf16[2,128,128]{2,1,0:T(8,128)(2,1)S(1)}, bf16[2,128,128]{2,1,0:T(8,128)(2,1)S(1)}, u32[]{:S(2)}, u32[]{:S(2)}) collective-permute-start(bf16[2,128,128]{2,1,0:T(8,128)(2,1)S(1)} %pad_maximum_fusion.1), channel_id=1, source_target_pairs={{0,4},{4,8},{8,12},{12,0},{16,20},{20,24},{24,28},{28,16},{32,36},... | collective-permute-start | bytes 196616 | tf_op jit(solution)/shard_map/ppermute | solution.py:265
  33.1 7.5 %collective-permute-start.9 = (bf16[8,128,128]{2,1,0:T(8,128)(2,1)S(1)}, bf16[8,128,128]{2,1,0:T(8,128)(2,1)S(1)}, u32[]{:S(2)}, u32[]{:S(2)}) collective-permute-start(bf16[8,128,128]{2,1,0:T(8,128)(2,1)S(1)} %constant_dynamic-update-slice_fusion.refs_0_), channel_id=1, source_target_pairs={{0,32},{4,36},{8,40},{12,44},{16,48},{20,52},{24,56},{28,60},{32,6... | collective-permute-start | bytes 786440 | tf_op jit(solution)/shard_map/ppermute | solution.py:272
  34.2 7.6 %collective-permute-start.13 = (bf16[8,128,128]{2,1,0:T(8,128)(2,1)S(1)}, bf16[8,128,128]{2,1,0:T(8,128)(2,1)S(1)}, u32[]{:S(2)}, u32[]{:S(2)}) collective-permute-start(bf16[8,128,128]{2,1,0:T(8,128)(2,1)S(1)} %constant_dynamic-update-slice_fusion.refs_0_), channel_id=1, source_target_pairs={{0,224},{4,228},{8,232},{12,236},{16,240},{20,244},{24,248},{28,25... | collective-permute-start | bytes 786440 | tf_op jit(solution)/shard_map/ppermute | solution.py:273
  40.5 8.6 %collective-permute-start.10 = (bf16[8,128,128]{2,1,0:T(8,128)(2,1)S(1)}, bf16[8,128,128]{2,1,0:T(8,128)(2,1)S(1)}, u32[]{:S(2)}, u32[]{:S(2)}) collective-permute-start(bf16[8,128,128]{2,1,0:T(8,128)(2,1)S(1)} %collective-permute-done.9.refs_0_), channel_id=1, source_target_pairs={{0,32},{4,36},{8,40},{12,44},{16,48},{20,52},{24,56},{28,60},{32,6... | collective-permute-start | bytes 786440 | tf_op jit(solution)/shard_map/ppermute | solution.py:272
  41.8 8.7 %collective-permute-start.14 = (bf16[8,128,128]{2,1,0:T(8,128)(2,1)S(1)}, bf16[8,128,128]{2,1,0:T(8,128)(2,1)S(1)}, u32[]{:S(2)}, u32[]{:S(2)}) collective-permute-start(bf16[8,128,128]{2,1,0:T(8,128)(2,1)S(1)} %collective-permute-done.13.refs_1_), channel_id=1, source_target_pairs={{0,224},{4,228},{8,232},{12,236},{16,240},{20,244},{24,248},{28,25... | collective-permute-start | bytes 786440 | tf_op jit(solution)/shard_map/ppermute | solution.py:273
  49.2 7.6 %collective-permute-start.11 = (bf16[8,128,128]{2,1,0:T(8,128)(2,1)S(1)}, bf16[8,128,128]{2,1,0:T(8,128)(2,1)S(1)}, u32[]{:S(2)}, u32[]{:S(2)}) collective-permute-start(bf16[8,128,128]{2,1,0:T(8,128)(2,1)S(1)} %collective-permute-done.10.refs_0_), channel_id=1, source_target_pairs={{0,32},{4,36},{8,40},{12,44},{16,48},{20,52},{24,56},{28,60},{32,6... | collective-permute-start | bytes 786440 | tf_op jit(solution)/shard_map/ppermute | solution.py:272
  50.5 9.0 %collective-permute-start.15 = (bf16[8,128,128]{2,1,0:T(8,128)(2,1)S(1)}, bf16[8,128,128]{2,1,0:T(8,128)(2,1)S(1)}, u32[]{:S(2)}, u32[]{:S(2)}) collective-permute-start(bf16[8,128,128]{2,1,0:T(8,128)(2,1)S(1)} %collective-permute-done.14.refs_1_), channel_id=1, source_target_pairs={{0,224},{4,228},{8,232},{12,236},{16,240},{20,244},{24,248},{28,25... | collective-permute-start | bytes 786440 | tf_op jit(solution)/shard_map/ppermute | solution.py:273
  56.8 6.1 %collective-permute-start.12 = (bf16[4,128,128]{2,1,0:T(8,128)(2,1)S(1)}, bf16[4,128,128]{2,1,0:T(8,128)(2,1)S(1)}, u32[]{:S(2)}, u32[]{:S(2)}) collective-permute-start(bf16[4,128,128]{2,1,0:T(8,128)(2,1)S(1)} %slice.8), channel_id=1, source_target_pairs={{0,32},{4,36},{8,40},{12,44},{16,48},{20,52},{24,56},{28,60},{32,6... | collective-permute-start | bytes 393224 | tf_op jit(solution)/shard_map/ppermute | solution.py:275
  59.5 6.3 %collective-permute-start.16 = (bf16[4,128,128]{2,1,0:T(8,128)(2,1)S(1)}, bf16[4,128,128]{2,1,0:T(8,128)(2,1)S(1)}, u32[]{:S(2)}, u32[]{:S(2)}) collective-permute-start(bf16[4,128,128]{2,1,0:T(8,128)(2,1)S(1)} %slice.9), channel_id=1, source_target_pairs={{0,224},{4,228},{8,232},{12,236},{16,240},{20,244},{24,248},{28,25... | collective-permute-start | bytes 393224 | tf_op jit(solution)/shard_map/ppermute | solution.py:276
